TPU v7x, 32 devices: a whole 2x2x4 slice. The times are simulated.
32 devices in a mesh: seq: 4 (over x, core), ctx: 8 (over z, y).
Axes of the slice: x: 2, y: 2, z: 4, core: 2. Of those that a mesh axis runs over, the one named last changes fastest.
Arguments:
- tokens: bfloat16 [4096, 1536], P(('seq', 'ctx')), may hold values from -6 to 6
- segments: int32 [4, 1024], P('seq'), may hold values from 0 to 1023, as said below
- w_query: bfloat16 [1536, 1536], P(('seq', 'ctx')), may hold values from -0.15625 to 0.15625
- b_query: bfloat16 [1536], P(('seq', 'ctx')), may hold values from -3 to 3
- w_key: bfloat16 [1536, 256], P(('seq', 'ctx')), may hold values from -0.15625 to 0.15625
- b_key: bfloat16 [256], replicated, may hold values from -3 to 3
- w_value: bfloat16 [1536, 256], P(('seq', 'ctx')), may hold values from -0.15625 to 0.15625
- b_value: bfloat16 [256], P(('seq', 'ctx')), may hold values from -3 to 3
- w_out: bfloat16 [1536, 1536], P(('seq', 'ctx')), may hold values from -0.3125 to 0.3125
- norm_attn: bfloat16 [1536], P(('seq', 'ctx')), may hold values from 0.25 to 1.75
- w_gate: bfloat16 [1536, 8960], P(('seq', 'ctx')), may hold values from -0.15625 to 0.15625
- w_up: bfloat16 [1536, 8960], P(('seq', 'ctx')), may hold values from -0.15625 to 0.15625
- w_down: bfloat16 [8960, 1536], P(('seq', 'ctx')), may hold values from -0.0625 to 0.0625
- norm_mlp: bfloat16 [1536], P(('seq', 'ctx')), may hold values from 0.25 to 1.75
- cotangent: bfloat16 [4096, 1536], P(('seq', 'ctx')), may hold values from -6 to 6
Outputs:
- output: float32 [4096, 1536], P(('seq', 'ctx'))
- grad_tokens: float32 [4096, 1536], P(('seq', 'ctx'))
- grad_w_query: float32 [1536, 1536], P(('seq', 'ctx'))
- grad_b_query: float32 [1536], P(('seq', 'ctx'))
- grad_w_key: float32 [1536, 256], P(('seq', 'ctx'))
- grad_b_key: float32 [256], replicated
- grad_w_value: float32 [1536, 256], P(('seq', 'ctx'))
- grad_b_value: float32 [256], P(('seq', 'ctx'))
- grad_w_out: float32 [1536, 1536], P(('seq', 'ctx'))
- grad_norm_attn: float32 [1536], P(('seq', 'ctx'))
- grad_w_gate: float32 [1536, 8960], P(('seq', 'ctx'))
- grad_w_up: float32 [1536, 8960], P(('seq', 'ctx'))
- grad_w_down: float32 [8960, 1536], P(('seq', 'ctx'))
- grad_norm_mlp: float32 [1536], P(('seq', 'ctx'))
Inputs may be any that keep to these rules, and one draw needn't show every extreme that they name: `segments`: within each sequence the ids never fall, and a document's id is the place of its first token. One sequence, which one drawn from the seed, is a single document of 1024 tokens; in every other sequence the last token is a document of its own.
All inputs are finite; a program needn't handle non-finite values.
Results may differ from a plain program's by a relative error of at most 0.033.
Values may be sent and summed in bfloat16 or wider, within the bound.
No kernel may reach another device: no remote copies, remote signals or barrier semaphores. Data moves between devices by JAX's collectives and lax.ppermute only.
A program may use at most 512 MiB of HBM per device.

v0:
```python
import math

import jax
import jax.numpy as jnp
from jax import lax
from jax.sharding import PartitionSpec as P

HEADS = 12
KV_HEADS = 2
HEAD_DIM = 128
WIDTH = 1536
KV_WIDTH = 256


EPS = 1e-06
THETA = 1000000.0
NEGATIVE = -1e30


def doc_positions(ident):
    length = ident.shape[0]
    index = jnp.arange(length, dtype=jnp.int32)
    boundary = jnp.concatenate([jnp.ones((1,), jnp.bool_), ident[1:] != ident[:-1]])
    first = lax.cummax(jnp.where(boundary, index, 0), axis=0)
    return index - first


def rope_tables(positions):
    half = HEAD_DIM // 2
    freqs = THETA ** (-(2.0 * jnp.arange(half, dtype=jnp.float32)) / HEAD_DIM)
    angles = positions.astype(jnp.float32)[:, None] * freqs[None, :]
    cosine = jnp.concatenate([jnp.cos(angles), jnp.cos(angles)], axis=-1)[:, None, :]
    sine = jnp.concatenate([jnp.sin(angles), jnp.sin(angles)], axis=-1)[:, None, :]
    return (cosine, sine)


def rotate(values, cosine, sine, sign):
    half = values.shape[-1] // 2
    turned = jnp.concatenate([-values[..., half:], values[..., :half]], axis=-1)
    return values * cosine + sign * turned * sine


def inverse_rms(values):
    return lax.rsqrt(jnp.mean(values * values, axis=-1, keepdims=True) + EPS)


def matmul(left, right):
    return jnp.dot(left, right, preferred_element_type=jnp.float32)


def against(left, weight):
    return lax.dot_general(
        left, weight, (((1,), (1,)), ((), ())), preferred_element_type=jnp.float32
    )


def outer(left, right):
    return lax.dot_general(
        left, right, (((0,), (0,)), ((), ())), preferred_element_type=jnp.float32
    )


def block_scores(queries, keys, query_index, query_ids, start, ident):
    rows = queries.shape[0]
    count = keys.shape[0]
    group = HEADS // KV_HEADS
    query_group = queries.reshape(rows, KV_HEADS, group, HEAD_DIM)
    key_group = keys.reshape(count, KV_HEADS, HEAD_DIM)
    scores = jnp.einsum(
        "qkgd,skd->kgqs", query_group, key_group, preferred_element_type=jnp.float32
    ) * HEAD_DIM ** (-0.5)
    key_index = start + jnp.arange(count, dtype=jnp.int32)
    key_ids = lax.dynamic_slice_in_dim(ident, start, count)
    allowed = (key_index[None, :] <= query_index[:, None]) & (
        key_ids[None, :] == query_ids[:, None]
    )
    return (scores, allowed)


def stats_step(carry, keys, start, context):
    queries, query_index, query_ids, ident = context
    top, total = carry
    scores, allowed = block_scores(queries, keys, query_index, query_ids, start, ident)
    newtop = jnp.maximum(top, jnp.max(jnp.where(allowed, scores, NEGATIVE), axis=-1))
    weights = jnp.where(allowed, jnp.exp(scores - newtop[..., None]), 0.0)
    return (newtop, jnp.sum(weights, axis=-1))


def mixing_step(carry, keys, values, start, context):
    queries, query_index, query_ids, ident, logsum = context
    mixing, exact = carry
    scores, allowed = block_scores(queries, keys, query_index, query_ids, start, ident)
    shares = jnp.where(allowed, jnp.exp(scores - logsum[..., None]), 0.0)
    value_group = values.reshape(values.shape[0], KV_HEADS, HEAD_DIM)
    mixing = mixing + jnp.einsum(
        "kgqs,skd->kgqd",
        shares.astype(jnp.bfloat16),
        value_group,
        preferred_element_type=jnp.float32,
    )
    exact = exact + jnp.einsum(
        "kgqs,skd->kgqd",
        shares,
        value_group.astype(jnp.float32),
        precision=lax.Precision.HIGHEST,
        preferred_element_type=jnp.float32,
    )
    return (mixing, exact)


def backward_step(grad_query, keys, values, start, context):
    queries, query_index, query_ids, ident, grad_mixed, logsum, delta = context
    scores, allowed = block_scores(queries, keys, query_index, query_ids, start, ident)
    shares = jnp.where(allowed, jnp.exp(scores - logsum[..., None]), 0.0)
    rows = queries.shape[0]
    count = keys.shape[0]
    group = HEADS // KV_HEADS
    grad_group = grad_mixed.reshape(rows, KV_HEADS, group, HEAD_DIM)
    query_group = queries.reshape(rows, KV_HEADS, group, HEAD_DIM)
    key_group = keys.reshape(count, KV_HEADS, HEAD_DIM)
    value_group = values.reshape(count, KV_HEADS, HEAD_DIM)
    grad_shares = jnp.einsum(
        "qkgd,skd->kgqs", grad_group, value_group, preferred_element_type=jnp.float32
    )
    grad_value = jnp.einsum(
        "kgqs,qkgd->skd",
        shares.astype(jnp.bfloat16),
        grad_group,
        preferred_element_type=jnp.float32,
    )
    grad_scores = (shares * (grad_shares - delta[..., None])).astype(jnp.bfloat16)
    factor = HEAD_DIM ** (-0.5)
    grad_query = grad_query + factor * jnp.einsum(
        "kgqs,skd->qkgd", grad_scores, key_group, preferred_element_type=jnp.float32
    )
    grad_key = factor * jnp.einsum(
        "kgqs,qkgd->skd", grad_scores, query_group, preferred_element_type=jnp.float32
    )
    return (grad_query, (grad_key.reshape(count, KV_WIDTH), grad_value.reshape(count, KV_WIDTH)))


def body(
    tokens,
    segments,
    w_query,
    b_query,
    w_key,
    b_key,
    w_value,
    b_value,
    w_out,
    norm_attn,
    w_gate,
    w_up,
    w_down,
    norm_mlp,
    cotangent,
):
    rows = tokens.shape[0]
    ident = segments[0]
    length = ident.shape[0]
    group = HEADS // KV_HEADS
    offset = lax.axis_index("ctx") * rows
    query_index = offset + jnp.arange(rows, dtype=jnp.int32)
    query_ids = lax.dynamic_slice_in_dim(ident, offset, rows)
    positions = lax.dynamic_slice_in_dim(doc_positions(ident), offset, rows)
    cosine, sine = rope_tables(positions)
    block = math.gcd(512, length)
    starts = jnp.arange(0, length, block, dtype=jnp.int32)
    attn_set = (
        lax.all_gather(w_query, ("seq", "ctx"), axis=0, tiled=True),
        lax.all_gather(b_query, ("seq", "ctx"), axis=0, tiled=True),
        lax.all_gather(w_key, ("seq", "ctx"), axis=0, tiled=True),
        lax.all_gather(w_value, ("seq", "ctx"), axis=0, tiled=True),
        lax.all_gather(b_value, ("seq", "ctx"), axis=0, tiled=True),
        lax.all_gather(w_out, ("seq", "ctx"), axis=0, tiled=True),
        lax.all_gather(norm_attn, ("seq", "ctx"), axis=0, tiled=True),
    )
    query_weight, query_bias, key_weight, value_weight, value_bias, out_weight, attn_gain = attn_set
    inputs = tokens.astype(jnp.float32)
    scale_attn = inverse_rms(inputs)
    normed = (inputs * scale_attn * attn_gain.astype(jnp.float32)).astype(jnp.bfloat16)
    query_pre = matmul(normed, query_weight) + query_bias.astype(jnp.float32)
    key_pre = matmul(normed, key_weight) + b_key.astype(jnp.float32)
    value_low = (matmul(normed, value_weight) + value_bias.astype(jnp.float32)).astype(jnp.bfloat16)
    query_rot = (
        rotate(query_pre.reshape(rows, HEADS, HEAD_DIM), cosine, sine, 1.0)
        .reshape(rows, WIDTH)
        .astype(jnp.bfloat16)
    )
    key_rot = (
        rotate(key_pre.reshape(rows, KV_HEADS, HEAD_DIM), cosine, sine, 1.0)
        .reshape(rows, KV_WIDTH)
        .astype(jnp.bfloat16)
    )
    context = (query_rot, query_index, query_ids, ident)
    start_state = (
        jnp.full((KV_HEADS, group, rows), NEGATIVE, jnp.float32),
        jnp.zeros((KV_HEADS, group, rows), jnp.float32),
    )
    top, total = stats_step(
        start_state, lax.all_gather(key_rot, "ctx", axis=0, tiled=True), jnp.int32(0), context
    )
    keys_all, values_all = (
        lax.all_gather(key_rot, "ctx", axis=0, tiled=True),
        lax.all_gather(value_low, "ctx", axis=0, tiled=True),
    )
    logsum = top + jnp.log(total)
    key_blocks = keys_all.reshape(-1, block, KV_WIDTH)
    value_blocks = values_all.reshape(-1, block, KV_WIDTH)
    mix_context = (query_rot, query_index, query_ids, ident, logsum)

    def mix_scan(carry, item):
        return (mixing_step(carry, item[0], item[1], item[2], mix_context), None)

    empty = jnp.zeros((KV_HEADS, group, rows, HEAD_DIM), jnp.float32)
    mixing, exact = lax.scan(mix_scan, (empty, empty), (key_blocks, value_blocks, starts))[0]
    mixed = mixing.transpose(2, 0, 1, 3).reshape(rows, WIDTH).astype(jnp.bfloat16)
    middle = inputs + matmul(mixed, out_weight)
    mlp_set = (
        lax.all_gather(w_gate, ("seq", "ctx"), axis=0, tiled=True),
        lax.all_gather(w_up, ("seq", "ctx"), axis=0, tiled=True),
        lax.all_gather(w_down, ("seq", "ctx"), axis=0, tiled=True),
        lax.all_gather(norm_mlp, ("seq", "ctx"), axis=0, tiled=True),
    )
    gate_weight, up_weight, down_weight, mlp_gain = mlp_set
    scale_mlp = inverse_rms(middle)
    normed_mlp = (middle * scale_mlp * mlp_gain.astype(jnp.float32)).astype(jnp.bfloat16)
    gate = matmul(normed_mlp, gate_weight)
    upper = matmul(normed_mlp, up_weight)
    hidden = (jax.nn.silu(gate) * upper).astype(jnp.bfloat16)
    output = middle + matmul(hidden, down_weight)
    gate_back, up_back, down_back, gain_back = (
        lax.all_gather(w_gate, ("seq", "ctx"), axis=0, tiled=True),
        lax.all_gather(w_up, ("seq", "ctx"), axis=0, tiled=True),
        lax.all_gather(w_down, ("seq", "ctx"), axis=0, tiled=True),
        lax.all_gather(norm_mlp, ("seq", "ctx"), axis=0, tiled=True),
    )
    grad_hidden = against(cotangent, down_back)
    logistic = jax.nn.sigmoid(gate)
    grad_gate = (grad_hidden * upper * logistic * (1.0 + gate * (1.0 - logistic))).astype(
        jnp.bfloat16
    )
    grad_upper = (grad_hidden * gate * logistic).astype(jnp.bfloat16)
    grad_normed_mlp = against(grad_gate, gate_back) + against(grad_upper, up_back)
    grad_norm_mlp = jnp.sum(grad_normed_mlp * middle * scale_mlp, axis=0)
    weighted_mlp = grad_normed_mlp * gain_back.astype(jnp.float32)
    grad_middle = (
        cotangent.astype(jnp.float32)
        + scale_mlp * weighted_mlp
        - middle
        * (scale_mlp * scale_mlp * scale_mlp)
        * jnp.mean(weighted_mlp * middle, axis=-1, keepdims=True)
    )
    grad_w_down = outer(hidden, cotangent)
    grad_w_gate = outer(normed_mlp, grad_gate)
    grad_w_up = outer(normed_mlp, grad_upper)
    sum_gate, sum_up, sum_down, sum_gain = (
        lax.psum_scatter(grad_w_gate, ("seq", "ctx"), scatter_dimension=0, tiled=True),
        lax.psum_scatter(grad_w_up, ("seq", "ctx"), scatter_dimension=0, tiled=True),
        lax.psum_scatter(grad_w_down, ("seq", "ctx"), scatter_dimension=0, tiled=True),
        lax.psum_scatter(grad_norm_mlp, ("seq", "ctx"), scatter_dimension=0, tiled=True),
    )
    query_back, key_back, value_back, out_back, attn_gain_back = (
        lax.all_gather(w_query, ("seq", "ctx"), axis=0, tiled=True),
        lax.all_gather(w_key, ("seq", "ctx"), axis=0, tiled=True),
        lax.all_gather(w_value, ("seq", "ctx"), axis=0, tiled=True),
        lax.all_gather(w_out, ("seq", "ctx"), axis=0, tiled=True),
        lax.all_gather(norm_attn, ("seq", "ctx"), axis=0, tiled=True),
    )
    grad_branch = grad_middle.astype(jnp.bfloat16)
    grad_w_out = outer(mixed, grad_branch)
    grad_mixed = against(grad_branch, out_back).astype(jnp.bfloat16)
    grad_heads = (
        grad_mixed.reshape(rows, KV_HEADS, group, HEAD_DIM)
        .astype(jnp.float32)
        .transpose(1, 2, 0, 3)
    )
    delta = jnp.sum(grad_heads * exact, axis=-1)
    back_context = (query_rot, query_index, query_ids, ident, grad_mixed, logsum, delta)

    def back_scan(carry, item):
        return backward_step(carry, item[0], item[1], item[2], back_context)

    grad_query_rot, terms = lax.scan(
        back_scan,
        jnp.zeros((rows, KV_HEADS, group, HEAD_DIM), jnp.float32),
        (key_blocks, value_blocks, starts),
    )
    key_sum, value_sum = (
        lax.psum_scatter(
            terms[0].reshape(length, KV_WIDTH).astype(jnp.bfloat16),
            "ctx",
            scatter_dimension=0,
            tiled=True,
        ).astype(jnp.float32),
        lax.psum_scatter(
            terms[1].reshape(length, KV_WIDTH).astype(jnp.bfloat16),
            "ctx",
            scatter_dimension=0,
            tiled=True,
        ).astype(jnp.float32),
    )
    grad_query = (
        rotate(grad_query_rot.reshape(rows, HEADS, HEAD_DIM), cosine, sine, -1.0)
        .reshape(rows, WIDTH)
        .astype(jnp.bfloat16)
    )
    grad_key = (
        rotate(key_sum.reshape(rows, KV_HEADS, HEAD_DIM), cosine, sine, -1.0)
        .reshape(rows, KV_WIDTH)
        .astype(jnp.bfloat16)
    )
    grad_value = value_sum.astype(jnp.bfloat16)
    grad_w_query = outer(normed, grad_query)
    grad_b_query = jnp.sum(grad_query.astype(jnp.float32), axis=0)
    grad_w_key = outer(normed, grad_key)
    grad_b_key = lax.psum(jnp.sum(grad_key.astype(jnp.float32), axis=0), ("seq", "ctx"))
    grad_w_value = outer(normed, grad_value)
    grad_b_value = jnp.sum(grad_value.astype(jnp.float32), axis=0)
    grad_normed = (
        against(grad_query, query_back)
        + against(grad_key, key_back)
        + against(grad_value, value_back)
    )
    grad_norm_attn = jnp.sum(grad_normed * inputs * scale_attn, axis=0)
    weighted_attn = grad_normed * attn_gain_back.astype(jnp.float32)
    grad_tokens = (
        grad_middle
        + scale_attn * weighted_attn
        - inputs
        * (scale_attn * scale_attn * scale_attn)
        * jnp.mean(weighted_attn * inputs, axis=-1, keepdims=True)
    )
    attn_sums = (
        lax.psum_scatter(grad_w_query, ("seq", "ctx"), scatter_dimension=0, tiled=True),
        lax.psum_scatter(grad_b_query, ("seq", "ctx"), scatter_dimension=0, tiled=True),
        lax.psum_scatter(grad_w_key, ("seq", "ctx"), scatter_dimension=0, tiled=True),
        lax.psum_scatter(grad_w_value, ("seq", "ctx"), scatter_dimension=0, tiled=True),
        lax.psum_scatter(grad_b_value, ("seq", "ctx"), scatter_dimension=0, tiled=True),
        lax.psum_scatter(grad_w_out, ("seq", "ctx"), scatter_dimension=0, tiled=True),
        lax.psum_scatter(grad_norm_attn, ("seq", "ctx"), scatter_dimension=0, tiled=True),
    )
    return (
        output,
        grad_tokens,
        attn_sums[0],
        attn_sums[1],
        attn_sums[2],
        grad_b_key,
        attn_sums[3],
        attn_sums[4],
        attn_sums[5],
        attn_sums[6],
        sum_gate,
        sum_up,
        sum_down,
        sum_gain,
    )


def solution(mesh):
    return jax.shard_map(
        body,
        mesh=mesh,
        in_specs=(
            P(("seq", "ctx"), None),
            P("seq", None),
            P(("seq", "ctx"), None),
            P(("seq", "ctx")),
            P(("seq", "ctx"), None),
            P(),
            P(("seq", "ctx"), None),
            P(("seq", "ctx")),
            P(("seq", "ctx"), None),
            P(("seq", "ctx")),
            P(("seq", "ctx"), None),
            P(("seq", "ctx"), None),
            P(("seq", "ctx"), None),
            P(("seq", "ctx")),
            P(("seq", "ctx"), None),
        ),
        out_specs=(
            P(("seq", "ctx"), None),
            P(("seq", "ctx"), None),
            P(("seq", "ctx"), None),
            P(("seq", "ctx")),
            P(("seq", "ctx"), None),
            P(),
            P(("seq", "ctx"), None),
            P(("seq", "ctx")),
            P(("seq", "ctx"), None),
            P(("seq", "ctx")),
            P(("seq", "ctx"), None),
            P(("seq", "ctx"), None),
            P(("seq", "ctx"), None),
            P(("seq", "ctx")),
        ),
        check_vma=False,
    )
```

profile of v0, /device:TPU:0, one launch (start us, length us, event | category | flops | bytes accessed | tf_op | source)
XLA Modules:
  0.0 2780.4 jit_solution(2542129656698086505)
XLA Ops:
  14.7 42.6 %all-reduce.10 = (bf16[1536]{0:T(1024)(128)(2,1)S(1)}, bf16[1536]{0:T(1024)(128)(2,1)S(1)}, bf16[256]{0:T(256)(128)(2,1)S(1)}, bf16[1536]{0:T(1024)(128)(2,1)S(1)}) all-reduce(bf16[1536]{0:T(1024)(128)(2,1)S(1)} %dynamic-update-slice, bf16[1536]{0:T(1024)(128)(2,1)S(1)} %dynamic-update-slice.1, ...), channel_id=1, replica_groups=mesh['seq'=4,'ctx'=8] {'seq','ctx'}, use_global_device_ids=true, to_apply=%add | all-reduce | flops 4864 | bytes 19456
  58.0 72.9 %all_gather.50 = bf16[1536,256]{1,0:T(8,128)(2,1)S(1)} all-gather(bf16[48,256]{1,0:T(8,128)(2,1)S(1)} %copy-done.49), channel_id=1, replica_groups=mesh['seq'=4,'ctx'=8] {'seq','ctx'}, dimensions={0}, use_global_device_ids=true | all-gather | bytes 811008 | tf_op jit(solution)/shard_map/all_gather | solution.py:173
  135.3 31.8 %all_gather.51 = bf16[1024,256]{1,0:T(8,128)(2,1)S(1)} all-gather(bf16[128,256]{1,0:T(8,128)(2,1)S(1)} %fusion.63), channel_id=1, replica_groups=mesh['seq'=4,'ctx'=8] {'ctx'}, dimensions={0}, use_global_device_ids=true | all-gather | bytes 589824 | tf_op jit(solution)/shard_map/all_gather | solution.py:205
  169.4 75.0 %all_gather.54 = bf16[1536,256]{1,0:T(8,128)(2,1)S(1)} all-gather(bf16[48,256]{1,0:T(8,128)(2,1)S(1)} %copy-done.50), channel_id=1, replica_groups=mesh['seq'=4,'ctx'=8] {'seq','ctx'}, dimensions={0}, use_global_device_ids=true | all-gather | bytes 811008 | tf_op jit(solution)/shard_map/all_gather | solution.py:174
  245.6 34.0 %all_gather.56 = bf16[1024,256]{1,0:T(8,128)(2,1)S(1)} all-gather(bf16[128,256]{1,0:T(8,128)(2,1)S(1)} %fusion.46), channel_id=1, replica_groups=mesh['seq'=4,'ctx'=8] {'ctx'}, dimensions={0}, use_global_device_ids=true | all-gather | bytes 589824 | tf_op jit(solution)/shard_map/all_gather | solution.py:206
  292.4 29.6 %while.28 = (s32[]{:T(128)}, f32[2,6,128,128]{3,2,1,0:T(8,128)}, f32[2,6,128,128]{3,2,1,0:T(8,128)}, s32[2]{0:T(128)}, s32[1024]{0:T(1024)S(1)}, /*index=5*/s32[...) while((s32[]{:T(128)}, f32[2,6,128,128]{3,2,1,0:T(8,128)}, ...), condition=%wide.region_6.7_spmd.clone, body=%wide.region_5.6_spmd.clone.sunk | while | flops 1617101440 | bytes 22658972 | solution.py:217
  348.3 152.2 %all-gather.12.cloned.1.call-done = bf16[1536,8960]{1,0:T(8,128)(2,1)} async-done(((bf16[48,8960]{1,0:T(8,128)(2,1)}), bf16[1536,8960]{1,0:T(8,128)(2,1)}) %all-gather.12.cloned.1.call-update) | async-done | bytes 27525136 | tf_op jit(solution)/shard_map/all_gather | solution.py:222
  515.3 152.1 %all-gather.14.cloned.1.call-done = bf16[8960,1536]{1,0:T(8,128)(2,1)} async-done(((bf16[280,1536]{1,0:T(8,128)(2,1)}), bf16[8960,1536]{1,0:T(8,128)(2,1)}) %all-gather.14.cloned.1.call-update) | async-done | bytes 27525136 | tf_op jit(solution)/shard_map/all_gather | solution.py:223
  667.4 17.7 multiply_convert_fusion
  685.1 15.6 fusion.78
  700.7 15.5 multiply_reduce_fusion
  724.1 29.9 %while.29 = (s32[]{:T(128)}, f32[128,2,6,128]{0,3,2,1:T(8,128)S(1)}, bf16[2,512,256]{1,2,0:T(8,128)(2,1)}, bf16[2,512,256]{2,1,0:T(8,128)(2,1)}, bf16[2,512,256]...) while((s32[]{:T(128)}, ...), condition=%wide.region_11.12_spmd.clone, body=%wide.region_10.11_spmd.clone.sunk | while | flops 1015546496 | bytes 45578168 | solution.py:285
  757.0 59.3 %reduce-scatter.12.cloned.1.call-done = bf16[128,256]{1,0:T(8,128)(2,1)} async-done(((bf16[1024,256]{1,0:T(8,128)(2,1)}), bf16[128,256]{1,0:T(8,128)(2,1)}) %reduce-scatter.12.cloned.1.call-update) | async-done | bytes 65552 | tf_op jit(solution)/shard_map/reduce_scatter | solution.py:291
  820.8 60.1 %reduce-scatter.14.cloned.1.call-done = bf16[128,256]{1,0:T(8,128)(2,1)} async-done(((bf16[1024,256]{1,0:T(8,128)(2,1)}), bf16[128,256]{1,0:T(8,128)(2,1)}) %reduce-scatter.14.cloned.1.call-update) | async-done | bytes 65552 | tf_op jit(solution)/shard_map/reduce_scatter | solution.py:297
  897.5 23.4 fusion.80
  921.0 23.2 fusion.81
  945.2 23.1 fusion.82
  988.0 40.8 %all-reduce.9 = (f32[1536]{0:T(1024)S(1)}, f32[256]{0:T(256)}, f32[256]{0:T(256)S(1)}, f32[1536]{0:T(1024)S(1)}, f32[1536]{0:T(1024)S(1)}) all-reduce(f32[1536]{0:T(1024)S(1)} %copy-done.45, f32[256]{0:T(256)S(1)} %copy-done.53, f32[256]{0:T(256)S(1)} %convert_reduce_fusion.1, ...), channel_id=5, replica_groups=mesh['seq'=4,'ctx'=8] {'seq','ctx'}, use_global_device_ids=true, to_apply=%region_17.18.clone | all-reduce | flops 5120 | bytes 40960
  1032.3 52.3 %reduce-scatter.20.cloned.1.call-done = f32[48,256]{1,0:T(8,128)} async-done(((f32[1536,256]{1,0:T(8,128)}), f32[48,256]{1,0:T(8,128)}) %reduce-scatter.20.cloned.1.call-update) | async-done | bytes 49168 | tf_op jit(solution)/shard_map/reduce_scatter | solution.py:339
  1084.6 140.9 %reduce-scatter.16.cloned.1.call-done = f32[48,1536]{1,0:T(8,128)} async-done(((f32[1536,1536]{1,0:T(8,128)}), f32[48,1536]{1,0:T(8,128)}) %reduce-scatter.16.cloned.1.call-update) | async-done | bytes 294928 | tf_op jit(solution)/shard_map/reduce_scatter | solution.py:336
  1225.5 142.1 %reduce-scatter.22.cloned.1.call-done = f32[48,1536]{1,0:T(8,128)} async-done(((f32[1536,1536]{1,0:T(8,128)}), f32[48,1536]{1,0:T(8,128)}) %reduce-scatter.22.cloned.1.call-update) | async-done | bytes 294928 | tf_op jit(solution)/shard_map/reduce_scatter | solution.py:341
  1367.6 468.2 %reduce-scatter.24.cloned.1.call-done = f32[48,8960]{1,0:T(8,128)} async-done(((f32[1536,8960]{1,0:T(8,128)}), f32[48,8960]{1,0:T(8,128)}) %reduce-scatter.24.cloned.1.call-update) | async-done | bytes 1720336 | tf_op jit(solution)/shard_map/reduce_scatter | solution.py:259
  1835.8 469.5 %reduce-scatter.26.cloned.1.call-done = f32[48,8960]{1,0:T(8,128)} async-done(((f32[1536,8960]{1,0:T(8,128)}), f32[48,8960]{1,0:T(8,128)}) %reduce-scatter.26.cloned.1.call-update) | async-done | bytes 1720336 | tf_op jit(solution)/shard_map/reduce_scatter | solution.py:260
  2305.4 468.3 %reduce-scatter.28.cloned.1.call-done = f32[280,1536]{1,0:T(8,128)} async-done(((f32[8960,1536]{1,0:T(8,128)}), f32[280,1536]{1,0:T(8,128)}) %reduce-scatter.28.cloned.1.call-update) | async-done | bytes 1720336
  (318 shorter events, 176.7 us)
Async XLA Ops:
  7.2 50.1 %copy-start.2 = (bf16[128,1536]{1,0:T(8,128)(2,1)S(1)}, bf16[128,1536]{1,0:T(8,128)(2,1)}, u32[]{:S(2)}) copy-start(bf16[128,1536]{1,0:T(8,128)(2,1)} %param.19) | copy-start | bytes 1179652
  7.2 50.8 %copy-start.49 = (bf16[48,256]{1,0:T(8,128)(2,1)S(1)}, bf16[48,256]{1,0:T(8,128)(2,1)}, u32[]{:S(2)}) copy-start(bf16[48,256]{1,0:T(8,128)(2,1)} %param.23) | copy-start | bytes 73732
  7.2 125.0 %copy-start.42 = (s32[1,1024]{1,0:T(1,128)S(1)}, s32[1,1024]{1,0:T(1,128)}, u32[]{:S(2)}) copy-start(s32[1,1024]{1,0:T(1,128)} %param.20) | copy-start | bytes 12292
  7.2 275.3 %all-gather.6.cloned.1.call-start = ((), (), s32[]{:S(2)}) async-start(), calls=%async_computation.9 | async-start | bytes 4866048 | tf_op jit(solution)/shard_map/all_gather | solution.py:171
  7.9 317.9 %all-gather.8.cloned.1.call-start = ((), (), s32[]{:S(2)}) async-start(), calls=%async_computation.10 | async-start | bytes 4866048 | tf_op jit(solution)/shard_map/all_gather | solution.py:176
  8.7 324.9 %all-gather.10.cloned.1.call-start = ((), (), s32[]{:S(2)}) async-start(), calls=%async_computation.11 | async-start | bytes 28385280 | tf_op jit(solution)/shard_map/all_gather | solution.py:221
  9.4 491.1 %all-gather.12.cloned.1.call-start = ((), (), s32[]{:S(2)}) async-start(), calls=%async_computation.12 | async-start | bytes 28385280 | tf_op jit(solution)/shard_map/all_gather | solution.py:222
  10.0 657.4 %all-gather.14.cloned.1.call-start = ((), (), s32[]{:S(2)}) async-start(), calls=%async_computation.13 | async-start | bytes 28385280 | tf_op jit(solution)/shard_map/all_gather | solution.py:223
  10.6 805.7 %reduce-scatter.12.cloned.1.call-start = ((), (), s32[]{:S(2)}) async-start(), calls=%async_computation.14 | async-start | bytes 589824 | tf_op jit(solution)/shard_map/reduce_scatter | solution.py:291
  58.0 224.5 %copy-start.46 = (f32[128]{0:T(128)}, f32[128]{0:T(128)S(1)}, u32[]{:S(2)}) copy-start(f32[128]{0:T(128)S(1)} %get-tuple-element.389) | copy-start | bytes 1540
  329.2 387.0 %copy-start.4 = (f32[128,1536]{1,0:T(8,128)}, f32[128,1536]{1,0:T(8,128)S(1)}, u32[]{:S(2)}) copy-start(f32[128,1536]{1,0:T(8,128)S(1)} %get-tuple-element.395) | copy-start | bytes 2359300
  329.4 171.1 %copy-start.11 = (bf16[128,1536]{1,0:T(8,128)(2,1)}, bf16[128,1536]{1,0:T(8,128)(2,1)S(1)}, u32[]{:S(2)}) copy-start(bf16[128,1536]{1,0:T(8,128)(2,1)S(1)} %multiply_convert_fusion.3) | copy-start | bytes 1179652
  754.0 63.6 %copy-start.31 = (f32[128,2,128]{2,1,0:T(2,128)S(1)}, f32[128,2,128]{2,1,0:T(2,128)}, u32[]{:S(2)}) copy-start(f32[128,2,128]{2,1,0:T(2,128)} %copy-done.30) | copy-start | bytes 393220
  754.0 65.1 %copy-start.3 = (bf16[128,1536]{1,0:T(8,128)(2,1)S(1)}, bf16[128,1536]{1,0:T(8,128)(2,1)}, u32[]{:S(2)}) copy-start(bf16[128,1536]{1,0:T(8,128)(2,1)} %param.19) | copy-start | bytes 1179652
  754.0 65.1 %copy-start.47 = (f32[128]{0:T(128)S(1)}, f32[128]{0:T(128)}, u32[]{:S(2)}) copy-start(f32[128]{0:T(128)} %copy-done.46) | copy-start | bytes 1540
  756.1 124.8 %reduce-scatter.14.cloned.1.call-start = ((), (), s32[]{:S(2)}) async-start(), calls=%async_computation.15 | async-start | bytes 589824 | tf_op jit(solution)/shard_map/reduce_scatter | solution.py:297
  756.9 275.5 %reduce-scatter.18.cloned.1.call-start = ((), (), s32[]{:S(2)}) async-start(), calls=%async_computation.17 | async-start | bytes 1622016 | tf_op jit(solution)/shard_map/reduce_scatter | solution.py:338
  820.8 263.9 %reduce-scatter.20.cloned.1.call-start = ((), (), s32[]{:S(2)}) async-start(), calls=%async_computation.18 | async-start | bytes 1622016 | tf_op jit(solution)/shard_map/reduce_scatter | solution.py:339
  883.5 342.0 %reduce-scatter.16.cloned.1.call-start = ((), (), s32[]{:S(2)}) async-start(), calls=%async_computation.16 | async-start | bytes 9732096 | tf_op jit(solution)/shard_map/reduce_scatter | solution.py:336
  890.2 477.4 %reduce-scatter.22.cloned.1.call-start = ((), (), s32[]{:S(2)}) async-start(), calls=%async_computation.19 | async-start | bytes 9732096 | tf_op jit(solution)/shard_map/reduce_scatter | solution.py:341
  896.5 939.3 %reduce-scatter.24.cloned.1.call-start = ((), (), s32[]{:S(2)}) async-start(), calls=%async_computation.20 | async-start | bytes 56770560 | tf_op jit(solution)/shard_map/reduce_scatter | solution.py:259
  920.9 1384.4 %reduce-scatter.26.cloned.1.call-start = ((), (), s32[]{:S(2)}) async-start(), calls=%async_computation.21 | async-start | bytes 56770560 | tf_op jit(solution)/shard_map/reduce_scatter | solution.py:260
  944.3 1829.4 %reduce-scatter.28.cloned.1.call-start = ((), (), s32[]{:S(2)}) async-start(), calls=%async_computation.22 | async-start | bytes 56770560
  987.0 44.2 %copy-start.10 = (f32[128,1536]{1,0:T(8,128)S(1)}, f32[128,1536]{1,0:T(8,128)}, u32[]{:S(2)}) copy-start(f32[128,1536]{1,0:T(8,128)} %copy-done.8) | copy-start | bytes 2359300
  (60 other events, 350.7 us)
Sparse Core Ops, SparseCore 0:
  11.0 70.4 all-gather.5
  84.4 66.0 all-gather.7
  153.4 180.0 all-gather.9
  336.3 164.1 all-gather.11
  503.3 164.1 all-gather.13
  756.2 60.0 reduce-scatter.11
  820.0 60.9 reduce-scatter.13
  886.8 96.0 reduce-scatter.17
  988.7 95.8 reduce-scatter.19
  1091.0 134.4 reduce-scatter.15
  1233.0 134.5 reduce-scatter.21
  1374.4 461.3 reduce-scatter.23
  1844.0 461.3 reduce-scatter.25
  2312.2 461.4 reduce-scatter.27
where the time goes:
time: 2790 us; the launch traced here: 2780 us
  waiting for transfers between devices  2170 us (78%)
  blocking collectives  297 us (11%)
  matrix products  223 us (8%)
  local copies, waits for them, and re-layouts  41.5 us (1%)
    unnamed x15, waiting for transfers between devices  472 us
    reduce_scatter x1, waiting for transfers between devices, body(): lax.psum_scatter(grad_w_up, ('seq', 'ctx'), scatter_dimension=0, tiled=True)  470 us
    reduce_scatter x1, waiting for transfers between devices, body(): lax.psum_scatter(grad_w_gate, ('seq', 'ctx'), scatter_dimension=0, tiled=...  468 us
    all_gather x1, waiting for transfers between devices, body(): lax.all_gather(w_up, ('seq', 'ctx'), axis=0, tiled=True)  152 us
    all_gather x1, waiting for transfers between devices, body(): lax.all_gather(w_down, ('seq', 'ctx'), axis=0, tiled=True)  152 us
    reduce_scatter x1, waiting for transfers between devices, body(): lax.psum_scatter(grad_w_out, ('seq', 'ctx'), scatter_dimension=0, tiled=T...  142 us
    reduce_scatter x1, waiting for transfers between devices, body(): lax.psum_scatter(grad_w_query, ('seq', 'ctx'), scatter_dimension=0, tiled...  141 us
    dot_general x7, matrix products, outer(): lax.dot_general(left, right, (((0,), (0,)), ((), ())), preferred_element_...  83.9 us
  transfers between devices with their start and end apart: 14, of which 11 were waited for; matrix products, arithmetic and copies ran while one was open for 7% of the time, Pallas kernels for 0%

commit v1 on v0

v1 whole, which is shorter than its diff:
```python
import functools

import jax
import jax.numpy as jnp
from jax import lax
from jax.experimental import pallas as pl
from jax.experimental.pallas import tpu as pltpu
from jax.sharding import PartitionSpec as P

HEADS = 12
KV_HEADS = 2
HEAD_DIM = 128
WIDTH = 1536
KV_WIDTH = 256
GROUP = HEADS // KV_HEADS
QKV = WIDTH + 2 * KV_WIDTH

EPS = 1e-06
THETA = 1000000.0
NEGATIVE = -1e30
FACTOR = HEAD_DIM ** (-0.5)
VMEM_LIMIT = 56 * 1024 * 1024

ALL = ("seq", "ctx")
BF = jnp.bfloat16
F32 = jnp.float32


def rope_tables(positions):
    half = HEAD_DIM // 2
    freqs = THETA ** (-(2.0 * jnp.arange(half, dtype=F32)) / HEAD_DIM)
    angles = positions.astype(F32)[:, None] * freqs[None, :]
    cosine, sine = jnp.cos(angles), jnp.sin(angles)
    cosine = jnp.concatenate([cosine, cosine], axis=-1)
    sine = jnp.concatenate([sine, sine], axis=-1)
    return cosine, sine


def rotate(values, cosine, sine, sign):
    rows, width = values.shape
    split = values.reshape(rows, width // HEAD_DIM, HEAD_DIM)
    half = HEAD_DIM // 2
    turned = jnp.concatenate([-split[..., half:], split[..., :half]], axis=-1)
    out = split * cosine[:, None, :] + sign * turned * sine[:, None, :]
    return out.reshape(rows, width)


def inverse_rms(values):
    return lax.rsqrt(jnp.mean(values * values, axis=-1, keepdims=True) + EPS)


def matmul(left, right):
    return jnp.dot(left, right, preferred_element_type=F32)


def against(left, weight):
    return lax.dot_general(left, weight, (((1,), (1,)), ((), ())), preferred_element_type=F32)


def outer(left, right):
    return lax.dot_general(left, right, (((0,), (0,)), ((), ())), preferred_element_type=F32)


def allowed_of(lo_ref, hi_ref, rows, length):
    places = lax.broadcasted_iota(jnp.int32, (rows, length), 1)
    return (places >= lo_ref[...]) & (places <= hi_ref[...])


def forward_kernel(q_ref, k_ref, v_ref, lo_ref, hi_ref, mixed_ref, logsum_ref):
    scores = against(q_ref[...], k_ref[...]) * FACTOR
    allowed = allowed_of(lo_ref, hi_ref, *scores.shape)
    scores = jnp.where(allowed, scores, NEGATIVE)
    top = jnp.max(scores, axis=-1, keepdims=True)
    weights = jnp.exp(scores - top)
    total = jnp.sum(weights, axis=-1, keepdims=True)
    shares = (weights * (1.0 / total)).astype(BF)
    mixed_ref[...] = matmul(shares, v_ref[...]).astype(BF)
    logsum_ref[0] = top + jnp.log(total)


def backward_kernel(
    q_ref, k_ref, v_ref, g_ref, lo_ref, hi_ref, logsum_ref, dq_ref, dk_ref, dv_ref, dk_sum, dv_sum
):
    member = lax.rem(pl.program_id(0), GROUP)
    queries, keys, grads = q_ref[...], k_ref[...], g_ref[...]
    scores = against(queries, keys) * FACTOR
    allowed = allowed_of(lo_ref, hi_ref, *scores.shape)
    shares = jnp.where(allowed, jnp.exp(jnp.where(allowed, scores, NEGATIVE) - logsum_ref[0]), 0.0)
    grad_shares = against(grads, v_ref[...])
    delta = jnp.sum(shares * grad_shares, axis=-1, keepdims=True)
    grad_scores = (shares * (grad_shares - delta)).astype(BF)
    dq_ref[...] = matmul(grad_scores, keys) * FACTOR
    dk = outer(grad_scores, queries) * FACTOR
    dv = outer(shares.astype(BF), grads)

    @pl.when(member == 0)
    def _():
        dk_sum[...] = dk
        dv_sum[...] = dv

    @pl.when(member > 0)
    def _():
        dk_sum[...] += dk
        dv_sum[...] += dv

    @pl.when(member == GROUP - 1)
    def _():
        dk_ref[...] = dk_sum[...].astype(BF)
        dv_ref[...] = dv_sum[...].astype(BF)


def attention_forward(queries, keys, values, lo, hi):
    rows, length = queries.shape[0], keys.shape[0]
    head = pl.BlockSpec((rows, HEAD_DIM), lambda h: (0, h))
    kv = pl.BlockSpec((length, HEAD_DIM), lambda h: (0, h // GROUP))
    column = pl.BlockSpec((rows, 1), lambda h: (0, 0))
    stat = pl.BlockSpec((1, rows, 1), lambda h: (h, 0, 0))
    return pl.pallas_call(
        forward_kernel,
        grid=(HEADS,),
        in_specs=[head, kv, kv, column, column],
        out_specs=[head, stat],
        out_shape=[
            jax.ShapeDtypeStruct((rows, WIDTH), BF),
            jax.ShapeDtypeStruct((HEADS, rows, 1), F32),
        ],
        compiler_params=pltpu.CompilerParams(vmem_limit_bytes=VMEM_LIMIT),
        cost_estimate=pl.CostEstimate(
            flops=4 * rows * length * WIDTH,
            bytes_accessed=4 * length * KV_WIDTH + 4 * rows * WIDTH,
            transcendentals=rows * length * HEADS,
        ),
        name="attention_forward",
    )(queries, keys, values, lo, hi)


def attention_backward(queries, keys, values, grads, lo, hi, logsum):
    rows, length = queries.shape[0], keys.shape[0]
    head = pl.BlockSpec((rows, HEAD_DIM), lambda h: (0, h))
    kv = pl.BlockSpec((length, HEAD_DIM), lambda h: (0, h // GROUP))
    column = pl.BlockSpec((rows, 1), lambda h: (0, 0))
    stat = pl.BlockSpec((1, rows, 1), lambda h: (h, 0, 0))
    return pl.pallas_call(
        backward_kernel,
        grid=(HEADS,),
        in_specs=[head, kv, kv, head, column, column, stat],
        out_specs=[head, kv, kv],
        out_shape=[
            jax.ShapeDtypeStruct((rows, WIDTH), F32),
            jax.ShapeDtypeStruct((length, KV_WIDTH), BF),
            jax.ShapeDtypeStruct((length, KV_WIDTH), BF),
        ],
        scratch_shapes=[pltpu.VMEM((length, HEAD_DIM), F32), pltpu.VMEM((length, HEAD_DIM), F32)],
        compiler_params=pltpu.CompilerParams(vmem_limit_bytes=VMEM_LIMIT),
        cost_estimate=pl.CostEstimate(
            flops=10 * rows * length * WIDTH,
            bytes_accessed=8 * length * KV_WIDTH + 8 * rows * WIDTH,
            transcendentals=rows * length * HEADS,
        ),
        name="attention_backward",
    )(queries, keys, values, grads, lo, hi, logsum)


def gather(value, axis):
    return lax.all_gather(value, axis, axis=0, tiled=True)


def scatter_sum(value, axis):
    return lax.psum_scatter(value, axis, scatter_dimension=0, tiled=True)


def swap(value, axis):
    return lax.all_to_all(value, axis, 0, 0, tiled=True)


def body(
    tokens,
    segments,
    w_query,
    b_query,
    w_key,
    b_key,
    w_value,
    b_value,
    w_out,
    norm_attn,
    w_gate,
    w_up,
    w_down,
    norm_mlp,
    cotangent,
    *,
    seq,
    ctx,
):
    rows = tokens.shape[0]
    devices = seq * ctx
    share = w_query.shape[0]
    vshare = b_value.shape[0]
    ident = segments[0]
    length = ident.shape[0]
    offset = lax.axis_index("ctx") * rows
    hi = offset + jnp.arange(rows, dtype=jnp.int32)
    lo = lax.dynamic_slice_in_dim(ident, offset, rows)
    cosine_all, sine_all = rope_tables(jnp.arange(length, dtype=jnp.int32) - ident)
    cosine = lax.dynamic_slice_in_dim(cosine_all, offset, rows)
    sine = lax.dynamic_slice_in_dim(sine_all, offset, rows)
    hi, lo = hi[:, None], lo[:, None]

    small = jnp.stack([norm_attn, norm_mlp, b_query, jnp.pad(b_value, (0, share - vshare))], axis=1)
    small = jnp.pad(small, ((0, 0), (0, 124)))
    proj = gather(jnp.concatenate([w_query, w_key, w_value, small], axis=1), ALL)
    qkv_weight = proj[:, :QKV]
    vectors = proj[:, QKV:QKV + 4].astype(F32).T
    attn_gain, mlp_gain, query_bias = vectors[0][None], vectors[1][None], vectors[2][None]
    value_bias = vectors[3].reshape(devices, share)[:, :vshare].reshape(1, KV_WIDTH)
    tokens_all = gather(tokens, "ctx")
    out_weight = gather(w_out, ALL)

    hidden_share = w_down.shape[0]
    chunk = seq * hidden_share

    def to_columns(weight):
        parts = weight.reshape(share, seq, ctx, hidden_share).transpose(2, 0, 1, 3)
        return parts.reshape(ctx * share, chunk)

    gate_weight = gather(swap(to_columns(w_gate), "ctx"), "seq")
    up_weight = gather(swap(to_columns(w_up), "ctx"), "seq")
    down_weight = gather(w_down, "seq")
    cotangent_all = gather(cotangent, "ctx")

    inputs = tokens.astype(F32)
    scale_attn = inverse_rms(inputs)
    normed = (inputs * scale_attn * attn_gain).astype(BF)
    inputs_all = tokens_all.astype(F32)
    normed_all = (inputs_all * inverse_rms(inputs_all) * attn_gain).astype(BF)
    query_pre = matmul(normed, qkv_weight[:, :WIDTH]) + query_bias
    key_value = matmul(normed_all, qkv_weight[:, WIDTH:])
    queries = rotate(query_pre, cosine, sine, 1.0).astype(BF)
    keys = rotate(key_value[:, :KV_WIDTH] + b_key.astype(F32)[None], cosine_all, sine_all, 1.0).astype(BF)
    values = (key_value[:, KV_WIDTH:] + value_bias).astype(BF)
    mixed, logsum = attention_forward(queries, keys, values, lo, hi)
    middle = inputs + matmul(mixed, out_weight)

    scale_mlp = inverse_rms(middle)
    normed_mlp = gather((middle * scale_mlp * mlp_gain).astype(BF), "ctx")
    gate = matmul(normed_mlp, gate_weight)
    upper = matmul(normed_mlp, up_weight)
    grad_hidden = against(cotangent_all, down_weight)
    logistic = jax.nn.sigmoid(gate)
    hidden = (gate * logistic * upper).astype(BF)
    grad_gate = (grad_hidden * upper * logistic * (1.0 + gate * (1.0 - logistic))).astype(BF)
    grad_upper = (grad_hidden * gate * logistic).astype(BF)
    back = against(grad_gate, gate_weight) + against(grad_upper, up_weight)
    grad_normed_mlp = scatter_sum(back.astype(BF), "ctx").astype(F32)
    output = middle + scatter_sum(matmul(hidden, down_weight).astype(BF), "ctx").astype(F32)

    grad_w_down = scatter_sum(outer(hidden, cotangent_all).astype(BF), "seq").astype(F32)

    def from_columns(grad):
        parts = swap(scatter_sum(grad.astype(BF), "seq"), "ctx").astype(F32)
        parts = parts.reshape(ctx, share, seq, hidden_share).transpose(1, 2, 0, 3)
        return parts.reshape(share, devices * hidden_share)

    grad_w_gate = from_columns(outer(normed_mlp, grad_gate))
    grad_w_up = from_columns(outer(normed_mlp, grad_upper))

    cotangent_wide = cotangent.astype(F32)
    grad_norm_mlp = jnp.sum(grad_normed_mlp * middle * scale_mlp, axis=0)
    weighted_mlp = grad_normed_mlp * mlp_gain
    grad_middle = (
        cotangent_wide
        + scale_mlp * weighted_mlp
        - middle * (scale_mlp * scale_mlp * scale_mlp) * jnp.mean(weighted_mlp * middle, axis=-1, keepdims=True)
    )

    grad_branch = grad_middle.astype(BF)
    grad_mixed = against(grad_branch, out_weight).astype(BF)
    grad_w_out = scatter_sum(outer(mixed, grad_branch).astype(BF), ALL).astype(F32)
    dq, dk, dv = attention_backward(queries, keys, values, grad_mixed, lo, hi, logsum)
    terms = swap(jnp.concatenate([dk, dv], axis=1), "ctx").reshape(ctx, rows, 2 * KV_WIDTH)
    terms = jnp.sum(terms.astype(F32), axis=0)
    grad_query = rotate(dq, cosine, sine, -1.0).astype(BF)
    grad_key = rotate(terms[:, :KV_WIDTH], cosine, sine, -1.0).astype(BF)
    grad_value = terms[:, KV_WIDTH:].astype(BF)
    grad_qkv = jnp.concatenate([grad_query, grad_key, grad_value], axis=1)

    columns = QKV // ctx
    turned = grad_qkv.reshape(rows, ctx, columns).transpose(1, 0, 2).reshape(ctx * rows, columns)
    grad_w_qkv = outer(normed_all, swap(turned, "ctx"))
    grad_w_qkv = swap(scatter_sum(grad_w_qkv.astype(BF), "seq"), "ctx").astype(F32)
    grad_w_qkv = grad_w_qkv.reshape(ctx, share, columns).transpose(1, 0, 2).reshape(share, QKV)

    grad_normed = against(grad_qkv, qkv_weight)
    grad_norm_attn = jnp.sum(grad_normed * inputs * scale_attn, axis=0)
    weighted_attn = grad_normed * attn_gain
    grad_tokens = (
        grad_middle
        + scale_attn * weighted_attn
        - inputs * (scale_attn * scale_attn * scale_attn) * jnp.mean(weighted_attn * inputs, axis=-1, keepdims=True)
    )

    bias = jnp.sum(grad_qkv.astype(F32), axis=0)
    parts = jnp.concatenate(
        [
            grad_norm_attn.reshape(devices, share),
            grad_norm_mlp.reshape(devices, share),
            bias[:WIDTH].reshape(devices, share),
            bias[WIDTH + KV_WIDTH:].reshape(devices, vshare),
            jnp.broadcast_to(bias[None, WIDTH:WIDTH + KV_WIDTH], (devices, KV_WIDTH)),
        ],
        axis=1,
    )
    sums = jnp.sum(swap(parts, ALL), axis=0)
    g_norm_attn, g_norm_mlp, g_b_query, g_b_value, g_b_key = jnp.split(
        sums, [share, 2 * share, 3 * share, 3 * share + vshare]
    )
    return (
        output,
        grad_tokens,
        grad_w_qkv[:, :WIDTH],
        g_b_query,
        grad_w_qkv[:, WIDTH:WIDTH + KV_WIDTH],
        g_b_key,
        grad_w_qkv[:, WIDTH + KV_WIDTH:],
        g_b_value,
        grad_w_out,
        g_norm_attn,
        grad_w_gate,
        grad_w_up,
        grad_w_down,
        g_norm_mlp,
    )


def solution(mesh):
    rows2, rows1 = P(ALL, None), P(ALL)
    return jax.shard_map(
        functools.partial(body, seq=mesh.shape["seq"], ctx=mesh.shape["ctx"]),
        mesh=mesh,
        in_specs=(
            rows2,
            P("seq", None),
            rows2,
            rows1,
            rows2,
            P(),
            rows2,
            rows1,
            rows2,
            rows1,
            rows2,
            rows2,
            rows2,
            rows1,
            rows2,
        ),
        out_specs=(
            rows2,
            rows2,
            rows2,
            rows1,
            rows2,
            P(),
            rows2,
            rows1,
            rows2,
            rows1,
            rows2,
            rows2,
            rows2,
            rows1,
        ),
        check_vma=False,
    )
```

time: 2790 us -> 899 us (0.32)
  waiting for transfers between devices: 2170 us -> 583 us
  blocking collectives: 297 us -> 45.6 us
  matrix products: 223 us -> 100 us
  starting transfers between devices: 1.14 us -> 30.9 us
    reduce_scatter x8 -> x7, waiting for transfers between devices: 1390 us -> 192 us  [scatter_sum(): return lax.psum_scatter(value, axis, scatter_dimension=0, tiled=True)]
    unnamed x15, waiting for transfers between devices: 472 us -> 2.93 us
    all_gather x4 -> x0, blocking collectives: 214 us -> none  [the longest x1 75 us: body(): lax.all_gather(w_value, ('seq', 'ctx'), axis=0, tiled=True)]
    all_to_all x0 -> x6, waiting for transfers between devices: none -> 92.2 us  [swap(): return lax.all_to_all(value, axis, 0, 0, tiled=True)]
    unnamed x2 -> x0, blocking collectives: 83.4 us -> none
    dot_general x7 -> x5, matrix products: 83.9 us -> 30.1 us  [outer(): lax.dot_general(left, right, (((0,), (0,)), ((), ())), preferred_element_...]
    all_to_all x0 -> x2, blocking collectives: none -> 45.6 us  [swap(): return lax.all_to_all(value, axis, 0, 0, tiled=True)]
    dot_general x24 -> x6, matrix products: 81 us -> 37.2 us  [matmul(): return jnp.dot(left, right, preferred_element_type=F32)]
  transfers between devices with their start and end apart: 14 -> 21, of which waited for: 11 -> 16; matrix products, arithmetic and copies ran while one was open for 7% -> 18% of each run, Pallas kernels for 0% -> 3%
where the time goes in v1:
time: 899 us; the launch traced here: 892 us
  waiting for transfers between devices  583 us (65%)
  matrix products  100 us (11%)
  local copies, waits for them, and re-layouts  60.7 us (7%)
  blocking collectives  45.6 us (5%)
  other arithmetic  32.6 us (4%)
  starting transfers between devices  30.9 us (3%)
  Pallas kernels  24.7 us (3%)
  between operations  14.8 us (2%)
    all_gather x8, waiting for transfers between devices, gather(): return lax.all_gather(value, axis, axis=0, tiled=True)  296 us
    reduce_scatter x7, waiting for transfers between devices, scatter_sum(): return lax.psum_scatter(value, axis, scatter_dimension=0, tiled=True)  192 us
    all_to_all x6, waiting for transfers between devices, swap(): return lax.all_to_all(value, axis, 0, 0, tiled=True)  92.2 us
    all_to_all x2, blocking collectives, swap(): return lax.all_to_all(value, axis, 0, 0, tiled=True)  45.6 us
    dot_general x6, matrix products, matmul(): return jnp.dot(left, right, preferred_element_type=F32)  37.2 us
    dot_general x5, matrix products, against(): lax.dot_general(left, weight, (((1,), (1,)), ((), ())), preferred_element...  32.7 us
    dot_general x5, matrix products, outer(): lax.dot_general(left, right, (((0,), (0,)), ((), ())), preferred_element_...  30.1 us
    all_to_all x6, starting transfers between devices, swap(): return lax.all_to_all(value, axis, 0, 0, tiled=True)  29.2 us
  transfers between devices with their start and end apart: 21, of which 16 were waited for; matrix products, arithmetic and copies ran while one was open for 18% of the time, Pallas kernels for 3%

profile of v1, /device:TPU:0, one launch (start us, length us, event | category | flops | bytes accessed | tf_op | source)
XLA Modules:
  0.0 892.0 jit_solution(7768032459616312419)
XLA Ops:
  33.5 23.0 %all-to-all-done = bf16[8,48,1120]{2,1,0:T(8,128)(2,1)S(1)} async-done(((bf16[8,48,1120]{2,1,0:T(8,128)(2,1)}), bf16[8,48,1120]{2,1,0:T(8,128)(2,1)S(1)}, u32[]{:S(2)}, u32[]{:S(2)}) %all-to-all-start) | async-done | bytes 860192 | tf_op jit(solution)/shard_map/all_to_all | solution.py:173
  58.0 27.3 %all-gather.11.cloned.1.call-done = bf16[1024,1536]{1,0:T(8,128)(2,1)} async-done(((bf16[128,1536]{1,0:T(8,128)(2,1)}), bf16[1024,1536]{1,0:T(8,128)(2,1)}) %all-gather.11.cloned.1.call-update) | async-done | bytes 3145744 | tf_op jit(solution)/shard_map/all_gather | solution.py:165
  87.8 70.7 %all-gather.9.cloned.1.call-done = bf16[1536,2176]{1,0:T(8,128)(2,1)} async-done(((bf16[48,2176]{1,0:T(8,128)(2,1)}), bf16[1536,2176]{1,0:T(8,128)(2,1)}) %all-gather.9.cloned.1.call-update) | async-done | bytes 6684688 | tf_op jit(solution)/shard_map/all_gather | solution.py:165
  176.6 10.4 %attention_forward.1 = (bf16[128,1536]{1,0:T(8,128)(2,1)}, f32[12,128,1]{2,1,0:T(8,128)}) custom-call(bf16[128,1536]{1,0:T(8,128)(2,1)} %add_convert_fusion.2.q_ref, bf16[1024,256]{1,0:T(8,128)(2,1)} %fusion.12.k_ref, bf16[1024,256]{1,0:T(8,128)(2,1)} %get-tuple-element.39.v_ref, s32[128,1]{1,0:T(8,128)} %copy.68.lo_ref, s32[128,1]{1,0:T(8,128)} %iota_add_fusion.hi_ref), custom_call_target="tpu_custom_call" | custom-call | flops 805306368 | bytes 1835008 | tf_op jit(solution)/shard_map/attention_forward/pallas_call | solution.py:118
  187.0 36.7 %all-gather.13.cloned.1.call-done = bf16[1536,1536]{1,0:T(8,128)(2,1)} async-done(((bf16[48,1536]{1,0:T(8,128)(2,1)}), bf16[1536,1536]{1,0:T(8,128)(2,1)}) %all-gather.13.cloned.1.call-update) | async-done | bytes 4718608 | tf_op jit(solution)/shard_map/all_gather | solution.py:165
  235.1 27.5 %all_to_all.78 = bf16[8,48,1120]{2,1,0:T(8,128)(2,1)} all-to-all(bf16[8,48,1120]{2,1,0:T(8,128)(2,1)S(1)} %all_to_all.55), channel_id=1, replica_groups=mesh['seq'=4,'ctx'=8] {'ctx'}, dimensions={0} | all-to-all | bytes 1720320 | tf_op jit(solution)/shard_map/all_to_all | solution.py:173
  264.4 53.9 %all-gather.15.cloned.1.call-done = bf16[1024,1536]{1,0:T(8,128)(2,1)} async-done(((bf16[128,1536]{1,0:T(8,128)(2,1)}), bf16[1024,1536]{1,0:T(8,128)(2,1)}) %all-gather.15.cloned.1.call-update) | async-done | bytes 3145744 | tf_op jit(solution)/shard_map/all_gather | solution.py:165
  318.4 9.0 %fusion.46 = f32[1024,1120]{0,1:T(8,128)} fusion(bf16[1024,1536]{1,0:T(8,128)(2,1)} %all-gather.15.cloned.1.call-done, bf16[1536,1120]{1,0:T(8,128)(2,1)} %all-gather.17.cloned.1.call-done), kind=kOutput, calls=%fused_computation.118 | convolution fusion | flops 3523215360 | bytes 11173888 | tf_op jit(solution)/shard_map/dot_general | solution.py:53
  327.3 21.9 %all-gather.19.cloned.1.call-done = bf16[1536,1120]{1,0:T(8,128)(2,1)} async-done(((bf16[384,1120]{1,0:T(8,128)(2,1)}), bf16[1536,1120]{1,0:T(8,128)(2,1)}) %all-gather.19.cloned.1.call-update) | async-done | bytes 3440656 | tf_op jit(solution)/shard_map/all_gather | solution.py:165
  349.2 8.9 fusion.47
  358.1 22.9 %all-gather.21.cloned.1.call-done = bf16[1120,1536]{1,0:T(8,128)(2,1)} async-done(((bf16[280,1536]{1,0:T(8,128)(2,1)}), bf16[1120,1536]{1,0:T(8,128)(2,1)}) %all-gather.21.cloned.1.call-update) | async-done | bytes 3440656 | tf_op jit(solution)/shard_map/all_gather | solution.py:165
  381.0 62.7 %all-gather.23.cloned.1.call-done = bf16[1024,1536]{1,0:T(8,128)(2,1)} async-done(((bf16[128,1536]{1,0:T(8,128)(2,1)}), bf16[1024,1536]{1,0:T(8,128)(2,1)}) %all-gather.23.cloned.1.call-update) | async-done | bytes 3145744 | tf_op jit(solution)/shard_map/all_gather | solution.py:165
  443.7 12.5 %multiply_convert_fusion = (bf16[1024,1120]{0,1:T(8,128)(2,1)S(1)}, bf16[1024,1120]{0,1:T(8,128)(2,1)S(1)}, bf16[1024,1120]{0,1:T(8,128)(2,1)}) fusion(f32[1024,1120]{0,1:T(8,128)} %fusion.46, f32[1024,1120]{0,1:T(8,128)} %fusion.47, bf16[1024,1536]{1,0:T(8,128)(2,1)} %all-gather.23.cloned.1.call-done, bf16[1120,1536]{1,0:T(8,128)(2,1)} %all-gather.21.cloned.1.call-done), kind=kOutput, calls=%fused_computation.14 | convolution fusion | flops 3541565440 | bytes 22642688 | tf_op jit(solution)/shard_map/dot_general | solution.py:57
  466.6 8.6 convolution_convert_fusion.4
  475.7 8.2 convolution_convert_fusion.1
  489.6 8.1 convolution_convert_fusion
  511.6 28.2 %reduce-scatter.14.cloned.1.call-done = bf16[128,1536]{1,0:T(8,128)(2,1)} async-done(((bf16[1024,1536]{1,0:T(8,128)(2,1)}), bf16[128,1536]{1,0:T(8,128)(2,1)}) %reduce-scatter.14.cloned.1.call-update) | async-done | bytes 393232 | tf_op jit(solution)/shard_map/reduce_scatter | solution.py:169
  541.1 76.1 %reduce-scatter.12.cloned.1.call-done = bf16[128,1536]{1,0:T(8,128)(2,1)} async-done(((bf16[1024,1536]{1,0:T(8,128)(2,1)}), bf16[128,1536]{1,0:T(8,128)(2,1)}) %reduce-scatter.12.cloned.1.call-update) | async-done | bytes 393232 | tf_op jit(solution)/shard_map/reduce_scatter | solution.py:169
  624.2 14.3 %attention_backward.1 = (f32[128,1536]{1,0:T(8,128)}, bf16[1024,256]{1,0:T(8,128)(2,1)}, bf16[1024,256]{1,0:T(8,128)(2,1)}) custom-call(bf16[128,1536]{1,0:T(8,128)(2,1)} %add_convert_fusion.2.q_ref, bf16[1024,256]{1,0:T(8,128)(2,1)} %fusion.12.k_ref, bf16[1024,256]{1,0:T(8,128)(2,1)} %get-tuple-element.39.v_ref, ...), custom_call_target="tpu_custom_call" | custom-call | flops 2013265920 | bytes 3670016 | tf_op jit(solution)/shard_map/attention_backward/pallas_call | solution.py:143
  651.0 19.6 %all-to-all-done.2 = bf16[8,128,512]{2,1,0:T(8,128)(2,1)} async-done(((bf16[8,128,512]{2,1,0:T(8,128)(2,1)}), bf16[8,128,512]{2,1,0:T(8,128)(2,1)}, u32[]{:S(2)}, u32[]{:S(2)}) %all-to-all-start.2) | async-done | bytes 1048608 | tf_op jit(solution)/shard_map/all_to_all | solution.py:173
  672.9 18.1 %all_to_all.79 = bf16[8,128,256]{2,1,0:T(8,128)(2,1)S(1)} all-to-all(bf16[8,128,256]{2,1,0:T(8,128)(2,1)S(1)} %bitcast.108), channel_id=1, replica_groups=mesh['seq'=4,'ctx'=8] {'ctx'}, dimensions={0} | all-to-all | bytes 1048576 | tf_op jit(solution)/shard_map/all_to_all | solution.py:173
  719.1 22.8 %all-to-all-done.6 = bf16[8,48,1120]{2,1,0:T(8,128)(2,1)} async-done(((bf16[8,48,1120]{2,1,0:T(8,128)(2,1)}), bf16[8,48,1120]{2,1,0:T(8,128)(2,1)}, u32[]{:S(2)}, u32[]{:S(2)}) %all-to-all-start.6) | async-done | bytes 860192 | tf_op jit(solution)/shard_map/all_to_all | solution.py:173
  748.7 19.6 %all-to-all-done.7 = bf16[8,48,1120]{2,1,0:T(8,128)(2,1)} async-done(((bf16[8,48,1120]{2,1,0:T(8,128)(2,1)}), bf16[8,48,1120]{2,1,0:T(8,128)(2,1)}, u32[]{:S(2)}, u32[]{:S(2)}) %all-to-all-start.7) | async-done | bytes 860192 | tf_op jit(solution)/shard_map/all_to_all | solution.py:173
  799.3 84.3 %reduce-scatter.18.cloned.1.call-done = bf16[48,1536]{1,0:T(8,128)(2,1)} async-done(((bf16[1536,1536]{1,0:T(8,128)(2,1)}), bf16[48,1536]{1,0:T(8,128)(2,1)}) %reduce-scatter.18.cloned.1.call-update) | async-done | bytes 147472 | tf_op jit(solution)/shard_map/reduce_scatter | solution.py:169
  (202 shorter events, 182.3 us)
Async XLA Ops:
  7.2 78.0 %all-gather.11.cloned.1.call-start = ((), (), s32[]{:S(2)}) async-start(), calls=%async_computation.16 | async-start | bytes 3538944 | tf_op jit(solution)/shard_map/all_gather | solution.py:165
  7.9 150.6 %all-gather.9.cloned.1.call-start = ((), (), s32[]{:S(2)}) async-start(), calls=%async_computation.15 | async-start | bytes 6893568 | tf_op jit(solution)/shard_map/all_gather | solution.py:165
  11.1 212.6 %all-gather.13.cloned.1.call-start = ((), (), s32[]{:S(2)}) async-start(), calls=%async_computation.17 | async-start | bytes 4866048 | tf_op jit(solution)/shard_map/all_gather | solution.py:165
  17.5 39.0 %all-to-all-start = ((bf16[8,48,1120]{2,1,0:T(8,128)(2,1)}), bf16[8,48,1120]{2,1,0:T(8,128)(2,1)S(1)}, u32[]{:S(2)}, u32[]{:S(2)}) async-start(bf16[8,48,1120]{2,1,0:T(8,128)(2,1)} %all_to_all.52), calls=%async_computation | async-start | bytes 1769472 | tf_op jit(solution)/shard_map/all_to_all | solution.py:173
  24.8 239.6 %all-gather.17.cloned.1.call-start = ((), (), s32[]{:S(2)}) async-start(), calls=%async_computation.19 | async-start | bytes 4423680 | tf_op jit(solution)/shard_map/all_gather | solution.py:165
  33.5 127.6 %copy-start.21 = (f32[128]{0:T(128)}, f32[128]{0:T(128)S(1)}, u32[]{:S(2)}) copy-start(f32[128]{0:T(128)S(1)} %get-tuple-element.61) | copy-start | bytes 1540
  57.4 260.9 %all-gather.15.cloned.1.call-start = ((), (), s32[]{:S(2)}) async-start(), calls=%async_computation.18 | async-start | bytes 3538944 | tf_op jit(solution)/shard_map/all_gather | solution.py:165
  87.8 78.2 %copy-start.18 = (f32[1024]{0:T(1024)}, f32[1024]{0:T(1024)S(1)}, u32[]{:S(2)}) copy-start(f32[1024]{0:T(1024)S(1)} %add_rsqrt_fusion) | copy-start | bytes 12292
  227.9 121.3 %all-gather.19.cloned.1.call-start = ((), (), s32[]{:S(2)}) async-start(), calls=%async_computation.20 | async-start | bytes 4423680 | tf_op jit(solution)/shard_map/all_gather | solution.py:165
  262.7 118.3 %all-gather.21.cloned.1.call-start = ((), (), s32[]{:S(2)}) async-start(), calls=%async_computation.21 | async-start | bytes 4300800 | tf_op jit(solution)/shard_map/all_gather | solution.py:165
  263.4 180.2 %all-gather.23.cloned.1.call-start = ((), (), s32[]{:S(2)}) async-start(), calls=%async_computation.23 | async-start | bytes 3538944 | tf_op jit(solution)/shard_map/all_gather | solution.py:165
  264.2 275.6 %reduce-scatter.14.cloned.1.call-start = ((), (), s32[]{:S(2)}) async-start(), calls=%async_computation.24 | async-start | bytes 3538944 | tf_op jit(solution)/shard_map/reduce_scatter | solution.py:169
  466.5 150.6 %reduce-scatter.12.cloned.1.call-start = ((), (), s32[]{:S(2)}) async-start(), calls=%async_computation.22 | async-start | bytes 3538944 | tf_op jit(solution)/shard_map/reduce_scatter | solution.py:169
  475.2 232.4 %reduce-scatter.22.cloned.1.call-start = ((), (), s32[]{:S(2)}) async-start(), calls=%async_computation.28 | async-start | bytes 4423680 | tf_op jit(solution)/shard_map/reduce_scatter | solution.py:169
  489.6 229.5 %reduce-scatter.24.cloned.1.call-start = ((), (), s32[]{:S(2)}) async-start(), calls=%async_computation.29 | async-start | bytes 4423680 | tf_op jit(solution)/shard_map/reduce_scatter | solution.py:169
  503.5 242.6 %reduce-scatter.20.cloned.1.call-start = ((), (), s32[]{:S(2)}) async-start(), calls=%async_computation.27 | async-start | bytes 4300800 | tf_op jit(solution)/shard_map/reduce_scatter | solution.py:169
  511.6 105.5 %copy-start.10 = (bf16[128,1536]{1,0:T(8,128)(2,1)S(1)}, bf16[128,1536]{1,0:T(8,128)(2,1)}, u32[]{:S(2)}) copy-start(bf16[128,1536]{1,0:T(8,128)(2,1)} %param.29) | copy-start | bytes 1179652
  640.8 29.8 %all-to-all-start.2 = ((bf16[8,128,512]{2,1,0:T(8,128)(2,1)}), bf16[8,128,512]{2,1,0:T(8,128)(2,1)}, u32[]{:S(2)}, u32[]{:S(2)}) async-start(bf16[8,128,512]{2,1,0:T(8,128)(2,1)} %bitcast.99), calls=%async_computation.4 | async-start | bytes 2097152 | tf_op jit(solution)/shard_map/all_to_all | solution.py:173
  645.0 126.2 %reduce-scatter.16.cloned.1.call-start = ((), (), s32[]{:S(2)}) async-start(), calls=%async_computation.25 | async-start | bytes 983040 | tf_op jit(solution)/shard_map/reduce_scatter | solution.py:169
  693.4 190.3 %reduce-scatter.18.cloned.1.call-start = ((), (), s32[]{:S(2)}) async-start(), calls=%async_computation.26 | async-start | bytes 4866048 | tf_op jit(solution)/shard_map/reduce_scatter | solution.py:169
  703.8 11.0 %all-to-all-start.5 = ((f32[32,1,408]{2,1,0:T(1,128)}), f32[32,1,408]{2,1,0:T(1,128)S(1)}, u32[]{:S(2)}, u32[]{:S(2)}) async-start(f32[32,1,408]{2,1,0:T(1,128)} %all_to_all.64), calls=%async_computation.8 | async-start | bytes 131072 | tf_op jit(solution)/shard_map/all_to_all | solution.py:173
  714.9 27.0 %all-to-all-start.6 = ((bf16[8,48,1120]{2,1,0:T(8,128)(2,1)}), bf16[8,48,1120]{2,1,0:T(8,128)(2,1)}, u32[]{:S(2)}, u32[]{:S(2)}) async-start(bf16[8,48,1120]{2,1,0:T(8,128)(2,1)} %bitcast.112), calls=%async_computation.10 | async-start | bytes 1769472 | tf_op jit(solution)/shard_map/all_to_all | solution.py:173
  741.9 26.4 %all-to-all-start.7 = ((bf16[8,48,1120]{2,1,0:T(8,128)(2,1)}), bf16[8,48,1120]{2,1,0:T(8,128)(2,1)}, u32[]{:S(2)}, u32[]{:S(2)}) async-start(bf16[8,48,1120]{2,1,0:T(8,128)(2,1)} %bitcast.111), calls=%async_computation.11 | async-start | bytes 1769472 | tf_op jit(solution)/shard_map/all_to_all | solution.py:173
  771.3 26.6 %all-to-all-start.4 = ((bf16[8,48,256]{2,1,0:T(8,128)(2,1)}), bf16[8,48,256]{2,1,0:T(8,128)(2,1)S(1)}, u32[]{:S(2)}, u32[]{:S(2)}) async-start(bf16[8,48,256]{2,1,0:T(8,128)(2,1)} %bitcast.116), calls=%async_computation.7 | async-start | bytes 393216 | tf_op jit(solution)/shard_map/all_to_all | solution.py:173
  (25 other events, 290.7 us)
Sparse Core Ops, SparseCore 0:
  10.2 74.9 all-gather.10
  88.7 69.7 all-gather.8
  161.4 62.2 all-gather.12
  225.7 29.5 all-gather.16
  257.9 60.4 all-gather.14
  319.8 29.3 all-gather.18
  350.7 30.1 all-gather.20
  383.2 60.4 all-gather.22
  466.7 73.0 reduce-scatter.13
  543.2 73.8 reduce-scatter.11
  619.7 39.6 reduce-scatter.21
  662.0 40.4 reduce-scatter.23
  705.0 39.8 reduce-scatter.19
  748.0 23.2 reduce-scatter.15
  776.6 106.9 reduce-scatter.17

commit v2 on v1

v2 whole, which is shorter than its diff:
```python
import functools
import math

import jax
import jax.numpy as jnp
from jax import lax
from jax.experimental import pallas as pl
from jax.experimental.pallas import tpu as pltpu
from jax.sharding import Mesh
from jax.sharding import PartitionSpec as P

HEADS = 12
KV_HEADS = 2
HEAD_DIM = 128
WIDTH = 1536
KV_WIDTH = 256
GROUP = HEADS // KV_HEADS
QKV = WIDTH + 2 * KV_WIDTH
LANES = 128

EPS = 1e-06
THETA = 1000000.0
NEGATIVE = -1e30
FACTOR = HEAD_DIM ** (-0.5)
VMEM_LIMIT = 58 * 1024 * 1024

CTX = ("z", "y")
ALL = ("seq", "z", "y")
BF = jnp.bfloat16
F32 = jnp.float32
LEFT = 1024
VMEM = pl.BlockSpec(memory_space=pltpu.VMEM)
SMEM = pl.BlockSpec(memory_space=pltpu.SMEM)


def shape(dims, kind):
    return jax.ShapeDtypeStruct(dims, kind)


def cost(flops, nbytes, exps=0):
    return pl.CostEstimate(flops=int(flops), bytes_accessed=int(nbytes), transcendentals=int(exps))


def whole(value):
    return pl.BlockSpec(value.shape, lambda i: (0,) * value.ndim)


def params():
    return pltpu.CompilerParams(vmem_limit_bytes=VMEM_LIMIT)


def inverse_rms(values):
    return lax.rsqrt(jnp.mean(values * values, axis=-1, keepdims=True) + EPS)


def matmul(left, right):
    return jnp.dot(left, right, preferred_element_type=F32)


def against(left, weight):
    return lax.dot_general(left, weight, (((1,), (1,)), ((), ())), preferred_element_type=F32)


def outer(left, right):
    return lax.dot_general(left, right, (((0,), (0,)), ((), ())), preferred_element_type=F32)


def rope_tables(positions):
    half = HEAD_DIM // 2
    freqs = THETA ** (-(2.0 * jnp.arange(half, dtype=F32)) / HEAD_DIM)
    angles = positions.astype(F32)[:, None] * freqs[None, :]
    cosine, sine = jnp.cos(angles), jnp.sin(angles)
    return jnp.concatenate([cosine, cosine], axis=-1), jnp.concatenate([-sine, sine], axis=-1)


def rotate(head, cosine, sine):
    return head * cosine + pltpu.roll(head, HEAD_DIM // 2, 1) * sine


def rotate_back(head, cosine, sine):
    return head * cosine - pltpu.roll(head, HEAD_DIM // 2, 1) * sine


def columns_out_kernel(gate_ref, up_ref, out_ref, *, seq, ctx, run, padded):
    chunk = seq * padded
    rows = gate_ref.shape[0]
    blank = jnp.zeros((rows, padded - run), BF)
    for which, ref in enumerate((gate_ref, up_ref)):
        for part in range(ctx):
            pieces = []
            for place in range(seq):
                start = (place * ctx + part) * run
                pieces += [ref[:, start:start + run], blank]
            out_ref[part, :, which * chunk:(which + 1) * chunk] = jnp.concatenate(pieces, axis=1)


def columns_out(gate, up, seq, ctx, run, padded):
    rows = gate.shape[0]
    return pl.pallas_call(
        functools.partial(columns_out_kernel, seq=seq, ctx=ctx, run=run, padded=padded),
        in_specs=[VMEM, VMEM],
        out_specs=VMEM,
        out_shape=shape((ctx, rows, 2 * seq * padded), BF),
        compiler_params=params(),
        cost_estimate=cost(0, 4 * gate.size * 2),
        name="columns_out",
    )(gate, up)


def columns_in_kernel(gate_in_ref, up_in_ref, gate_ref, up_ref, *, seq, ctx, run, padded):
    for in_ref, ref in ((gate_in_ref, gate_ref), (up_in_ref, up_ref)):
        pieces = []
        for place in range(seq):
            for part in range(ctx):
                pieces.append(in_ref[part, :, place * padded:place * padded + run])
        ref[...] = jnp.concatenate(pieces, axis=1).astype(F32)


def columns_in(gate, up, seq, ctx, run, padded):
    rows = gate.shape[1]
    return pl.pallas_call(
        functools.partial(columns_in_kernel, seq=seq, ctx=ctx, run=run, padded=padded),
        in_specs=[VMEM, VMEM],
        out_specs=[VMEM, VMEM],
        out_shape=[shape((rows, seq * ctx * run), F32)] * 2,
        compiler_params=params(),
        cost_estimate=cost(0, gate.size * 12),
        name="columns_in",
    )(gate, up)


def runs_of(core, own_ref, other_ref):
    run = own_ref.shape[0] // 2
    for x in range(2):
        for flip, ref in enumerate((own_ref, other_ref)):
            start = pl.multiple_of((2 * x + (core ^ flip)) * run, LANES)
            yield pl.ds(start, run), ref, slice(x * run, (x + 1) * run)


def times(core, left_ref, own_ref, other_ref, width):
    total = None
    for lanes, ref, rows in runs_of(core, own_ref, other_ref):
        term = matmul(left_ref[:, lanes], ref[rows, :width])
        total = term if total is None else total + term
    return total


def project_kernel(
    core_ref, tokens_ref, left_ref, left_other_ref, right_ref, right_other_ref,
    gain_ref, qbias_ref, kbias_ref, vbias_ref, cos_ref, sin_ref,
    normed_ref, query_ref, pair_out_ref,
):
    core = core_ref[0]
    inputs = tokens_ref[...].astype(F32)
    normed_ref[...] = (inputs * inverse_rms(inputs) * gain_ref[...]).astype(BF)
    left = times(core, normed_ref, left_ref, left_other_ref, LEFT)
    right = times(core, normed_ref, right_ref, right_other_ref, QKV - LEFT)
    query = jnp.concatenate([left, right[:, :WIDTH - LEFT]], axis=1) + qbias_ref[...]
    pair = right[:, WIDTH - LEFT:]
    key = pair[:, :KV_WIDTH] + kbias_ref[...]
    cosine, sine = cos_ref[...], sin_ref[...]
    for h in range(HEADS):
        lanes = slice(h * HEAD_DIM, (h + 1) * HEAD_DIM)
        query_ref[:, lanes] = rotate(query[:, lanes], cosine, sine).astype(BF)
    for g in range(KV_HEADS):
        lanes = slice(g * HEAD_DIM, (g + 1) * HEAD_DIM)
        pair_out_ref[:, lanes] = rotate(key[:, lanes], cosine, sine).astype(BF)
    pair_out_ref[:, KV_WIDTH:] = (pair[:, KV_WIDTH:] + vbias_ref[...]).astype(BF)


def project(core, tokens, left, right, gain, qbias, kbias, vbias, cosine, sine):
    rows = tokens.shape[0]
    return pl.pallas_call(
        project_kernel,
        in_specs=[SMEM] + [VMEM] * 11,
        out_specs=[VMEM] * 3,
        out_shape=[shape((rows, WIDTH), BF), shape((rows, WIDTH), BF), shape((rows, 2 * KV_WIDTH), BF)],
        compiler_params=params(),
        cost_estimate=cost(2 * rows * WIDTH * QKV, 2 * WIDTH * QKV + 6 * rows * WIDTH),
        name="project",
    )(core, tokens, *left, *right, gain, qbias, kbias, vbias, cosine, sine)


def vectors_kernel(core_ref, own_ref, other_ref, out_ref):
    for lanes, ref, rows in runs_of(core_ref[0], own_ref, other_ref):
        out_ref[:, lanes] = ref[rows, :].astype(F32).T[:out_ref.shape[0]]


def vectors_of(core, right, count):
    depth, width = right[0].shape
    block = pl.BlockSpec((depth, LANES), lambda i: (0, width // LANES - 1))
    return pl.pallas_call(
        vectors_kernel,
        grid=(1,),
        in_specs=[SMEM, block, block],
        out_specs=pl.BlockSpec((count, 2 * depth), lambda i: (0, 0)),
        out_shape=shape((count, 2 * depth), F32),
        compiler_params=params(),
        cost_estimate=cost(0, 4 * depth * LANES),
        name="vectors",
    )(core, *right)


def allowed_of(lo_ref, hi_ref, rows, length):
    places = lax.broadcasted_iota(jnp.int32, (rows, length), 1)
    return (places >= lo_ref[...]) & (places <= hi_ref[...])


def forward_kernel(q_ref, k_ref, v_ref, lo_ref, hi_ref, mixed_ref, logsum_ref):
    scores = against(q_ref[...], k_ref[...]) * FACTOR
    allowed = allowed_of(lo_ref, hi_ref, *scores.shape)
    scores = jnp.where(allowed, scores, NEGATIVE)
    top = jnp.max(scores, axis=-1, keepdims=True)
    weights = jnp.exp(scores - top)
    total = jnp.sum(weights, axis=-1, keepdims=True)
    shares = (weights * (1.0 / total)).astype(BF)
    mixed_ref[...] = matmul(shares, v_ref[...]).astype(BF)
    logsum_ref[0] = top + jnp.log(total)


def attention_forward(queries, pair, lo, hi):
    rows, length = queries.shape[0], pair.shape[0]
    head = pl.BlockSpec((rows, HEAD_DIM), lambda h: (0, h))
    key = pl.BlockSpec((length, HEAD_DIM), lambda h: (0, h // GROUP))
    value = pl.BlockSpec((length, HEAD_DIM), lambda h: (0, KV_HEADS + h // GROUP))
    column = pl.BlockSpec((rows, 1), lambda h: (0, 0))
    stat = pl.BlockSpec((1, rows, 1), lambda h: (h, 0, 0))
    return pl.pallas_call(
        forward_kernel,
        grid=(HEADS,),
        in_specs=[head, key, value, column, column],
        out_specs=[head, stat],
        out_shape=[shape((rows, WIDTH), BF), shape((HEADS, rows, 1), F32)],
        compiler_params=params(),
        cost_estimate=cost(4 * rows * length * WIDTH, 4 * length * KV_WIDTH + 4 * rows * WIDTH, rows * length * HEADS),
        name="attention_forward",
    )(queries, pair, pair, lo, hi)


def backward_kernel(
    core_ref, q_ref, k_ref, v_ref, g_ref, lo_ref, hi_ref, logsum_ref, cos_ref, sin_ref, cosq_ref, sinq_ref,
    normed_ref, mixed_ref, branch_ref, dq_ref, dkv_ref, keep_ref, send_ref, dk_sum, dv_sum, turned_ref,
):
    head = pl.program_id(0)

    @pl.when(head == 0)
    def _():
        turned_ref[...] = normed_ref[...].astype(F32).T.astype(BF)

    group = head // GROUP
    member = lax.rem(head, GROUP)
    queries, keys, grads = q_ref[...], k_ref[...], g_ref[...]
    scores = against(queries, keys) * FACTOR
    allowed = allowed_of(lo_ref, hi_ref, *scores.shape)
    shares = jnp.where(allowed, jnp.exp(jnp.where(allowed, scores, NEGATIVE) - logsum_ref[0]), 0.0)
    grad_shares = against(grads, v_ref[...])
    delta = jnp.sum(shares * grad_shares, axis=-1, keepdims=True)
    grad_scores = (shares * (grad_shares - delta)).astype(BF)
    dq = matmul(grad_scores, keys) * FACTOR
    dq = rotate_back(dq, cosq_ref[...], sinq_ref[...]).astype(BF)
    dq_ref[...] = dq
    dk = outer(grad_scores, queries) * FACTOR
    dv = outer(shares.astype(BF), grads)

    @pl.when(member == 0)
    def _():
        dk_sum[...] = dk
        dv_sum[...] = dv

    @pl.when(member > 0)
    def _():
        dk_sum[...] += dk
        dv_sum[...] += dv

    @pl.when(member == GROUP - 1)
    def _():
        here = pl.multiple_of(group * HEAD_DIM, HEAD_DIM)
        there = pl.multiple_of(KV_WIDTH + group * HEAD_DIM, HEAD_DIM)
        dkv_ref[:, pl.ds(here, HEAD_DIM)] = rotate_back(dk_sum[...], cos_ref[...], sin_ref[...]).astype(BF)
        dkv_ref[:, pl.ds(there, HEAD_DIM)] = dv_sum[...].astype(BF)

    core = core_ref[0]
    columns = pl.ds(pl.multiple_of(head * HEAD_DIM, HEAD_DIM), HEAD_DIM)
    for lanes, ref, rows in runs_of(core, keep_ref, send_ref):
        ref[rows, columns] = matmul(turned_ref[lanes, :], dq).astype(BF)
    run = keep_ref.shape[0] // 2
    heads = run // HEAD_DIM
    place = head // heads
    row = pl.multiple_of(place // 2 * run + lax.rem(head, heads) * HEAD_DIM, HEAD_DIM)
    terms = outer(mixed_ref[...], branch_ref[...]).astype(BF)
    mine = lax.rem(place, 2) == core

    @pl.when(mine)
    def _():
        keep_ref[pl.ds(row, HEAD_DIM), WIDTH:] = terms

    @pl.when(jnp.logical_not(mine))
    def _():
        send_ref[pl.ds(row, HEAD_DIM), WIDTH:] = terms


def attention_backward(
    core, queries, pair, grads, lo, hi, logsum, cosine, sine, cosine_own, sine_own, normed, mixed, grad_branch
):
    rows, length = queries.shape[0], pair.shape[0]
    once = pl.Buffered(1)
    head = pl.BlockSpec((rows, HEAD_DIM), lambda h: (0, h))
    key = pl.BlockSpec((length, HEAD_DIM), lambda h: (0, h // GROUP))
    value = pl.BlockSpec((length, HEAD_DIM), lambda h: (0, KV_HEADS + h // GROUP))
    column = pl.BlockSpec((rows, 1), lambda h: (0, 0))
    stat = pl.BlockSpec((1, rows, 1), lambda h: (h, 0, 0))
    fixed = lambda x: pl.BlockSpec(x.shape, lambda h: (0, 0), pipeline_mode=once)
    terms = shape((WIDTH // 2, 2 * WIDTH), BF)
    return pl.pallas_call(
        backward_kernel,
        grid=(HEADS,),
        in_specs=[SMEM, head, key, value, head, column, column, stat]
        + [fixed(x) for x in (cosine, sine, cosine_own, sine_own, normed)]
        + [head, fixed(grad_branch)],
        out_specs=[head, pl.BlockSpec((length, 2 * KV_WIDTH), lambda h: (0, 0))]
        + [pl.BlockSpec(terms.shape, lambda h: (0, 0))] * 2,
        out_shape=[shape((rows, WIDTH), BF), shape((length, 2 * KV_WIDTH), BF), terms, terms],
        scratch_shapes=[
            pltpu.VMEM((length, HEAD_DIM), F32),
            pltpu.VMEM((length, HEAD_DIM), F32),
            pltpu.VMEM((WIDTH, rows), BF),
        ],
        compiler_params=params(),
        cost_estimate=cost(10 * rows * length * WIDTH, 16 * length * KV_WIDTH, rows * length * HEADS),
        name="attention_backward",
    )(core, queries, pair, pair, grads, lo, hi, logsum, cosine, sine, cosine_own, sine_own, normed, mixed, grad_branch)


def branch_kernel(core_ref, mixed_ref, *refs):
    weights, (tokens_ref, gain_ref, middle_ref, normed_ref) = refs[:4], refs[4:]
    width = weights[0].shape[1]
    parts = [times(core_ref[0], mixed_ref, weights[2 * i], weights[2 * i + 1], width) for i in range(2)]
    middle = tokens_ref[...].astype(F32) + jnp.concatenate(parts, axis=1)
    middle_ref[...] = middle
    normed_ref[...] = (middle * inverse_rms(middle) * gain_ref[...]).astype(BF)


def branch(core, mixed, out_weight, tokens, gain):
    rows = mixed.shape[0]
    return pl.pallas_call(
        branch_kernel,
        in_specs=[SMEM] + [VMEM] * 7,
        out_specs=[VMEM] * 2,
        out_shape=[shape((rows, WIDTH), F32), shape((rows, WIDTH), BF)],
        compiler_params=params(),
        cost_estimate=cost(2 * rows * WIDTH * WIDTH, 2 * WIDTH * WIDTH),
        name="branch",
    )(core, mixed, *out_weight, tokens, gain)


def mlp_kernel(
    near_ref, other_ref, cot_near_ref, cot_other_ref, gate_ref, up_ref, down_ref,
    hidden_ref, grad_gate_ref, grad_up_ref, back_ref, forth_ref,
):
    tokens = jnp.concatenate([near_ref[...], other_ref[...]], axis=0)
    cotangent = jnp.concatenate([cot_near_ref[...], cot_other_ref[...]], axis=0)
    gate = matmul(tokens, gate_ref[...])
    upper = matmul(tokens, up_ref[...])
    grad_hidden = against(cotangent, down_ref[...])
    logistic = 1.0 / (1.0 + jnp.exp(-gate))
    silu = gate * logistic
    hidden = (silu * upper).astype(BF)
    hidden_ref[...] = hidden
    grad_gate = (grad_hidden * upper * logistic * (1.0 + gate * (1.0 - logistic))).astype(BF)
    grad_upper = (grad_hidden * silu).astype(BF)
    grad_gate_ref[...] = grad_gate
    grad_up_ref[...] = grad_upper
    back_ref[...] = (against(grad_gate, gate_ref[...]) + against(grad_upper, up_ref[...])).astype(BF)
    forth_ref[...] = matmul(hidden, down_ref[...]).astype(BF)


def mlp(near, other, cot_near, cot_other, gate_up, down):
    rows = 2 * near.shape[0]
    chunk = down.shape[0]
    part = lambda n: pl.BlockSpec((WIDTH, chunk), lambda i: (0, n))
    made = [shape((rows, width), BF) for width in (chunk, chunk, chunk, WIDTH, WIDTH)]
    return pl.pallas_call(
        mlp_kernel,
        grid=(1,),
        in_specs=[whole(near)] * 4 + [part(0), part(1), whole(down)],
        out_specs=[whole(x) for x in made],
        out_shape=made,
        compiler_params=params(),
        cost_estimate=cost(12 * rows * WIDTH * chunk, 6 * WIDTH * chunk + 14 * rows * WIDTH, rows * chunk),
        name="mlp",
    )(near, other, cot_near, cot_other, gate_up, gate_up, down)


def outer_kernel(*refs, counts):
    blocks, position = [], 0
    for count in counts:
        blocks.append(jnp.concatenate([ref[...] for ref in refs[position:position + count]], axis=0))
        position += count
    for right, out_ref in zip(blocks[1:], refs[position:]):
        out_ref[...] = outer(blocks[0], right).astype(BF)


def outer_blocks(lefts, rights, name):
    depth = sum(x.shape[0] for x in lefts)
    width = lefts[0].shape[1]
    across = [blocks[0].shape[1] for blocks in rights]
    tile = 384 if width % 384 == 0 else width
    flat = [x for blocks in rights for x in blocks]
    return pl.pallas_call(
        functools.partial(outer_kernel, counts=(len(lefts), *map(len, rights))),
        grid=(width // tile,),
        in_specs=[pl.BlockSpec((x.shape[0], tile), lambda i: (0, i)) for x in lefts]
        + [pl.BlockSpec(x.shape, lambda i: (0, 0), pipeline_mode=pl.Buffered(1)) for x in flat],
        out_specs=[pl.BlockSpec((tile, n), lambda i: (i, 0)) for n in across],
        out_shape=[shape((width, n), BF) for n in across],
        compiler_params=params(),
        cost_estimate=cost(2 * depth * width * sum(across), 2 * (depth + width) * (width + sum(across))),
        name=name,
    )(*lefts, *flat)


def middle_kernel(
    core_ref, first_ref, middle_ref, cotangent_ref, gain_ref, *refs
):
    weights, second, (grad_ref, branch_ref, mixed_ref, norm_ref) = refs[:4], refs[4:-4], refs[-4:]
    total = jnp.concatenate(
        [jnp.sum(first_ref[...].astype(F32), axis=0), sum(ref[...].astype(F32) for ref in second)], axis=0
    )
    middle = middle_ref[...]
    scale = inverse_rms(middle)
    norm_ref[...] = jnp.sum(total * middle * scale, axis=0, keepdims=True)
    weighted = total * gain_ref[...]
    grad = (
        cotangent_ref[...].astype(F32)
        + scale * weighted
        - middle * (scale * scale * scale) * jnp.mean(weighted * middle, axis=-1, keepdims=True)
    )
    grad_ref[...] = grad
    low = grad.astype(BF)
    branch_ref[...] = low
    width = weights[0].shape[1]
    core = core_ref[0]
    for first, second in zip(runs_of(core, *weights[:2]), runs_of(core, *weights[2:])):
        lanes, ref, rows = first
        mixed_ref[:, lanes] = (
            against(low[:, :width], ref[rows, :]) + against(low[:, width:], second[1][rows, :])
        ).astype(BF)


def middle_back(core, terms, middle, cotangent, gain, out_weight):
    rows = middle.shape[0]
    return pl.pallas_call(
        middle_kernel,
        in_specs=[SMEM] + [VMEM] * (8 + len(terms[1])),
        out_specs=[VMEM] * 4,
        out_shape=[shape((rows, WIDTH), F32), shape((rows, WIDTH), BF), shape((rows, WIDTH), BF), shape((1, WIDTH), F32)],
        compiler_params=params(),
        cost_estimate=cost(2 * rows * WIDTH * WIDTH, 2 * WIDTH * WIDTH + 20 * rows * WIDTH),
        name="middle_back",
    )(core, terms[0], middle, cotangent, gain, *out_weight, *terms[1])


def tokens_kernel(
    core_ref, grads_ref, left_ref, left_other_ref, right_ref, right_other_ref, tokens_ref, gain_ref, middle_ref,
    out_ref, norm_ref, bias_ref, total_ref,
):
    grads = grads_ref[...]
    bias_ref[...] = jnp.sum(grads.astype(F32), axis=0, keepdims=True)
    core = core_ref[0]
    for first, second in zip(runs_of(core, left_ref, left_other_ref), runs_of(core, right_ref, right_other_ref)):
        lanes, ref, rows = first
        total_ref[:, lanes] = against(grads[:, :LEFT], ref[rows, :]) + against(
            grads[:, LEFT:], second[1][rows, :QKV - LEFT]
        )
    grad_normed = total_ref[...]
    inputs = tokens_ref[...].astype(F32)
    scale = inverse_rms(inputs)
    norm_ref[...] = jnp.sum(grad_normed * inputs * scale, axis=0, keepdims=True)
    weighted = grad_normed * gain_ref[...]
    out_ref[...] = (
        middle_ref[...]
        + scale * weighted
        - inputs * (scale * scale * scale) * jnp.mean(weighted * inputs, axis=-1, keepdims=True)
    )


def tokens_back(core, grads, left, right, tokens, gain, middle):
    rows = tokens.shape[0]
    return pl.pallas_call(
        tokens_kernel,
        in_specs=[SMEM] + [VMEM] * 8,
        out_specs=[VMEM] * 3,
        out_shape=[shape((rows, WIDTH), F32), shape((1, WIDTH), F32), shape((1, QKV), F32)],
        scratch_shapes=[pltpu.VMEM((rows, WIDTH), F32)],
        compiler_params=params(),
        cost_estimate=cost(2 * rows * WIDTH * QKV, 2 * WIDTH * QKV + 12 * rows * WIDTH),
        name="tokens_back",
    )(core, grads, *left, *right, tokens, gain, middle)


def gather(value, axis):
    return lax.all_gather(value, axis, axis=0, tiled=True)


def scatter_sum(value, axis):
    return lax.psum_scatter(value, axis, scatter_dimension=0, tiled=True)


def swap(value, axis):
    return lax.all_to_all(value, axis, 0, 0, tiled=True)


def hop(value, axis, size=2, flip=1):
    return lax.ppermute(value, axis, [(i, i ^ flip) for i in range(size)])


def after(value, *earlier):
    return lax.optimization_barrier((value, *earlier))[0]


def together(*values):
    return lax.optimization_barrier(values)


def gather_near(value, nz):
    copies = jnp.broadcast_to(value[None], (nz, *value.shape)).reshape(-1, value.shape[1])
    return swap(copies, "z").reshape(nz, *value.shape)


def add_low(left, right):
    return (left.astype(F32) + right.astype(F32)).astype(BF)


def exchange_near(blocks, nz, own_z):
    out = [lax.dynamic_index_in_dim(blocks, own_z, 0, keepdims=False)]
    for flip in range(1, nz):
        out.append(hop(lax.dynamic_index_in_dim(blocks, own_z ^ flip, 0, keepdims=False), "z", nz, flip))
    return out


def add_up(blocks):
    total = blocks[0].astype(F32)
    for block in blocks[1:]:
        total = total + block.astype(F32)
    return total


def pair(own, other, bit, axis):
    first, second = jnp.where(bit == 0, own, other), jnp.where(bit == 0, other, own)
    return jnp.stack([first, second], axis=axis)


def gather_z(value, nz, own_z):
    blocks = jnp.stack([value] + [hop(value, "z", nz, j) for j in range(1, nz)])
    return jnp.concatenate([lax.dynamic_slice_in_dim(blocks, own_z ^ j, 1) for j in range(nz)], axis=0)


def halve(value, axis, flip, size, bit, dim):
    keep = lax.dynamic_index_in_dim(value, bit, dim, keepdims=False)
    send = lax.dynamic_index_in_dim(value, 1 - bit, dim, keepdims=False)
    return add_low(keep, hop(send, axis, size, flip))


def sum_all(value, seq, nz):
    for axis, size in (("seq", seq), ("y", 2), ("z", nz)):
        flip = 1
        while flip < size:
            value = value + hop(value, axis, size, flip)
            flip *= 2
    return value


def body(
    tokens,
    segments,
    w_query,
    b_query,
    w_key,
    b_key,
    w_value,
    b_value,
    w_out,
    norm_attn,
    w_gate,
    w_up,
    w_down,
    norm_mlp,
    cotangent,
    *,
    seq,
    ctx,
):
    rows = tokens.shape[0]
    half = rows // 2
    nz = ctx // 2
    devices = seq * ctx
    share = w_query.shape[0]
    vshare = b_value.shape[0]
    run = w_down.shape[0]
    unit = LANES // math.gcd(LANES, seq)
    padded = -(-run // unit) * unit
    ident = segments[0]
    length = ident.shape[0]
    own_z, own_y, place = lax.axis_index("z"), lax.axis_index("y"), lax.axis_index("seq")
    index = 2 * own_z + own_y

    small = jnp.stack([norm_attn, norm_mlp, b_query, jnp.pad(b_value, (0, share - vshare))], axis=1)
    small = jnp.pad(small, ((0, 0), (0, LANES - 4)))
    projections = jnp.concatenate([w_query, w_key, w_value, small], axis=1)
    x, core = place // 2, place % 2
    over = lambda v, axis: hop(v, "seq", seq, 2) if axis == "x" else hop(v, "seq", seq, 1) if axis == "core" else hop(v, "y")
    flat = lambda v: v.reshape(2 * ctx * share, v.shape[-1])
    cuts = [slice(i * half, (i + 1) * half) for i in range(2)]
    count = nz * half
    cosine, sine = rope_tables(jnp.arange(length, dtype=jnp.int32) - ident)
    offset = index * rows
    hi = (offset + jnp.arange(rows, dtype=jnp.int32))[:, None]
    lo = lax.dynamic_slice_in_dim(ident, offset, rows)[:, None]
    tables = [cosine, sine] + [lax.dynamic_slice_in_dim(x, offset, rows) for x in (cosine, sine)] + [lo, hi]
    near = gather_near(projections, nz)
    turned = columns_out(w_gate, w_up, seq, ctx, run, padded).reshape(ctx * share, -1)
    turned = swap(after(turned, near), CTX)
    left, right = near[:, :, :LEFT], near[:, :, LEFT:]
    left_got, right_got, near, tables = together(
        over(left, "y"), over(right, "x"), gather_z(after(w_out, near), nz, own_z), tables
    )
    left, right = pair(left, left_got, own_y, 1), pair(right, right_got, x, 0)
    out_left, out_right = near[:, :, :WIDTH // 2], near[:, :, WIDTH // 2:]
    left_got, right_got, out_left_got, out_right_got = together(
        over(left, "x"), over(right, "y"), over(out_left, "y"), over(out_right, "x")
    )
    left, right = flat(pair(left, left_got, x, 0)), flat(pair(right, right_got, own_y, 2))
    out_left, out_right = pair(out_left, out_left_got, own_y, 1), pair(out_right, out_right_got, x, 0)
    left_got, right_got, out_left_got, out_right_got = together(
        over(left, "core"), over(right, "core"), over(out_left, "x"), over(out_right, "y")
    )
    left, right = (left, left_got), (right, right_got)
    out_left, out_right = flat(pair(out_left, out_left_got, x, 0)), flat(pair(out_right, out_right_got, own_y, 2))
    out_weight = (out_left, over(out_left, "core"), out_right, over(out_right, "core"))
    down = jnp.pad(w_down, ((0, padded - run), (0, 0)))
    down = gather(down, "seq")
    gate_up = gather(after(turned, left_got), "seq")
    cotangent_low = after(cotangent, turned)
    cot_near = [gather_near(cotangent_low[cuts[0]], nz).reshape(count, WIDTH)]
    cosine, sine, cosine_own, sine_own, lo, hi = tables
    core = core.astype(jnp.int32)[None]
    vectors = vectors_of(core, right, 8)
    attn_gain, mlp_gain, query_bias = vectors[0:1], vectors[1:2], vectors[2:3]
    value_bias = vectors[3].reshape(devices, share)[:, :vshare].reshape(1, KV_WIDTH)

    normed, queries, kv = project(
        core, tokens, left, right, attn_gain, query_bias, b_key.astype(F32)[None], value_bias, cosine_own, sine_own
    )
    near = gather_near(after(kv, cot_near[0]), nz)
    cot_near.append(gather_near(after(cotangent, near)[cuts[1]], nz).reshape(count, WIDTH))
    other = hop(near, "y")
    cot_other = [hop(after(x, other), "y") for x in cot_near]
    kv = pair(near, other, own_y, 1).reshape(length, 2 * KV_WIDTH)
    mixed, logsum = attention_forward(queries, kv, lo, hi)
    mixed, out_weight, cot_other[0] = together(mixed, out_weight, cot_other[0])
    middle, normed_mlp = branch(core, mixed, out_weight, tokens, mlp_gain)

    x_near = [gather_near(after(normed_mlp, cot_near[1])[cut], nz).reshape(count, WIDTH) for cut in cuts]
    x_other = [hop(x, "y") for x in x_near]
    runs = [mlp(x_near[0], x_other[0], cot_near[0], cot_other[0], gate_up, down)]
    x_other[1] = after(x_other[1], *runs[0])
    runs.append(mlp(x_near[1], x_other[1], cot_near[1], cot_other[1], gate_up, down))
    hidden, grads_gate, grads_up, back, forth = zip(*runs)
    sums = []
    for rows_back in back:
        sums.append(add_low(rows_back[:count], hop(after(rows_back[count:], *sums), "y")))
    far = [swap(sums[0], "z").reshape(nz, half, WIDTH), exchange_near(sums[1].reshape(nz, half, WIDTH), nz, own_z)]
    x_all = [x_near[0], x_other[0], x_near[1], x_other[1]]
    cots = [cot_near[0], cot_other[0], cot_near[1], cot_other[1]]
    forth_got = [hop(after(x[count:], *sums), "y") for x in forth]
    grads_gate, grads_up = after((grads_gate, grads_up), sums[1], far[0])
    hidden = after(hidden, forth_got[0])
    grad_w_gate, grad_w_up = outer_blocks(x_all, [grads_gate, grads_up], "gate_up_grads")
    grad_w_gate, grad_w_up = scatter_sum(grad_w_gate, "seq"), scatter_sum(grad_w_up, "seq")
    (grad_w_down,) = outer_blocks(hidden, [cots], "down_grads")
    grad_w_down = scatter_sum(grad_w_down, "seq")[:run].astype(F32)

    far, forth_got = together(far, forth_got)
    grad_middle, grad_branch, grad_mixed, norm_mlp_sum = middle_back(core, far, middle, cotangent, mlp_gain, out_weight)
    dq, dkv, keep, send = attention_backward(
        core, queries, kv, grad_mixed, lo, hi, logsum, cosine, sine, cosine_own, sine_own, normed, mixed, grad_branch
    )
    forth = jnp.concatenate(
        [add_low(x[:count], y).reshape(nz, half, WIDTH) for x, y in zip(forth, forth_got)], axis=1
    )
    forth = exchange_near(forth, nz, own_z)
    terms = swap(dkv, CTX).reshape(ctx, rows, 2 * KV_WIDTH)
    terms = jnp.sum(terms.astype(F32), axis=0).astype(BF)

    over_core = lambda v: halve(v, "seq", 1, seq, place % 2, 1)
    over_x = lambda v: halve(v, "seq", 2, seq, place // 2, 0)
    over_y = lambda v: halve(v, "y", 1, 2, own_y, v.ndim - 3)
    sides = add_low(keep, over(send, "core")).reshape(2, nz, 2, share, -1)
    grad_query, grad_out = over_x(sides[..., :WIDTH]), over_y(sides[..., WIDTH:])
    terms, sides_done = together(terms, sides[:1, :1, :1, :8, :LANES])
    grad_w_gate = swap(after(grad_w_gate, terms), CTX).reshape(ctx, share, -1)
    (grad_pair,) = outer_blocks([normed], [[terms]], "pair_grads")
    grad_tokens, norm_attn_sum, bias = tokens_back(
        core, jnp.concatenate([dq, after(terms, grad_pair)], axis=1), left, right, tokens, attn_gain, grad_middle
    )
    grad_pair, bias, forth, grad_out, grad_query = together(grad_pair, bias, forth, grad_out, grad_query)
    grad_pair = over_core(grad_pair.reshape(2, 2, nz, 2, share, -1))
    grad_out, grad_query = over_x(grad_out), over_y(grad_query)
    grad_w_gate, grad_out, grad_query, grad_pair = together(grad_w_gate, grad_out, grad_query, grad_pair)
    side = add_up(exchange_near(jnp.concatenate([grad_out, grad_query], axis=2), nz, own_z))
    grad_w_up = swap(after(grad_w_up, grad_w_gate), CTX).reshape(ctx, share, -1)
    grad_pair = add_up(exchange_near(over_y(over_x(grad_pair)), nz, own_z))
    grad_w_out, grad_w_query = side[:, :WIDTH], side[:, WIDTH:]
    grad_w_key, grad_w_value = grad_pair[:, :KV_WIDTH], grad_pair[:, KV_WIDTH:]
    output = middle + add_up(forth)
    grad_w_gate, grad_w_up = columns_in(grad_w_gate, grad_w_up, seq, ctx, run, padded)

    sums = sum_all(jnp.concatenate([norm_attn_sum, norm_mlp_sum, bias], axis=1), seq, nz)[0]
    number = place * ctx + index
    mine = lambda start, size: lax.dynamic_slice_in_dim(sums, start + number * size, size)
    g_norm_attn, g_norm_mlp, g_b_query = (mine(n * WIDTH, share) for n in range(3))
    g_b_key = sums[3 * WIDTH:3 * WIDTH + KV_WIDTH]
    g_b_value = mine(3 * WIDTH + KV_WIDTH, vshare)
    return (
        output,
        grad_tokens,
        grad_w_query,
        g_b_query,
        grad_w_key,
        g_b_key,
        grad_w_value,
        g_b_value,
        grad_w_out,
        g_norm_attn,
        grad_w_gate,
        grad_w_up,
        grad_w_down,
        g_norm_mlp,
    )


def solution(mesh):
    seq, ctx = mesh.shape["seq"], mesh.shape["ctx"]
    rows2, rows1 = P(ALL, None), P(ALL)
    return jax.shard_map(
        functools.partial(body, seq=seq, ctx=ctx),
        mesh=Mesh(mesh.devices.reshape(seq, ctx // 2, 2), ALL),
        in_specs=(
            rows2,
            P("seq", None),
            rows2,
            rows1,
            rows2,
            P(),
            rows2,
            rows1,
            rows2,
            rows1,
            rows2,
            rows2,
            rows2,
            rows1,
            rows2,
        ),
        out_specs=(
            rows2,
            rows2,
            rows2,
            rows1,
            rows2,
            P(),
            rows2,
            rows1,
            rows2,
            rows1,
            rows2,
            rows2,
            rows2,
            rows1,
        ),
        check_vma=False,
    )
```

time: 899 us -> 597 us (0.66)
  waiting for transfers between devices: 583 us -> 237 us
  Pallas kernels: 24.7 us -> 130 us
  matrix products: 100 us -> 0 us
  starting transfers between devices: 30.9 us -> 99.1 us
  blocking collectives: 45.6 us -> 20.2 us
  local copies, waits for them, and re-layouts: 60.7 us -> 42.7 us
  other arithmetic: 32.6 us -> 42.3 us
    all_gather x8 -> x2, waiting for transfers between devices: 296 us -> 0.01 us  [gather(): return lax.all_gather(value, axis, axis=0, tiled=True)]
    reduce_scatter x7 -> x3, waiting for transfers between devices: 192 us -> 0.02 us  [scatter_sum(): return lax.psum_scatter(value, axis, scatter_dimension=0, tiled=True)]
    ppermute x0 -> x49, waiting for transfers between devices: none -> 155 us  [hop(): return lax.ppermute(value, axis, [(i, i ^ flip) for i in range(size)])]
    pallas_call x2 -> x14, Pallas kernels: 24.7 us -> 130 us  [the longest x2 39.1 us: mlp(): pl.pallas_call(mlp_kernel, grid=(1,), in_specs=[whole(near)] * 4 + [part(...]
    dot_general x16 -> x0, matrix products: 100 us -> none  [the longest x6 37.2 us: matmul(): return jnp.dot(left, right, preferred_element_type=F32)]
    ppermute x0 -> x49, starting transfers between devices: none -> 51.4 us  [hop(): return lax.ppermute(value, axis, [(i, i ^ flip) for i in range(size)])]
    reshape x17 -> x1, local copies, waits for them, and re-layouts: 27.9 us -> 0.66 us  [body(): vectors[3].reshape(devices, share)[:, :vshare].reshape(1, KV_WIDTH)]
    all_to_all x2 -> x1, blocking collectives: 45.6 us -> 20.2 us  [swap(): return lax.all_to_all(value, axis, 0, 0, tiled=True)]
  transfers between devices with their start and end apart: 21 -> 64, of which waited for: 16 -> 31; matrix products, arithmetic and copies ran while one was open for 18% -> 12% of each run, Pallas kernels for 3% -> 19%
where the time goes in v2:
time: 597 us; the launch traced here: 586 us
  waiting for transfers between devices  237 us (40%)
  Pallas kernels  130 us (22%)
  starting transfers between devices  99.1 us (17%)
  local copies, waits for them, and re-layouts  42.7 us (7%)
  other arithmetic  42.3 us (7%)
  blocking collectives  20.2 us (3%)
  between operations  15.2 us (3%)
    ppermute x49, waiting for transfers between devices, hop(): return lax.ppermute(value, axis, [(i, i ^ flip) for i in range(size)])  155 us
    all_to_all x10, waiting for transfers between devices, swap(): return lax.all_to_all(value, axis, 0, 0, tiled=True)  81.7 us
    ppermute x49, starting transfers between devices, hop(): return lax.ppermute(value, axis, [(i, i ^ flip) for i in range(size)])  51.4 us
    all_to_all x10, starting transfers between devices, swap(): return lax.all_to_all(value, axis, 0, 0, tiled=True)  47.4 us
    pallas_call x2, Pallas kernels, mlp(): pl.pallas_call(mlp_kernel, grid=(1,), in_specs=[whole(near)] * 4 + [part(...  39.1 us
    pallas_call x3, Pallas kernels, outer_blocks(): pl.pallas_call(functools.partial(outer_kernel, counts=(len(lefts), *map(l...  24.5 us
    pallas_call x1, Pallas kernels, attention_backward(): pl.pallas_call(backward_kernel, grid=(HEADS,), in_specs=[SMEM, head, key,...  23.9 us
    all_to_all x1, blocking collectives, swap(): return lax.all_to_all(value, axis, 0, 0, tiled=True)  20.2 us
  transfers between devices with their start and end apart: 64, of which 31 were waited for; matrix products, arithmetic and copies ran while one was open for 12% of the time, Pallas kernels for 19%

profile of v2, /device:TPU:0, one launch (start us, length us, event | category | flops | bytes accessed | tf_op | source)
XLA Modules:
  0.0 585.8 jit_solution(6085572057995963019)
XLA Ops:
  10.6 6.3 %all-to-all-start = ((bf16[4,48,2176]{2,1,0:T(8,128)(2,1)}), bf16[4,48,2176]{2,1,0:T(8,128)(2,1)S(1)}, u32[]{:S(2)}, u32[]{:S(2)}) async-start(bf16[4,48,2176]{2,1,0:T(8,128)(2,1)} %broadcast_in_dim.21), calls=%async_computation | async-start | bytes 1671168 | tf_op jit(solution)/shard_map/all_to_all | solution.py:510
  21.3 17.2 %all-to-all-done = bf16[4,48,2176]{2,1,0:T(8,128)(2,1)S(1)} async-done(((bf16[4,48,2176]{2,1,0:T(8,128)(2,1)}), bf16[4,48,2176]{2,1,0:T(8,128)(2,1)S(1)}, u32[]{:S(2)}, u32[]{:S(2)}) %all-to-all-start) | async-done | bytes 835616 | tf_op jit(solution)/shard_map/all_to_all | solution.py:510
  53.2 6.9 %collective-permute-done.1 = bf16[4,48,1152]{2,1,0:T(8,128)(2,1)S(1)} collective-permute-done((bf16[4,48,1152]{2,1,0:T(8,128)(2,1)S(1)}, bf16[4,48,1152]{2,1,0:T(8,128)(2,1)S(1)}, u32[]{:S(2)}, u32[]{:S(2)}) %collective-permute-start.1) | collective-permute-done | bytes 442400 | tf_op jit(solution)/shard_map/ppermute | solution.py:514
  74.4 27.9 %collective-permute-done.7 = bf16[4,48,768]{2,1,0:T(8,128)(2,1)} collective-permute-done((bf16[4,48,768]{2,1,0:T(8,128)(2,1)}, bf16[4,48,768]{2,1,0:T(8,128)(2,1)}, u32[]{:S(2)}, u32[]{:S(2)}) %collective-permute-start.7) | collective-permute-done | bytes 294944 | tf_op jit(solution)/shard_map/ppermute | solution.py:514
  108.2 14.3 %collective-permute-done.11 = bf16[4,2,48,768]{3,2,0,1:T(8,128)(2,1)S(1)} collective-permute-done((bf16[4,2,48,768]{3,2,0,1:T(8,128)(2,1)S(1)}, bf16[4,2,48,768]{3,2,0,1:T(8,128)(2,1)S(1)}, u32[]{:S(2)}, u32[]{:S(2)}) %collective-permute-start.11) | collective-permute-done | bytes 589856 | tf_op jit(solution)/shard_map/ppermute | solution.py:514
  141.4 8.5 %all-to-all-done.2 = bf16[4,64,1536]{2,1,0:T(8,128)(2,1)S(1)} async-done(((bf16[4,64,1536]{2,1,0:T(8,128)(2,1)}), bf16[4,64,1536]{2,1,0:T(8,128)(2,1)S(1)}, u32[]{:S(2)}, u32[]{:S(2)}) %all-to-all-start.2) | async-done | bytes 786464 | tf_op jit(solution)/shard_map/all_to_all | solution.py:510
  157.9 12.0 %all-to-all-done.3 = bf16[4,128,512]{2,1,0:T(8,128)(2,1)} async-done(((bf16[4,128,512]{2,1,0:T(8,128)(2,1)}), bf16[4,128,512]{2,1,0:T(8,128)(2,1)}, u32[]{:S(2)}, u32[]{:S(2)}) %all-to-all-start.3) | async-done | bytes 524320 | tf_op jit(solution)/shard_map/all_to_all | solution.py:510
  176.7 6.4 %collective-permute-done.13 = bf16[4,128,512]{2,1,0:T(8,128)(2,1)} collective-permute-done((bf16[4,128,512]{2,1,0:T(8,128)(2,1)}, bf16[4,128,512]{2,1,0:T(8,128)(2,1)}, u32[]{:S(2)}, u32[]{:S(2)}) %collective-permute-start.13) | collective-permute-done | bytes 524320 | tf_op jit(solution)/shard_map/ppermute | solution.py:514
  186.8 10.4 %attention_forward.1 = (bf16[128,1536]{1,0:T(8,128)(2,1)}, f32[12,128,1]{2,1,0:T(8,128)}) custom-call(bf16[128,1536]{1,0:T(8,128)(2,1)} %get-tuple-element.122.q_ref, bf16[1024,512]{1,0:T(8,128)(2,1)} %bitcast.182, bf16[1024,512]{1,0:T(8,128)(2,1)} %bitcast.183, s32[128,1]{1,0:T(8,128)} %copy.45.lo_ref, s32[128,1]{1,0:T(8,128)} %iota_add_fusion.hi_ref), custom_call_target="tpu_custom_call" | custom-call | flops 805306368 | bytes 1835008 | tf_op jit(solution)/shard_map/attention_forward/pallas_call | solution.py:228
  206.7 20.2 %all_to_all.92 = bf16[4,64,1536]{2,1,0:T(8,128)(2,1)S(1)} all-to-all(bf16[4,64,1536]{2,1,0:T(8,128)(2,1)S(1)} %broadcast_in_dim.28), channel_id=1, replica_groups=mesh['seq'=4,'z'=4,'y'=2] {'z'}, dimensions={0} | all-to-all | bytes 1572864 | tf_op jit(solution)/shard_map/all_to_all | solution.py:510
  234.1 15.9 %all-to-all-done.7 = bf16[4,64,1536]{2,1,0:T(8,128)(2,1)S(1)} async-done(((bf16[4,64,1536]{2,1,0:T(8,128)(2,1)}), bf16[4,64,1536]{2,1,0:T(8,128)(2,1)S(1)}, u32[]{:S(2)}, u32[]{:S(2)}) %all-to-all-start.7) | async-done | bytes 786464 | tf_op jit(solution)/shard_map/all_to_all | solution.py:510
  253.4 19.5 %mlp.2 = (bf16[512,1152]{1,0:T(8,128)(2,1)}, bf16[512,1152]{1,0:T(8,128)(2,1)}, bf16[512,1152]{1,0:T(8,128)(2,1)}, bf16[512,1536]{1,0:T(8,128)(2,1)}, bf16[512,1536]{1,0:T(8,128)(2,1)}) custom-call(bf16[256,1536]{1,0:T(8,128)(2,1)} %bitcast.192, bf16[256,1536]{1,0:T(8,128)(2,1)} %copy-done.56, bf16[256,1536]{1,0:T(8,128)(2,1)} %bitcast.189, ...), custom_call_target="tpu_custom_call" | custom-call | flops 10871635968 | bytes 21626880 | tf_op jit(solution)/shard_map/mlp/pallas_call | solution.py:382
  274.7 11.6 %collective-permute-done.19.other_ref.refs_3_ = bf16[256,1536]{1,0:T(8,128)(2,1)} collective-permute-done((bf16[256,1536]{1,0:T(8,128)(2,1)S(1)}, bf16[256,1536]{1,0:T(8,128)(2,1)}, u32[]{:S(2)}, u32[]{:S(2)}) %collective-permute-start.19) | collective-permute-done | bytes 786464 | tf_op jit(solution)/shard_map/ppermute | solution.py:514
  287.2 19.7 %mlp.3 = (bf16[512,1152]{1,0:T(8,128)(2,1)}, bf16[512,1152]{1,0:T(8,128)(2,1)}, bf16[512,1152]{1,0:T(8,128)(2,1)}, bf16[512,1536]{1,0:T(8,128)(2,1)}, bf16[512,1536]{1,0:T(8,128)(2,1)}) custom-call(bf16[256,1536]{1,0:T(8,128)(2,1)} %bitcast.195, bf16[256,1536]{1,0:T(8,128)(2,1)} %collective-permute-done.19.other_ref.refs_3_, ...), custom_call_target="tpu_custom_call" | custom-call | flops 10871635968 | bytes 21626880 | tf_op jit(solution)/shard_map/mlp/pallas_call | solution.py:382
  315.2 7.8 %collective-permute-done.21 = bf16[256,1536]{1,0:T(8,128)(2,1)} collective-permute-done((bf16[256,1536]{1,0:T(8,128)(2,1)S(1)}, bf16[256,1536]{1,0:T(8,128)(2,1)}, u32[]{:S(2)}, u32[]{:S(2)}) %collective-permute-start.21) | collective-permute-done | bytes 786464 | tf_op jit(solution)/shard_map/ppermute | solution.py:514
  328.5 13.0 %gate_up_grads.1 = (bf16[1536,1152]{1,0:T(8,128)(2,1)}, bf16[1536,1152]{1,0:T(8,128)(2,1)}) custom-call(bf16[256,1536]{1,0:T(8,128)(2,1)} %bitcast.193, bf16[256,1536]{1,0:T(8,128)(2,1)} %copy-done.56, bf16[256,1536]{1,0:T(8,128)(2,1)} %bitcast.196, bf16[256,1536]{1,0:T(8,128)(2,1)} %collective-permute-done.19.other_ref.refs_3_, ...), custom_call_target="tpu_custom_call" | custom-call | flops 7247757312 | bytes 19660800 | tf_op jit(solution)/shard_map/gate_up_grads/pallas_call | solution.py:409
  344.5 10.5 %collective-permute-done.25 = bf16[256,1536]{1,0:T(8,128)(2,1)S(1)} collective-permute-done((bf16[256,1536]{1,0:T(8,128)(2,1)S(1)}, bf16[256,1536]{1,0:T(8,128)(2,1)S(1)}, u32[]{:S(2)}, u32[]{:S(2)}) %collective-permute-start.25) | collective-permute-done | bytes 786464 | tf_op jit(solution)/shard_map/ppermute | solution.py:514
  355.1 7.5 %down_grads.1 = bf16[1152,1536]{1,0:T(8,128)(2,1)} custom-call(bf16[512,1152]{1,0:T(8,128)(2,1)} %get-tuple-element.204.refs_0_, bf16[512,1152]{1,0:T(8,128)(2,1)} %get-tuple-element.205.refs_1_, bf16[256,1536]{1,0:T(8,128)(2,1)} %bitcast.190, bf16[256,1536]{1,0:T(8,128)(2,1)} %collective-permute-done.16.cot_other_ref.refs_3_, ...), custom_call_target="tpu_custom_call" | custom-call | flops 3623878656 | bytes 11698176 | tf_op jit(solution)/shard_map/down_grads/pallas_call | solution.py:409
  384.2 23.9 %attention_backward.1 = (bf16[128,1536]{1,0:T(8,128)(2,1)}, bf16[1024,512]{1,0:T(8,128)(2,1)}, bf16[768,3072]{1,0:T(8,128)(2,1)}, bf16[768,3072]{1,0:T(8,128)(2,1)}) custom-call(s32[1]{0:T(128)} %bitcast.core_ref, bf16[128,1536]{1,0:T(8,128)(2,1)} %get-tuple-element.122.q_ref, bf16[1024,512]{1,0:T(8,128)(2,1)} %bitcast.184, bf16[1024,512]{1,0:T(8,128)(2,1)} %bitcast.185, ...), custom_call_target="tpu_custom_call" | custom-call | flops 2013265920 | bytes 4194304 | tf_op jit(solution)/shard_map/attention_backward/pallas_call | solution.py:314
  430.1 9.7 %all-to-all-done.8 = bf16[8,128,512]{2,1,0:T(8,128)(2,1)} async-done(((bf16[8,128,512]{2,1,0:T(8,128)(2,1)}), bf16[8,128,512]{2,1,0:T(8,128)(2,1)}, u32[]{:S(2)}, u32[]{:S(2)}) %all-to-all-start.8) | async-done | bytes 1048608 | tf_op jit(solution)/shard_map/all_to_all | solution.py:510
  448.3 6.6 %tokens_back.1 = (f32[128,1536]{1,0:T(8,128)}, f32[1,1536]{1,0:T(1,128)}, f32[1,2048]{1,0:T(1,128)}) custom-call(s32[1]{0:T(128)} %bitcast.core_ref, bf16[128,2048]{1,0:T(8,128)(2,1)} %pad_maximum_fusion.11.grads_ref, bf16[768,1024]{1,0:T(8,128)(2,1)} %bitcast.171, bf16[768,1024]{1,0:T(8,128)(2,1)} %copy-done.5, bf16[768,1152]{1,0:T(8,128)(2,1)} %bitcast.167, ...), custom_call_target="tpu_custom_call" | custom-call | flops 805306368 | bytes 8650752 | tf_op jit(solution)/shard_map/tokens_back/pallas_call | solution.py:489
  459.3 13.7 %collective-permute-done.31 = bf16[2,4,48,1536]{3,2,1,0:T(8,128)(2,1)S(1)} collective-permute-done((bf16[2,4,48,1536]{3,2,1,0:T(8,128)(2,1)S(1)}, bf16[2,4,48,1536]{3,2,1,0:T(8,128)(2,1)S(1)}, u32[]{:S(2)}, u32[]{:S(2)}) %collective-permute-start.31) | collective-permute-done | bytes 1179680 | tf_op jit(solution)/shard_map/ppermute | solution.py:514
  507.4 14.2 %all-to-all-done.9.gate_in_ref = bf16[8,48,1152]{2,1,0:T(8,128)(2,1)S(1)} async-done(((bf16[8,48,1152]{2,1,0:T(8,128)(2,1)}), bf16[8,48,1152]{2,1,0:T(8,128)(2,1)S(1)}, u32[]{:S(2)}, u32[]{:S(2)}) %all-to-all-start.9) | async-done | bytes 884768 | tf_op jit(solution)/shard_map/all_to_all | solution.py:510
  537.0 26.1 %collective-permute-done.37 = bf16[48,3072]{1,0:T(8,128)(2,1)S(1)} collective-permute-done((bf16[48,3072]{1,0:T(8,128)(2,1)S(1)}, bf16[48,3072]{1,0:T(8,128)(2,1)S(1)}, u32[]{:S(2)}, u32[]{:S(2)}) %collective-permute-start.37) | collective-permute-done | bytes 294944 | tf_op jit(solution)/shard_map/ppermute | solution.py:514
  (345 shorter events, 240.6 us)
Async XLA Ops:
  17.0 233.5 %all-gather.5.cloned.1.call-start = ((), (), s32[]{:S(2)}) async-start(), calls=%async_computation.15 | async-start | bytes 4423680 | tf_op jit(solution)/shard_map/all_gather | solution.py:502
  60.3 42.1 %collective-permute-start.6 = (bf16[2,4,48,1152]{3,2,1,0:T(8,128)(2,1)S(1)}, bf16[2,4,48,1152]{3,2,1,0:T(8,128)(2,1)S(1)}, u32[]{:S(2)}, u32[]{:S(2)}) collective-permute-start(bf16[2,4,48,1152]{3,2,1,0:T(8,128)(2,1)S(1)} %pad_maximum_fusion.5), channel_id=1, source_target_pairs={{0,1},{1,0},{2,3},{3,2},{4,5},{5,4},{6,7},{7,6},{8,9},{9,8},{10,11... | collective-permute-start | bytes 2654216 | tf_op jit(solution)/shard_map/ppermute | solution.py:514
  62.0 40.4 %collective-permute-start.5 = (bf16[4,2,48,1024]{3,2,0,1:T(8,128)(2,1)S(1)}, bf16[4,2,48,1024]{3,2,0,1:T(8,128)(2,1)}, u32[]{:S(2)}, u32[]{:S(2)}) collective-permute-start(bf16[4,2,48,1024]{3,2,0,1:T(8,128)(2,1)S(1)} %pad_maximum_fusion.6), channel_id=1, source_target_pairs={{0,16},{8,24},{16,0},{24,8},{1,17},{9,25},{17,1},{25,9},{2,18},{10... | collective-permute-start | bytes 2359304 | tf_op jit(solution)/shard_map/ppermute | solution.py:514
  63.5 38.8 %collective-permute-start.7 = (bf16[4,48,768]{2,1,0:T(8,128)(2,1)}, bf16[4,48,768]{2,1,0:T(8,128)(2,1)}, u32[]{:S(2)}, u32[]{:S(2)}) collective-permute-start(bf16[4,48,768]{2,1,0:T(8,128)(2,1)} %get-tuple-element.246), channel_id=1, source_target_pairs={{0,1},{1,0},{2,3},{3,2},{4,5},{5,4},{6,7},{7,6},{8,9},{9,8},{10,11... | collective-permute-start | bytes 884744 | tf_op jit(solution)/shard_map/ppermute | solution.py:514
  63.8 38.5 %collective-permute-start.8 = (bf16[4,48,768]{2,1,0:T(8,128)(2,1)}, bf16[4,48,768]{2,1,0:T(8,128)(2,1)}, u32[]{:S(2)}, u32[]{:S(2)}) collective-permute-start(bf16[4,48,768]{2,1,0:T(8,128)(2,1)} %get-tuple-element.245), channel_id=1, source_target_pairs={{0,16},{8,24},{16,0},{24,8},{1,17},{9,25},{17,1},{25,9},{2,18},{10... | collective-permute-start | bytes 884744 | tf_op jit(solution)/shard_map/ppermute | solution.py:514
  68.9 54.6 %all-to-all-start.1 = ((bf16[8,48,2304]{2,1,0:T(8,128)(2,1)}), bf16[8,48,2304]{2,1,0:T(8,128)(2,1)}, u32[]{:S(2)}, u32[]{:S(2)}) async-start(bf16[8,48,2304]{2,1,0:T(8,128)(2,1)} %columns_out.1), calls=%async_computation.1 | async-start | bytes 3538944 | tf_op jit(solution)/shard_map/all_to_all | solution.py:510
  74.4 178.1 %all-gather.3.cloned.1.call-start = ((), (), s32[]{:S(2)}) async-start(), calls=%async_computation.14 | async-start | bytes 8847360 | tf_op jit(solution)/shard_map/all_gather | solution.py:502
  156.3 40.9 %collective-permute-start.14 = (bf16[768,768]{1,0:T(8,128)(2,1)S(1)}, bf16[768,768]{1,0:T(8,128)(2,1)S(1)}, u32[]{:S(2)}, u32[]{:S(2)}) collective-permute-start(bf16[768,768]{1,0:T(8,128)(2,1)S(1)} %bitcast.172), channel_id=1, source_target_pairs={{0,8},{8,0},{16,24},{24,16},{1,9},{9,1},{17,25},{25,17},{2,10},{10... | collective-permute-start | bytes 3538952 | tf_op jit(solution)/shard_map/ppermute | solution.py:514
  172.5 33.1 %all-to-all-start.4 = ((bf16[4,64,1536]{2,1,0:T(8,128)(2,1)}), bf16[4,64,1536]{2,1,0:T(8,128)(2,1)}, u32[]{:S(2)}, u32[]{:S(2)}) async-start(bf16[4,64,1536]{2,1,0:T(8,128)(2,1)} %broadcast_in_dim.27), calls=%async_computation.4 | async-start | bytes 1572864 | tf_op jit(solution)/shard_map/all_to_all | solution.py:510
  232.6 53.7 %collective-permute-start.20 = (bf16[256,1536]{1,0:T(8,128)(2,1)}, bf16[256,1536]{1,0:T(8,128)(2,1)S(1)}, u32[]{:S(2)}, u32[]{:S(2)}) collective-permute-start(bf16[256,1536]{1,0:T(8,128)(2,1)} %bitcast.41.cot_near_ref.refs_4_), channel_id=1, source_target_pairs={{0,1},{1,0},{2,3},{3,2},{4,5},{5,4},{6,7},{7,6},{8,9},{9,8},{10,11... | collective-permute-start | bytes 2359304 | tf_op jit(solution)/shard_map/ppermute | solution.py:514
  249.9 36.4 %collective-permute-start.19 = (bf16[256,1536]{1,0:T(8,128)(2,1)S(1)}, bf16[256,1536]{1,0:T(8,128)(2,1)}, u32[]{:S(2)}, u32[]{:S(2)}) collective-permute-start(bf16[256,1536]{1,0:T(8,128)(2,1)S(1)} %bitcast.194), channel_id=1, source_target_pairs={{0,1},{1,0},{2,3},{3,2},{4,5},{5,4},{6,7},{7,6},{8,9},{9,8},{10,11... | collective-permute-start | bytes 2359304 | tf_op jit(solution)/shard_map/ppermute | solution.py:514
  274.1 34.1 %collective-permute-start.18 = (bf16[256,1536]{1,0:T(8,128)(2,1)S(1)}, bf16[256,1536]{1,0:T(8,128)(2,1)S(1)}, u32[]{:S(2)}, u32[]{:S(2)}) collective-permute-start(bf16[256,1536]{1,0:T(8,128)(2,1)S(1)} %slice.104), channel_id=1, source_target_pairs={{0,1},{1,0},{2,3},{3,2},{4,5},{5,4},{6,7},{7,6},{8,9},{9,8},{10,11... | collective-permute-start | bytes 2359304 | tf_op jit(solution)/shard_map/ppermute | solution.py:514
  315.2 180.5 %reduce-scatter.4.cloned.1.call-start = ((), (), s32[]{:S(2)}) async-start(), calls=%async_computation.16 | async-start | bytes 4423680 | tf_op jit(solution)/shard_map/reduce_scatter | solution.py:506
  341.6 163.2 %reduce-scatter.8.cloned.1.call-start = ((), (), s32[]{:S(2)}) async-start(), calls=%async_computation.18 | async-start | bytes 4423680 | tf_op jit(solution)/shard_map/reduce_scatter | solution.py:506
  362.6 166.9 %reduce-scatter.6.cloned.1.call-start = ((), (), s32[]{:S(2)}) async-start(), calls=%async_computation.17 | async-start | bytes 4423680 | tf_op jit(solution)/shard_map/reduce_scatter | solution.py:506
  408.2 31.6 %all-to-all-start.8 = ((bf16[8,128,512]{2,1,0:T(8,128)(2,1)}), bf16[8,128,512]{2,1,0:T(8,128)(2,1)}, u32[]{:S(2)}, u32[]{:S(2)}) async-start(bf16[8,128,512]{2,1,0:T(8,128)(2,1)} %bitcast.50), calls=%async_computation.8 | async-start | bytes 2097152 | tf_op jit(solution)/shard_map/all_to_all | solution.py:510
  422.5 34.2 %collective-permute-start.32 = (bf16[4,2,48,1536]{3,2,0,1:T(8,128)(2,1)}, bf16[4,2,48,1536]{3,2,0,1:T(8,128)(2,1)}, u32[]{:S(2)}, u32[]{:S(2)}) collective-permute-start(bf16[4,2,48,1536]{3,2,0,1:T(8,128)(2,1)} %bitcast.161), channel_id=1, source_target_pairs={{0,16},{8,24},{16,0},{24,8},{1,17},{9,25},{17,1},{25,9},{2,18},{10... | collective-permute-start | bytes 3538952 | tf_op jit(solution)/shard_map/ppermute | solution.py:514
  425.1 49.3 %collective-permute-start.27 = (bf16[128,1536]{1,0:T(8,128)(2,1)}, bf16[128,1536]{1,0:T(8,128)(2,1)}, u32[]{:S(2)}, u32[]{:S(2)}) collective-permute-start(bf16[128,1536]{1,0:T(8,128)(2,1)} %get-tuple-element.216), channel_id=1, source_target_pairs={{0,2},{2,0},{4,6},{6,4},{1,3},{3,1},{5,7},{7,5},{8,10},{10,8},{12,... | collective-permute-start | bytes 1179656 | tf_op jit(solution)/shard_map/ppermute | solution.py:514
  427.7 46.6 %collective-permute-start.28 = (bf16[128,1536]{1,0:T(8,128)(2,1)}, bf16[128,1536]{1,0:T(8,128)(2,1)}, u32[]{:S(2)}, u32[]{:S(2)}) collective-permute-start(bf16[128,1536]{1,0:T(8,128)(2,1)} %get-tuple-element.217), channel_id=1, source_target_pairs={{0,4},{2,6},{4,0},{6,2},{1,5},{3,7},{5,1},{7,3},{8,12},{10,14},{12... | collective-permute-start | bytes 1179656 | tf_op jit(solution)/shard_map/ppermute | solution.py:514
  428.2 46.2 %collective-permute-start.29 = (bf16[128,1536]{1,0:T(8,128)(2,1)}, bf16[128,1536]{1,0:T(8,128)(2,1)}, u32[]{:S(2)}, u32[]{:S(2)}) collective-permute-start(bf16[128,1536]{1,0:T(8,128)(2,1)} %get-tuple-element.214), channel_id=1, source_target_pairs={{0,6},{2,4},{4,2},{6,0},{1,7},{3,5},{5,3},{7,1},{8,14},{10,12},{12... | collective-permute-start | bytes 1179656 | tf_op jit(solution)/shard_map/ppermute | solution.py:514
  526.1 37.1 %collective-permute-start.37 = (bf16[48,3072]{1,0:T(8,128)(2,1)S(1)}, bf16[48,3072]{1,0:T(8,128)(2,1)S(1)}, u32[]{:S(2)}, u32[]{:S(2)}) collective-permute-start(bf16[48,3072]{1,0:T(8,128)(2,1)S(1)} %get-tuple-element.226), channel_id=1, source_target_pairs={{0,4},{2,6},{4,0},{6,2},{1,5},{3,7},{5,1},{7,3},{8,12},{10,14},{12... | collective-permute-start | bytes 884744 | tf_op jit(solution)/shard_map/ppermute | solution.py:514
  526.5 36.7 %collective-permute-start.36 = (bf16[48,3072]{1,0:T(8,128)(2,1)S(1)}, bf16[48,3072]{1,0:T(8,128)(2,1)}, u32[]{:S(2)}, u32[]{:S(2)}) collective-permute-start(bf16[48,3072]{1,0:T(8,128)(2,1)S(1)} %get-tuple-element.224), channel_id=1, source_target_pairs={{0,2},{2,0},{4,6},{6,4},{1,3},{3,1},{5,7},{7,5},{8,10},{10,8},{12,... | collective-permute-start | bytes 884744 | tf_op jit(solution)/shard_map/ppermute | solution.py:514
  529.5 44.6 %all-to-all-start.10 = ((bf16[8,48,1152]{2,1,0:T(8,128)(2,1)}), bf16[8,48,1152]{2,1,0:T(8,128)(2,1)S(1)}, u32[]{:S(2)}, u32[]{:S(2)}) async-start(bf16[8,48,1152]{2,1,0:T(8,128)(2,1)} %bitcast.187), calls=%async_computation.12 | async-start | bytes 1769472 | tf_op jit(solution)/shard_map/all_to_all | solution.py:510
  534.2 30.2 %collective-permute-start.45 = (bf16[4,48,512]{2,1,0:T(8,128)(2,1)S(1)}, bf16[4,48,512]{2,1,0:T(8,128)(2,1)S(1)}, u32[]{:S(2)}, u32[]{:S(2)}) collective-permute-start(bf16[4,48,512]{2,1,0:T(8,128)(2,1)S(1)} %dynamic-slice_bitcast_fusion.7), channel_id=1, source_target_pairs={{0,1},{1,0},{2,3},{3,2},{4,5},{5,4},{6,7},{7,6},{8,9},{9,8},{10,11... | collective-permute-start | bytes 589832 | tf_op jit(solution)/shard_map/ppermute | solution.py:514
  (100 other events, 994.0 us)
Sparse Core Ops, SparseCore 0:
  19.9 35.8 all-gather.4
  123.6 52.2 all-gather.2
  341.7 39.3 reduce-scatter.3
  383.7 40.4 reduce-scatter.7
  426.6 44.3 reduce-scatter.5

commit v3 on v2

--- a/solution.py
+++ b/solution.py
@@ -164,17 +164,21 @@
         query_ref[:, lanes] = rotate(query[:, lanes], cosine, sine).astype(BF)
     for g in range(KV_HEADS):
         lanes = slice(g * HEAD_DIM, (g + 1) * HEAD_DIM)
-        pair_out_ref[:, lanes] = rotate(key[:, lanes], cosine, sine).astype(BF)
-    pair_out_ref[:, KV_WIDTH:] = (pair[:, KV_WIDTH:] + vbias_ref[...]).astype(BF)
-
-
-def project(core, tokens, left, right, gain, qbias, kbias, vbias, cosine, sine):
+        turned = rotate(key[:, lanes], cosine, sine).astype(BF)
+        for i in range(pair_out_ref.shape[0]):
+            pair_out_ref[i, :, lanes] = turned
+    value = (pair[:, KV_WIDTH:] + vbias_ref[...]).astype(BF)
+    for i in range(pair_out_ref.shape[0]):
+        pair_out_ref[i, :, KV_WIDTH:] = value
+
+
+def project(core, tokens, left, right, gain, qbias, kbias, vbias, cosine, sine, copies):
     rows = tokens.shape[0]
     return pl.pallas_call(
         project_kernel,
         in_specs=[SMEM] + [VMEM] * 11,
         out_specs=[VMEM] * 3,
-        out_shape=[shape((rows, WIDTH), BF), shape((rows, WIDTH), BF), shape((rows, 2 * KV_WIDTH), BF)],
+        out_shape=[shape((rows, WIDTH), BF), shape((rows, WIDTH), BF), shape((copies, rows, 2 * KV_WIDTH), BF)],
         compiler_params=params(),
         cost_estimate=cost(2 * rows * WIDTH * QKV, 2 * WIDTH * QKV + 6 * rows * WIDTH),
         name="project",
@@ -206,28 +210,44 @@
     return (places >= lo_ref[...]) & (places <= hi_ref[...])
 
 
+def heads_per_step(length):
+    return 3 if length <= 1024 else 1
+
+
+def lanes_of(i):
+    return slice(i * HEAD_DIM, (i + 1) * HEAD_DIM)
+
+
 def forward_kernel(q_ref, k_ref, v_ref, lo_ref, hi_ref, mixed_ref, logsum_ref):
-    scores = against(q_ref[...], k_ref[...]) * FACTOR
-    allowed = allowed_of(lo_ref, hi_ref, *scores.shape)
-    scores = jnp.where(allowed, scores, NEGATIVE)
-    top = jnp.max(scores, axis=-1, keepdims=True)
-    weights = jnp.exp(scores - top)
-    total = jnp.sum(weights, axis=-1, keepdims=True)
-    shares = (weights * (1.0 / total)).astype(BF)
-    mixed_ref[...] = matmul(shares, v_ref[...]).astype(BF)
-    logsum_ref[0] = top + jnp.log(total)
+    keys, values = k_ref[...], v_ref[...]
+    allowed = allowed_of(lo_ref, hi_ref, q_ref.shape[0], keys.shape[0])
+    for i in range(logsum_ref.shape[0]):
+        scores = jnp.where(allowed, against(q_ref[:, lanes_of(i)], keys) * FACTOR, NEGATIVE)
+        top = jnp.max(scores, axis=-1, keepdims=True)
+        weights = jnp.exp(scores - top)
+        total = jnp.sum(weights, axis=-1, keepdims=True)
+        shares = (weights * (1.0 / total)).astype(BF)
+        mixed_ref[:, lanes_of(i)] = matmul(shares, values).astype(BF)
+        logsum_ref[i] = top + jnp.log(total)
+
+
+def attention_specs(rows, length, many):
+    steps = GROUP // many
+    head = pl.BlockSpec((rows, many * HEAD_DIM), lambda h: (0, h))
+    key = pl.BlockSpec((length, HEAD_DIM), lambda h: (0, h // steps))
+    value = pl.BlockSpec((length, HEAD_DIM), lambda h: (0, KV_HEADS + h // steps))
+    column = pl.BlockSpec((rows, 1), lambda h: (0, 0))
+    stat = pl.BlockSpec((many, rows, 1), lambda h: (h, 0, 0))
+    return head, key, value, column, stat
 
 
 def attention_forward(queries, pair, lo, hi):
     rows, length = queries.shape[0], pair.shape[0]
-    head = pl.BlockSpec((rows, HEAD_DIM), lambda h: (0, h))
-    key = pl.BlockSpec((length, HEAD_DIM), lambda h: (0, h // GROUP))
-    value = pl.BlockSpec((length, HEAD_DIM), lambda h: (0, KV_HEADS + h // GROUP))
-    column = pl.BlockSpec((rows, 1), lambda h: (0, 0))
-    stat = pl.BlockSpec((1, rows, 1), lambda h: (h, 0, 0))
+    many = heads_per_step(length)
+    head, key, value, column, stat = attention_specs(rows, length, many)
     return pl.pallas_call(
         forward_kernel,
-        grid=(HEADS,),
+        grid=(HEADS // many,),
         in_specs=[head, key, value, column, column],
         out_specs=[head, stat],
         out_shape=[shape((rows, WIDTH), BF), shape((HEADS, rows, 1), F32)],
@@ -241,26 +261,30 @@
     core_ref, q_ref, k_ref, v_ref, g_ref, lo_ref, hi_ref, logsum_ref, cos_ref, sin_ref, cosq_ref, sinq_ref,
     normed_ref, mixed_ref, branch_ref, dq_ref, dkv_ref, keep_ref, send_ref, dk_sum, dv_sum, turned_ref,
 ):
-    head = pl.program_id(0)
-
-    @pl.when(head == 0)
+    step = pl.program_id(0)
+    many = logsum_ref.shape[0]
+    group = step // (GROUP // many)
+    member = lax.rem(step, GROUP // many)
+
+    @pl.when(step == 0)
     def _():
         turned_ref[...] = normed_ref[...].astype(F32).T.astype(BF)
 
-    group = head // GROUP
-    member = lax.rem(head, GROUP)
-    queries, keys, grads = q_ref[...], k_ref[...], g_ref[...]
-    scores = against(queries, keys) * FACTOR
-    allowed = allowed_of(lo_ref, hi_ref, *scores.shape)
-    shares = jnp.where(allowed, jnp.exp(jnp.where(allowed, scores, NEGATIVE) - logsum_ref[0]), 0.0)
-    grad_shares = against(grads, v_ref[...])
-    delta = jnp.sum(shares * grad_shares, axis=-1, keepdims=True)
-    grad_scores = (shares * (grad_shares - delta)).astype(BF)
-    dq = matmul(grad_scores, keys) * FACTOR
-    dq = rotate_back(dq, cosq_ref[...], sinq_ref[...]).astype(BF)
-    dq_ref[...] = dq
-    dk = outer(grad_scores, queries) * FACTOR
-    dv = outer(shares.astype(BF), grads)
+    keys, values = k_ref[...], v_ref[...]
+    allowed = allowed_of(lo_ref, hi_ref, q_ref.shape[0], keys.shape[0])
+    dk, dv = None, None
+    for i in range(many):
+        queries, grads = q_ref[:, lanes_of(i)], g_ref[:, lanes_of(i)]
+        scores = jnp.where(allowed, against(queries, keys) * FACTOR, NEGATIVE)
+        shares = jnp.where(allowed, jnp.exp(scores - logsum_ref[i]), 0.0)
+        grad_shares = against(grads, values)
+        delta = jnp.sum(shares * grad_shares, axis=-1, keepdims=True)
+        grad_scores = (shares * (grad_shares - delta)).astype(BF)
+        dq = matmul(grad_scores, keys) * FACTOR
+        dq_ref[:, lanes_of(i)] = rotate_back(dq, cosq_ref[...], sinq_ref[...]).astype(BF)
+        dk_here = outer(grad_scores, queries) * FACTOR
+        dv_here = outer(shares.astype(BF), grads)
+        dk, dv = (dk_here, dv_here) if i == 0 else (dk + dk_here, dv + dv_here)
 
     @pl.when(member == 0)
     def _():
@@ -272,7 +296,7 @@
         dk_sum[...] += dk
         dv_sum[...] += dv
 
-    @pl.when(member == GROUP - 1)
+    @pl.when(member == GROUP // many - 1)
     def _():
         here = pl.multiple_of(group * HEAD_DIM, HEAD_DIM)
         there = pl.multiple_of(KV_WIDTH + group * HEAD_DIM, HEAD_DIM)
@@ -280,23 +304,24 @@
         dkv_ref[:, pl.ds(there, HEAD_DIM)] = dv_sum[...].astype(BF)
 
     core = core_ref[0]
-    columns = pl.ds(pl.multiple_of(head * HEAD_DIM, HEAD_DIM), HEAD_DIM)
+    width = many * HEAD_DIM
+    columns = pl.ds(pl.multiple_of(step * width, HEAD_DIM), width)
     for lanes, ref, rows in runs_of(core, keep_ref, send_ref):
-        ref[rows, columns] = matmul(turned_ref[lanes, :], dq).astype(BF)
+        ref[rows, columns] = matmul(turned_ref[lanes, :], dq_ref[...]).astype(BF)
     run = keep_ref.shape[0] // 2
-    heads = run // HEAD_DIM
-    place = head // heads
-    row = pl.multiple_of(place // 2 * run + lax.rem(head, heads) * HEAD_DIM, HEAD_DIM)
+    steps = run // width
+    place = step // steps
+    row = pl.multiple_of(place // 2 * run + lax.rem(step, steps) * width, HEAD_DIM)
     terms = outer(mixed_ref[...], branch_ref[...]).astype(BF)
     mine = lax.rem(place, 2) == core
 
     @pl.when(mine)
     def _():
-        keep_ref[pl.ds(row, HEAD_DIM), WIDTH:] = terms
+        keep_ref[pl.ds(row, width), WIDTH:] = terms
 
     @pl.when(jnp.logical_not(mine))
     def _():
-        send_ref[pl.ds(row, HEAD_DIM), WIDTH:] = terms
+        send_ref[pl.ds(row, width), WIDTH:] = terms
 
 
 def attention_backward(
@@ -304,16 +329,13 @@
 ):
     rows, length = queries.shape[0], pair.shape[0]
     once = pl.Buffered(1)
-    head = pl.BlockSpec((rows, HEAD_DIM), lambda h: (0, h))
-    key = pl.BlockSpec((length, HEAD_DIM), lambda h: (0, h // GROUP))
-    value = pl.BlockSpec((length, HEAD_DIM), lambda h: (0, KV_HEADS + h // GROUP))
-    column = pl.BlockSpec((rows, 1), lambda h: (0, 0))
-    stat = pl.BlockSpec((1, rows, 1), lambda h: (h, 0, 0))
+    many = heads_per_step(length)
+    head, key, value, column, stat = attention_specs(rows, length, many)
     fixed = lambda x: pl.BlockSpec(x.shape, lambda h: (0, 0), pipeline_mode=once)
     terms = shape((WIDTH // 2, 2 * WIDTH), BF)
     return pl.pallas_call(
         backward_kernel,
-        grid=(HEADS,),
+        grid=(HEADS // many,),
         in_specs=[SMEM, head, key, value, head, column, column, stat]
         + [fixed(x) for x in (cosine, sine, cosine_own, sine_own, normed)]
         + [head, fixed(grad_branch)],
@@ -332,21 +354,25 @@
 
 
 def branch_kernel(core_ref, mixed_ref, *refs):
-    weights, (tokens_ref, gain_ref, middle_ref, normed_ref) = refs[:4], refs[4:]
+    weights, (tokens_ref, gain_ref, middle_ref, first_ref, second_ref) = refs[:4], refs[4:]
     width = weights[0].shape[1]
     parts = [times(core_ref[0], mixed_ref, weights[2 * i], weights[2 * i + 1], width) for i in range(2)]
     middle = tokens_ref[...].astype(F32) + jnp.concatenate(parts, axis=1)
     middle_ref[...] = middle
-    normed_ref[...] = (middle * inverse_rms(middle) * gain_ref[...]).astype(BF)
-
-
-def branch(core, mixed, out_weight, tokens, gain):
+    normed = (middle * inverse_rms(middle) * gain_ref[...]).astype(BF)
+    half = first_ref.shape[1]
+    for i in range(first_ref.shape[0]):
+        first_ref[i] = normed[:half]
+        second_ref[i] = normed[half:]
+
+
+def branch(core, mixed, out_weight, tokens, gain, copies):
     rows = mixed.shape[0]
     return pl.pallas_call(
         branch_kernel,
         in_specs=[SMEM] + [VMEM] * 7,
-        out_specs=[VMEM] * 2,
-        out_shape=[shape((rows, WIDTH), F32), shape((rows, WIDTH), BF)],
+        out_specs=[VMEM] * 3,
+        out_shape=[shape((rows, WIDTH), F32)] + [shape((copies, rows // 2, WIDTH), BF)] * 2,
         compiler_params=params(),
         cost_estimate=cost(2 * rows * WIDTH * WIDTH, 2 * WIDTH * WIDTH),
         name="branch",
@@ -355,8 +381,9 @@
 
 def mlp_kernel(
     near_ref, other_ref, cot_near_ref, cot_other_ref, gate_ref, up_ref, down_ref,
-    hidden_ref, grad_gate_ref, grad_up_ref, back_ref, forth_ref,
+    hidden_ref, grad_gate_ref, grad_up_ref, back_near_ref, back_other_ref, forth_near_ref, forth_other_ref,
 ):
+    rows = near_ref.shape[0]
     tokens = jnp.concatenate([near_ref[...], other_ref[...]], axis=0)
     cotangent = jnp.concatenate([cot_near_ref[...], cot_other_ref[...]], axis=0)
     gate = matmul(tokens, gate_ref[...])
@@ -370,15 +397,19 @@
     grad_upper = (grad_hidden * silu).astype(BF)
     grad_gate_ref[...] = grad_gate
     grad_up_ref[...] = grad_upper
-    back_ref[...] = (against(grad_gate, gate_ref[...]) + against(grad_upper, up_ref[...])).astype(BF)
-    forth_ref[...] = matmul(hidden, down_ref[...]).astype(BF)
+    back = (against(grad_gate, gate_ref[...]) + against(grad_upper, up_ref[...])).astype(BF)
+    back_near_ref[...] = back[:rows]
+    back_other_ref[...] = back[rows:]
+    forth = matmul(hidden, down_ref[...]).astype(BF)
+    forth_near_ref[...] = forth[:rows]
+    forth_other_ref[...] = forth[rows:]
 
 
 def mlp(near, other, cot_near, cot_other, gate_up, down):
     rows = 2 * near.shape[0]
     chunk = down.shape[0]
     part = lambda n: pl.BlockSpec((WIDTH, chunk), lambda i: (0, n))
-    made = [shape((rows, width), BF) for width in (chunk, chunk, chunk, WIDTH, WIDTH)]
+    made = [shape((rows, chunk), BF)] * 3 + [shape(near.shape, BF)] * 4
     return pl.pallas_call(
         mlp_kernel,
         grid=(1,),
@@ -525,6 +556,10 @@
 def gather_near(value, nz):
     copies = jnp.broadcast_to(value[None], (nz, *value.shape)).reshape(-1, value.shape[1])
     return swap(copies, "z").reshape(nz, *value.shape)
+
+
+def share_near(copies):
+    return swap(copies.reshape(-1, copies.shape[2]), "z").reshape(copies.shape)
 
 
 def add_low(left, right):
@@ -617,8 +652,8 @@
     hi = (offset + jnp.arange(rows, dtype=jnp.int32))[:, None]
     lo = lax.dynamic_slice_in_dim(ident, offset, rows)[:, None]
     tables = [cosine, sine] + [lax.dynamic_slice_in_dim(x, offset, rows) for x in (cosine, sine)] + [lo, hi]
-    near = gather_near(projections, nz)
     turned = columns_out(w_gate, w_up, seq, ctx, run, padded).reshape(ctx * share, -1)
+    near = gather_near(after(projections, turned), nz)
     turned = swap(after(turned, near), CTX)
     left, right = near[:, :, :LEFT], near[:, :, LEFT:]
     left_got, right_got, near, tables = together(
@@ -649,44 +684,42 @@
     value_bias = vectors[3].reshape(devices, share)[:, :vshare].reshape(1, KV_WIDTH)
 
     normed, queries, kv = project(
-        core, tokens, left, right, attn_gain, query_bias, b_key.astype(F32)[None], value_bias, cosine_own, sine_own
-    )
-    near = gather_near(after(kv, cot_near[0]), nz)
+        core, tokens, left, right, attn_gain, query_bias, b_key.astype(F32)[None], value_bias, cosine_own, sine_own, nz
+    )
+    near = share_near(after(kv, cot_near[0]))
     cot_near.append(gather_near(after(cotangent, near)[cuts[1]], nz).reshape(count, WIDTH))
     other = hop(near, "y")
     cot_other = [hop(after(x, other), "y") for x in cot_near]
     kv = pair(near, other, own_y, 1).reshape(length, 2 * KV_WIDTH)
     mixed, logsum = attention_forward(queries, kv, lo, hi)
     mixed, out_weight, cot_other[0] = together(mixed, out_weight, cot_other[0])
-    middle, normed_mlp = branch(core, mixed, out_weight, tokens, mlp_gain)
-
-    x_near = [gather_near(after(normed_mlp, cot_near[1])[cut], nz).reshape(count, WIDTH) for cut in cuts]
+    middle, *copies = branch(core, mixed, out_weight, tokens, mlp_gain, nz)
+
+    copies[1] = after(copies[1], cot_near[1], cot_other[1])
+    x_near = [share_near(x).reshape(count, WIDTH) for x in copies]
     x_other = [hop(x, "y") for x in x_near]
     runs = [mlp(x_near[0], x_other[0], cot_near[0], cot_other[0], gate_up, down)]
     x_other[1] = after(x_other[1], *runs[0])
     runs.append(mlp(x_near[1], x_other[1], cot_near[1], cot_other[1], gate_up, down))
-    hidden, grads_gate, grads_up, back, forth = zip(*runs)
+    hidden, grads_gate, grads_up, back_near, back_other, forth_near, forth_other = zip(*runs)
     sums = []
-    for rows_back in back:
-        sums.append(add_low(rows_back[:count], hop(after(rows_back[count:], *sums), "y")))
+    for i in range(2):
+        sums.append(add_low(back_near[i], hop(after(back_other[i], *sums), "y")))
     far = [swap(sums[0], "z").reshape(nz, half, WIDTH), exchange_near(sums[1].reshape(nz, half, WIDTH), nz, own_z)]
     x_all = [x_near[0], x_other[0], x_near[1], x_other[1]]
     cots = [cot_near[0], cot_other[0], cot_near[1], cot_other[1]]
-    forth_got = [hop(after(x[count:], *sums), "y") for x in forth]
-    grads_gate, grads_up = after((grads_gate, grads_up), sums[1], far[0])
-    hidden = after(hidden, forth_got[0])
+    forth_got = [hop(after(x, *sums), "y") for x in forth_other]
+    grads_gate, grads_up = after((grads_gate, grads_up), far, forth_got[0])
     grad_w_gate, grad_w_up = outer_blocks(x_all, [grads_gate, grads_up], "gate_up_grads")
     grad_w_gate, grad_w_up = scatter_sum(grad_w_gate, "seq"), scatter_sum(grad_w_up, "seq")
-    (grad_w_down,) = outer_blocks(hidden, [cots], "down_grads")
-    grad_w_down = scatter_sum(grad_w_down, "seq")[:run].astype(F32)
-
-    far, forth_got = together(far, forth_got)
+
     grad_middle, grad_branch, grad_mixed, norm_mlp_sum = middle_back(core, far, middle, cotangent, mlp_gain, out_weight)
+    grad_mixed, forth_got = together(grad_mixed, forth_got)
     dq, dkv, keep, send = attention_backward(
         core, queries, kv, grad_mixed, lo, hi, logsum, cosine, sine, cosine_own, sine_own, normed, mixed, grad_branch
     )
     forth = jnp.concatenate(
-        [add_low(x[:count], y).reshape(nz, half, WIDTH) for x, y in zip(forth, forth_got)], axis=1
+        [add_low(x, y).reshape(nz, half, WIDTH) for x, y in zip(forth_near, forth_got)], axis=1
     )
     forth = exchange_near(forth, nz, own_z)
     terms = swap(dkv, CTX).reshape(ctx, rows, 2 * KV_WIDTH)
@@ -697,18 +730,19 @@
     over_y = lambda v: halve(v, "y", 1, 2, own_y, v.ndim - 3)
     sides = add_low(keep, over(send, "core")).reshape(2, nz, 2, share, -1)
     grad_query, grad_out = over_x(sides[..., :WIDTH]), over_y(sides[..., WIDTH:])
-    terms, sides_done = together(terms, sides[:1, :1, :1, :8, :LANES])
+    (grad_w_down,) = outer_blocks(after(hidden, sides), [cots], "down_grads")
+    grad_w_down = scatter_sum(grad_w_down, "seq")[:run].astype(F32)
     grad_w_gate = swap(after(grad_w_gate, terms), CTX).reshape(ctx, share, -1)
-    (grad_pair,) = outer_blocks([normed], [[terms]], "pair_grads")
+    (grad_pair,) = outer_blocks([normed], [[after(terms, grad_out, grad_query)]], "pair_grads")
     grad_tokens, norm_attn_sum, bias = tokens_back(
         core, jnp.concatenate([dq, after(terms, grad_pair)], axis=1), left, right, tokens, attn_gain, grad_middle
     )
-    grad_pair, bias, forth, grad_out, grad_query = together(grad_pair, bias, forth, grad_out, grad_query)
+    grad_pair, bias, forth, grad_w_gate = together(grad_pair, bias, forth, grad_w_gate)
+    grad_w_up = swap(after(grad_w_up, grad_w_gate), CTX).reshape(ctx, share, -1)
     grad_pair = over_core(grad_pair.reshape(2, 2, nz, 2, share, -1))
     grad_out, grad_query = over_x(grad_out), over_y(grad_query)
-    grad_w_gate, grad_out, grad_query, grad_pair = together(grad_w_gate, grad_out, grad_query, grad_pair)
+    grad_w_up, grad_out, grad_query, grad_pair = together(grad_w_up, grad_out, grad_query, grad_pair)
     side = add_up(exchange_near(jnp.concatenate([grad_out, grad_query], axis=2), nz, own_z))
-    grad_w_up = swap(after(grad_w_up, grad_w_gate), CTX).reshape(ctx, share, -1)
     grad_pair = add_up(exchange_near(over_y(over_x(grad_pair)), nz, own_z))
     grad_w_out, grad_w_query = side[:, :WIDTH], side[:, WIDTH:]
     grad_w_key, grad_w_value = grad_pair[:, :KV_WIDTH], grad_pair[:, KV_WIDTH:]

time: 597 us -> 575 us (0.963)
  blocking collectives: 20.2 us -> 0 us
  local copies, waits for them, and re-layouts: 42.7 us -> 27.6 us
  starting transfers between devices: 99.1 us -> 112 us
    all_to_all x1 -> x0, blocking collectives: 20.2 us -> none  [swap(): return lax.all_to_all(value, axis, 0, 0, tiled=True)]
    ppermute x49, waiting for transfers between devices: 155 us -> 174 us  [hop(): return lax.ppermute(value, axis, [(i, i ^ flip) for i in range(size)])]
    all_to_all x10 -> x11, waiting for transfers between devices: 81.7 us -> 66 us  [swap(): return lax.all_to_all(value, axis, 0, 0, tiled=True)]
    all_to_all x10 -> x11, starting transfers between devices: 47.4 us -> 57.5 us  [swap(): return lax.all_to_all(value, axis, 0, 0, tiled=True)]
    pallas_call x2, Pallas kernels: 39.1 us -> 47.4 us  [mlp(): pl.pallas_call(mlp_kernel, grid=(1,), in_specs=[whole(near)] * 4 + [part(...]
    pallas_call x2, Pallas kernels: 34.3 us -> 27.6 us  [the longest x1 19.4 us: attention_backward(): pl.pallas_call(backward_kernel, grid=(HEADS // many,), in_specs=[SMEM, he...]
    unnamed x121 -> x97, local copies, waits for them, and re-layouts: 13.2 us -> 8.25 us
  transfers between devices with their start and end apart: 64 -> 65, of which waited for: 31 -> 30; matrix products, arithmetic and copies ran while one was open for 12% -> 9% of each run, Pallas kernels for 19% -> 21%
where the time goes in v3:
time: 575 us; the launch traced here: 567 us
  waiting for transfers between devices  240 us (42%)
  Pallas kernels  133 us (23%)
  starting transfers between devices  112 us (19%)
  other arithmetic  39 us (7%)
  local copies, waits for them, and re-layouts  27.6 us (5%)
  between operations  15.2 us (3%)
    ppermute x49, waiting for transfers between devices, hop(): return lax.ppermute(value, axis, [(i, i ^ flip) for i in range(size)])  174 us
    all_to_all x11, waiting for transfers between devices, swap(): return lax.all_to_all(value, axis, 0, 0, tiled=True)  66 us
    all_to_all x11, starting transfers between devices, swap(): return lax.all_to_all(value, axis, 0, 0, tiled=True)  57.5 us
    ppermute x49, starting transfers between devices, hop(): return lax.ppermute(value, axis, [(i, i ^ flip) for i in range(size)])  54.5 us
    pallas_call x2, Pallas kernels, mlp(): pl.pallas_call(mlp_kernel, grid=(1,), in_specs=[whole(near)] * 4 + [part(...  47.4 us
    pallas_call x3, Pallas kernels, outer_blocks(): pl.pallas_call(functools.partial(outer_kernel, counts=(len(lefts), *map(l...  25.2 us
    pallas_call x1, Pallas kernels, attention_backward(): pl.pallas_call(backward_kernel, grid=(HEADS // many,), in_specs=[SMEM, he...  19.4 us
    convert_element_type x12, other arithmetic, add_low(): return (left.astype(F32) + right.astype(F32)).astype(BF)  14.9 us
  transfers between devices with their start and end apart: 65, of which 30 were waited for; matrix products, arithmetic and copies ran while one was open for 9% of the time, Pallas kernels for 21%

profile of v3, /device:TPU:0, one launch (start us, length us, event | category | flops | bytes accessed | tf_op | source)
XLA Modules:
  0.0 566.6 jit_solution(2962660027205836491)
XLA Ops:
  13.0 6.3 %all-to-all-start = ((bf16[4,48,2176]{2,1,0:T(8,128)(2,1)}), bf16[4,48,2176]{2,1,0:T(8,128)(2,1)S(1)}, u32[]{:S(2)}, u32[]{:S(2)}) async-start(bf16[4,48,2176]{2,1,0:T(8,128)(2,1)} %broadcast_in_dim.15), calls=%async_computation | async-start | bytes 1671168 | tf_op jit(solution)/shard_map/all_to_all | solution.py:541
  23.7 17.2 %all-to-all-done = bf16[4,48,2176]{2,1,0:T(8,128)(2,1)S(1)} async-done(((bf16[4,48,2176]{2,1,0:T(8,128)(2,1)}), bf16[4,48,2176]{2,1,0:T(8,128)(2,1)S(1)}, u32[]{:S(2)}, u32[]{:S(2)}) %all-to-all-start) | async-done | bytes 835616 | tf_op jit(solution)/shard_map/all_to_all | solution.py:541
  55.6 6.2 %collective-permute-done.1 = bf16[4,48,1152]{2,1,0:T(8,128)(2,1)S(1)} collective-permute-done((bf16[4,48,1152]{2,1,0:T(8,128)(2,1)S(1)}, bf16[4,48,1152]{2,1,0:T(8,128)(2,1)S(1)}, u32[]{:S(2)}, u32[]{:S(2)}) %collective-permute-start.1) | collective-permute-done | bytes 442400 | tf_op jit(solution)/shard_map/ppermute | solution.py:545
  72.8 32.6 %collective-permute-done.7 = bf16[4,48,768]{2,1,0:T(8,128)(2,1)} collective-permute-done((bf16[4,48,768]{2,1,0:T(8,128)(2,1)}, bf16[4,48,768]{2,1,0:T(8,128)(2,1)}, u32[]{:S(2)}, u32[]{:S(2)}) %collective-permute-start.7) | collective-permute-done | bytes 294944 | tf_op jit(solution)/shard_map/ppermute | solution.py:545
  111.8 14.7 %collective-permute-done.11 = bf16[4,2,48,768]{3,2,0,1:T(8,128)(2,1)S(1)} collective-permute-done((bf16[4,2,48,768]{3,2,0,1:T(8,128)(2,1)S(1)}, bf16[4,2,48,768]{3,2,0,1:T(8,128)(2,1)S(1)}, u32[]{:S(2)}, u32[]{:S(2)}) %collective-permute-start.11) | collective-permute-done | bytes 589856 | tf_op jit(solution)/shard_map/ppermute | solution.py:545
  145.5 8.6 %all-to-all-done.2 = bf16[4,64,1536]{2,1,0:T(8,128)(2,1)S(1)} async-done(((bf16[4,64,1536]{2,1,0:T(8,128)(2,1)}), bf16[4,64,1536]{2,1,0:T(8,128)(2,1)S(1)}, u32[]{:S(2)}, u32[]{:S(2)}) %all-to-all-start.2) | async-done | bytes 786464 | tf_op jit(solution)/shard_map/all_to_all | solution.py:541
  160.6 11.7 %all-to-all-done.3 = bf16[4,128,512]{2,1,0:T(8,128)(2,1)} async-done(((bf16[4,128,512]{2,1,0:T(8,128)(2,1)}), bf16[4,128,512]{2,1,0:T(8,128)(2,1)}, u32[]{:S(2)}, u32[]{:S(2)}) %all-to-all-start.3) | async-done | bytes 524320 | tf_op jit(solution)/shard_map/all_to_all | solution.py:541
  189.3 8.2 %attention_forward.1 = (bf16[128,1536]{1,0:T(8,128)(2,1)}, f32[12,128,1]{2,1,0:T(8,128)}) custom-call(bf16[128,1536]{1,0:T(8,128)(2,1)} %get-tuple-element.125.q_ref, bf16[1024,512]{1,0:T(8,128)(2,1)} %bitcast.180, bf16[1024,512]{1,0:T(8,128)(2,1)} %bitcast.181, s32[128,1]{1,0:T(8,128)} %copy.45.lo_ref, s32[128,1]{1,0:T(8,128)} %iota_add_fusion.hi_ref), custom_call_target="tpu_custom_call" | custom-call | flops 805306368 | bytes 1835008 | tf_op jit(solution)/shard_map/attention_forward/pallas_call | solution.py:248
  212.5 16.3 %collective-permute-done.19.cot_other_ref.refs_5_ = bf16[256,1536]{1,0:T(8,128)(2,1)S(1)} collective-permute-done((bf16[256,1536]{1,0:T(8,128)(2,1)}, bf16[256,1536]{1,0:T(8,128)(2,1)S(1)}, u32[]{:S(2)}, u32[]{:S(2)}) %collective-permute-start.19) | collective-permute-done | bytes 786464 | tf_op jit(solution)/shard_map/ppermute | solution.py:545
  234.1 17.9 %all-to-all-done.7 = bf16[4,64,1536]{2,1,0:T(8,128)(2,1)S(1)} async-done(((bf16[4,64,1536]{2,1,0:T(8,128)(2,1)}), bf16[4,64,1536]{2,1,0:T(8,128)(2,1)S(1)}, u32[]{:S(2)}, u32[]{:S(2)}) %all-to-all-start.7) | async-done | bytes 786464 | tf_op jit(solution)/shard_map/all_to_all | solution.py:541
  253.4 19.4 %mlp.2 = (bf16[512,1152]{1,0:T(8,128)(2,1)}, bf16[512,1152]{1,0:T(8,128)(2,1)}, bf16[512,1152]{1,0:T(8,128)(2,1)}, bf16[256,1536]{1,0:T(8,128)(2,1)}, bf16[256,1...) custom-call(bf16[256,1536]{1,0:T(8,128)(2,1)} %bitcast.190, bf16[256,1536]{1,0:T(8,128)(2,1)} %copy-done.42, ...), custom_call_target="tpu_custom_call" | custom-call | flops 10871635968 | bytes 21626880 | tf_op jit(solution)/shard_map/mlp/pallas_call | solution.py:413
  274.4 28.0 %mlp.3 = (bf16[512,1152]{1,0:T(8,128)(2,1)}, bf16[512,1152]{1,0:T(8,128)(2,1)}, bf16[512,1152]{1,0:T(8,128)(2,1)}, bf16[256,1536]{1,0:T(8,128)(2,1)}, bf16[256,1...) custom-call(bf16[256,1536]{1,0:T(8,128)(2,1)} %bitcast.193, ...), custom_call_target="tpu_custom_call" | custom-call | flops 10871635968 | bytes 21626880 | tf_op jit(solution)/shard_map/mlp/pallas_call | solution.py:413
  307.8 13.8 %collective-permute-done.21 = bf16[256,1536]{1,0:T(8,128)(2,1)S(1)} collective-permute-done((bf16[256,1536]{1,0:T(8,128)(2,1)}, bf16[256,1536]{1,0:T(8,128)(2,1)S(1)}, u32[]{:S(2)}, u32[]{:S(2)}) %collective-permute-start.21) | collective-permute-done | bytes 786464 | tf_op jit(solution)/shard_map/ppermute | solution.py:545
  332.8 7.2 %collective-permute-done.23.refs_6_ = bf16[64,1536]{1,0:T(8,128)(2,1)S(1)} collective-permute-done((bf16[64,1536]{1,0:T(8,128)(2,1)S(1)}, bf16[64,1536]{1,0:T(8,128)(2,1)S(1)}, u32[]{:S(2)}, u32[]{:S(2)}) %collective-permute-start.23) | collective-permute-done | bytes 196640 | tf_op jit(solution)/shard_map/ppermute | solution.py:545
  340.0 13.1 %gate_up_grads.1 = (bf16[1536,1152]{1,0:T(8,128)(2,1)}, bf16[1536,1152]{1,0:T(8,128)(2,1)}) custom-call(bf16[256,1536]{1,0:T(8,128)(2,1)} %bitcast.191, bf16[256,1536]{1,0:T(8,128)(2,1)} %copy-done.42, bf16[256,1536]{1,0:T(8,128)(2,1)} %bitcast.194, bf16[256,1536]{1,0:T(8,128)(2,1)} %collective-permute-done.20.other_ref.refs_3_, ...), custom_call_target="tpu_custom_call" | custom-call | flops 7247757312 | bytes 19660800 | tf_op jit(solution)/shard_map/gate_up_grads/pallas_call | solution.py:440
  361.7 10.1 %collective-permute-done.26 = bf16[256,1536]{1,0:T(8,128)(2,1)S(1)} collective-permute-done((bf16[256,1536]{1,0:T(8,128)(2,1)S(1)}, bf16[256,1536]{1,0:T(8,128)(2,1)S(1)}, u32[]{:S(2)}, u32[]{:S(2)}) %collective-permute-start.26) | collective-permute-done | bytes 786464 | tf_op jit(solution)/shard_map/ppermute | solution.py:545
  371.7 19.4 %attention_backward.1 = (bf16[128,1536]{1,0:T(8,128)(2,1)}, bf16[1024,512]{1,0:T(8,128)(2,1)}, bf16[768,3072]{1,0:T(8,128)(2,1)}, bf16[768,3072]{1,0:T(8,128)(2,1)}) custom-call(s32[1]{0:T(128)} %bitcast.core_ref, bf16[128,1536]{1,0:T(8,128)(2,1)} %get-tuple-element.125.q_ref, bf16[1024,512]{1,0:T(8,128)(2,1)} %bitcast.182, bf16[1024,512]{1,0:T(8,128)(2,1)} %bitcast.183, ...), custom_call_target="tpu_custom_call" | custom-call | flops 2013265920 | bytes 4194304 | tf_op jit(solution)/shard_map/attention_backward/pallas_call | solution.py:336
  391.3 6.5 %all-to-all-start.8 = ((bf16[8,128,512]{2,1,0:T(8,128)(2,1)}), bf16[8,128,512]{2,1,0:T(8,128)(2,1)}, u32[]{:S(2)}, u32[]{:S(2)}) async-start(bf16[8,128,512]{2,1,0:T(8,128)(2,1)} %bitcast.49), calls=%async_computation.8 | async-start | bytes 2097152 | tf_op jit(solution)/shard_map/all_to_all | solution.py:541
  427.3 7.6 %down_grads.1 = bf16[1152,1536]{1,0:T(8,128)(2,1)} custom-call(bf16[512,1152]{1,0:T(8,128)(2,1)} %get-tuple-element.208.refs_0_, bf16[512,1152]{1,0:T(8,128)(2,1)} %get-tuple-element.209.refs_1_, bf16[256,1536]{1,0:T(8,128)(2,1)} %bitcast.188, bf16[256,1536]{1,0:T(8,128)(2,1)} %collective-permute-done.16.cot_other_ref.refs_3_, ...), custom_call_target="tpu_custom_call" | custom-call | flops 3623878656 | bytes 11698176 | tf_op jit(solution)/shard_map/down_grads/pallas_call | solution.py:440
  434.9 19.2 %collective-permute-done.29 = bf16[4,2,48,1536]{3,2,0,1:T(8,128)(2,1)} collective-permute-done((bf16[4,2,48,1536]{3,2,0,1:T(8,128)(2,1)}, bf16[4,2,48,1536]{3,2,0,1:T(8,128)(2,1)}, u32[]{:S(2)}, u32[]{:S(2)}) %collective-permute-start.29) | collective-permute-done | bytes 1179680 | tf_op jit(solution)/shard_map/ppermute | solution.py:545
  456.7 7.9 %all-to-all-start.9 = ((bf16[8,48,1152]{2,1,0:T(8,128)(2,1)}), bf16[8,48,1152]{2,1,0:T(8,128)(2,1)S(1)}, u32[]{:S(2)}, u32[]{:S(2)}) async-start(bf16[8,48,1152]{2,1,0:T(8,128)(2,1)} %bitcast.185), calls=%async_computation.10 | async-start | bytes 1769472 | tf_op jit(solution)/shard_map/all_to_all | solution.py:541
  473.7 7.1 %tokens_back.1 = (f32[128,1536]{1,0:T(8,128)}, f32[1,1536]{1,0:T(1,128)}, f32[1,2048]{1,0:T(1,128)}) custom-call(s32[1]{0:T(128)} %bitcast.core_ref, bf16[128,2048]{1,0:T(8,128)(2,1)} %pad_maximum_fusion.11.grads_ref, bf16[768,1024]{1,0:T(8,128)(2,1)} %bitcast.169, bf16[768,1024]{1,0:T(8,128)(2,1)} %copy-done.5, bf16[768,1152]{1,0:T(8,128)(2,1)} %bitcast.165, ...), custom_call_target="tpu_custom_call" | custom-call | flops 805306368 | bytes 8650752 | tf_op jit(solution)/shard_map/tokens_back/pallas_call | solution.py:520
  497.2 6.6 %all-to-all-start.10 = ((bf16[8,48,1152]{2,1,0:T(8,128)(2,1)}), bf16[8,48,1152]{2,1,0:T(8,128)(2,1)}, u32[]{:S(2)}, u32[]{:S(2)}) async-start(bf16[8,48,1152]{2,1,0:T(8,128)(2,1)} %bitcast.184), calls=%async_computation.12 | async-start | bytes 1769472 | tf_op jit(solution)/shard_map/all_to_all | solution.py:541
  536.1 12.5 %collective-permute-done.37 = bf16[48,3072]{1,0:T(8,128)(2,1)S(1)} collective-permute-done((bf16[48,3072]{1,0:T(8,128)(2,1)S(1)}, bf16[48,3072]{1,0:T(8,128)(2,1)S(1)}, u32[]{:S(2)}, u32[]{:S(2)}) %collective-permute-start.37) | collective-permute-done | bytes 294944 | tf_op jit(solution)/shard_map/ppermute | solution.py:545
  (315 shorter events, 233.2 us)
Async XLA Ops:
  13.0 27.8 %all-to-all-start = ((bf16[4,48,2176]{2,1,0:T(8,128)(2,1)}), bf16[4,48,2176]{2,1,0:T(8,128)(2,1)S(1)}, u32[]{:S(2)}, u32[]{:S(2)}) async-start(bf16[4,48,2176]{2,1,0:T(8,128)(2,1)} %broadcast_in_dim.15), calls=%async_computation | async-start | bytes 1671168 | tf_op jit(solution)/shard_map/all_to_all | solution.py:541
  19.3 233.2 %all-gather.5.cloned.1.call-start = ((), (), s32[]{:S(2)}) async-start(), calls=%async_computation.15 | async-start | bytes 4423680 | tf_op jit(solution)/shard_map/all_gather | solution.py:533
  62.1 43.3 %collective-permute-start.6 = (bf16[2,4,48,1152]{3,2,1,0:T(8,128)(2,1)S(1)}, bf16[2,4,48,1152]{3,2,1,0:T(8,128)(2,1)}, u32[]{:S(2)}, u32[]{:S(2)}) collective-permute-start(bf16[2,4,48,1152]{3,2,1,0:T(8,128)(2,1)S(1)} %pad_maximum_fusion.5), channel_id=1, source_target_pairs={{0,1},{1,0},{2,3},{3,2},{4,5},{5,4},{6,7},{7,6},{8,9},{9,8},{10,11... | collective-permute-start | bytes 2654216 | tf_op jit(solution)/shard_map/ppermute | solution.py:545
  63.8 41.6 %collective-permute-start.5 = (bf16[4,2,48,1024]{3,2,0,1:T(8,128)(2,1)S(1)}, bf16[4,2,48,1024]{3,2,0,1:T(8,128)(2,1)}, u32[]{:S(2)}, u32[]{:S(2)}) collective-permute-start(bf16[4,2,48,1024]{3,2,0,1:T(8,128)(2,1)S(1)} %pad_maximum_fusion.6), channel_id=1, source_target_pairs={{0,16},{8,24},{16,0},{24,8},{1,17},{9,25},{17,1},{25,9},{2,18},{10... | collective-permute-start | bytes 2359304 | tf_op jit(solution)/shard_map/ppermute | solution.py:545
  65.2 40.1 %collective-permute-start.7 = (bf16[4,48,768]{2,1,0:T(8,128)(2,1)}, bf16[4,48,768]{2,1,0:T(8,128)(2,1)}, u32[]{:S(2)}, u32[]{:S(2)}) collective-permute-start(bf16[4,48,768]{2,1,0:T(8,128)(2,1)} %get-tuple-element.250), channel_id=1, source_target_pairs={{0,1},{1,0},{2,3},{3,2},{4,5},{5,4},{6,7},{7,6},{8,9},{9,8},{10,11... | collective-permute-start | bytes 884744 | tf_op jit(solution)/shard_map/ppermute | solution.py:545
  65.5 39.8 %collective-permute-start.8 = (bf16[4,48,768]{2,1,0:T(8,128)(2,1)}, bf16[4,48,768]{2,1,0:T(8,128)(2,1)}, u32[]{:S(2)}, u32[]{:S(2)}) collective-permute-start(bf16[4,48,768]{2,1,0:T(8,128)(2,1)} %get-tuple-element.249), channel_id=1, source_target_pairs={{0,16},{8,24},{16,0},{24,8},{1,17},{9,25},{17,1},{25,9},{2,18},{10... | collective-permute-start | bytes 884744 | tf_op jit(solution)/shard_map/ppermute | solution.py:545
  67.2 61.4 %all-to-all-start.1 = ((bf16[8,48,2304]{2,1,0:T(8,128)(2,1)}), bf16[8,48,2304]{2,1,0:T(8,128)(2,1)}, u32[]{:S(2)}, u32[]{:S(2)}) async-start(bf16[8,48,2304]{2,1,0:T(8,128)(2,1)} %bitcast.28), calls=%async_computation.1 | async-start | bytes 3538944 | tf_op jit(solution)/shard_map/all_to_all | solution.py:541
  72.8 179.8 %all-gather.3.cloned.1.call-start = ((), (), s32[]{:S(2)}) async-start(), calls=%async_computation.14 | async-start | bytes 8847360 | tf_op jit(solution)/shard_map/all_gather | solution.py:533
  158.6 38.9 %collective-permute-start.14 = (bf16[768,768]{1,0:T(8,128)(2,1)S(1)}, bf16[768,768]{1,0:T(8,128)(2,1)S(1)}, u32[]{:S(2)}, u32[]{:S(2)}) collective-permute-start(bf16[768,768]{1,0:T(8,128)(2,1)S(1)} %bitcast.170), channel_id=1, source_target_pairs={{0,8},{8,0},{16,24},{24,16},{1,9},{9,1},{17,25},{25,17},{2,10},{10... | collective-permute-start | bytes 3538952 | tf_op jit(solution)/shard_map/ppermute | solution.py:545
  175.9 32.4 %all-to-all-start.6 = ((bf16[4,64,1536]{2,1,0:T(8,128)(2,1)}), bf16[4,64,1536]{2,1,0:T(8,128)(2,1)}, u32[]{:S(2)}, u32[]{:S(2)}) async-start(bf16[4,64,1536]{2,1,0:T(8,128)(2,1)} %broadcast_in_dim.38), calls=%async_computation.6 | async-start | bytes 1572864 | tf_op jit(solution)/shard_map/all_to_all | solution.py:541
  272.9 29.5 %collective-permute-start.18 = (bf16[256,1536]{1,0:T(8,128)(2,1)}, bf16[256,1536]{1,0:T(8,128)(2,1)S(1)}, u32[]{:S(2)}, u32[]{:S(2)}) collective-permute-start(bf16[256,1536]{1,0:T(8,128)(2,1)} %get-tuple-element.147), channel_id=1, source_target_pairs={{0,1},{1,0},{2,3},{3,2},{4,5},{5,4},{6,7},{7,6},{8,9},{9,8},{10,11... | collective-permute-start | bytes 2359304 | tf_op jit(solution)/shard_map/ppermute | solution.py:545
  304.0 36.0 %all-to-all-start.5 = ((bf16[4,64,1536]{2,1,0:T(8,128)(2,1)}), bf16[4,64,1536]{2,1,0:T(8,128)(2,1)S(1)}, u32[]{:S(2)}, u32[]{:S(2)}) async-start(bf16[4,64,1536]{2,1,0:T(8,128)(2,1)} %bitcast.41), calls=%async_computation.5 | async-start | bytes 1572864 | tf_op jit(solution)/shard_map/all_to_all | solution.py:541
  307.8 148.9 %reduce-scatter.4.cloned.1.call-start = ((), (), s32[]{:S(2)}) async-start(), calls=%async_computation.16 | async-start | bytes 4423680 | tf_op jit(solution)/shard_map/reduce_scatter | solution.py:537
  353.2 143.9 %reduce-scatter.6.cloned.1.call-start = ((), (), s32[]{:S(2)}) async-start(), calls=%async_computation.17 | async-start | bytes 4423680 | tf_op jit(solution)/shard_map/reduce_scatter | solution.py:537
  391.3 33.9 %all-to-all-start.8 = ((bf16[8,128,512]{2,1,0:T(8,128)(2,1)}), bf16[8,128,512]{2,1,0:T(8,128)(2,1)}, u32[]{:S(2)}, u32[]{:S(2)}) async-start(bf16[8,128,512]{2,1,0:T(8,128)(2,1)} %bitcast.49), calls=%async_computation.8 | async-start | bytes 2097152 | tf_op jit(solution)/shard_map/all_to_all | solution.py:541
  397.9 159.2 %reduce-scatter.8.cloned.1.call-start = ((), (), s32[]{:S(2)}) async-start(), calls=%async_computation.18 | async-start | bytes 4423680 | tf_op jit(solution)/shard_map/reduce_scatter | solution.py:537
  407.4 46.7 %collective-permute-start.29 = (bf16[4,2,48,1536]{3,2,0,1:T(8,128)(2,1)}, bf16[4,2,48,1536]{3,2,0,1:T(8,128)(2,1)}, u32[]{:S(2)}, u32[]{:S(2)}) collective-permute-start(bf16[4,2,48,1536]{3,2,0,1:T(8,128)(2,1)} %bitcast.159), channel_id=1, source_target_pairs={{0,16},{8,24},{16,0},{24,8},{1,17},{9,25},{17,1},{25,9},{2,18},{10... | collective-permute-start | bytes 3538952 | tf_op jit(solution)/shard_map/ppermute | solution.py:545
  409.9 54.7 %collective-permute-start.28 = (bf16[2,4,48,1536]{3,2,1,0:T(8,128)(2,1)}, bf16[2,4,48,1536]{3,2,1,0:T(8,128)(2,1)}, u32[]{:S(2)}, u32[]{:S(2)}) collective-permute-start(bf16[2,4,48,1536]{3,2,1,0:T(8,128)(2,1)} %dynamic-slice_bitcast_fusion), channel_id=1, source_target_pairs={{0,1},{1,0},{2,3},{3,2},{4,5},{5,4},{6,7},{7,6},{8,9},{9,8},{10,11... | collective-permute-start | bytes 3538952 | tf_op jit(solution)/shard_map/ppermute | solution.py:545
  412.5 69.0 %collective-permute-start.30 = (bf16[128,1536]{1,0:T(8,128)(2,1)}, bf16[128,1536]{1,0:T(8,128)(2,1)}, u32[]{:S(2)}, u32[]{:S(2)}) collective-permute-start(bf16[128,1536]{1,0:T(8,128)(2,1)} %get-tuple-element.220), channel_id=1, source_target_pairs={{0,2},{2,0},{4,6},{6,4},{1,3},{3,1},{5,7},{7,5},{8,10},{10,8},{12,... | collective-permute-start | bytes 1179656 | tf_op jit(solution)/shard_map/ppermute | solution.py:545
  417.9 63.7 %collective-permute-start.31 = (bf16[128,1536]{1,0:T(8,128)(2,1)}, bf16[128,1536]{1,0:T(8,128)(2,1)}, u32[]{:S(2)}, u32[]{:S(2)}) collective-permute-start(bf16[128,1536]{1,0:T(8,128)(2,1)} %get-tuple-element.221), channel_id=1, source_target_pairs={{0,4},{2,6},{4,0},{6,2},{1,5},{3,7},{5,1},{7,3},{8,12},{10,14},{12... | collective-permute-start | bytes 1179656 | tf_op jit(solution)/shard_map/ppermute | solution.py:545
  417.9 63.7 %collective-permute-start.32 = (bf16[128,1536]{1,0:T(8,128)(2,1)}, bf16[128,1536]{1,0:T(8,128)(2,1)}, u32[]{:S(2)}, u32[]{:S(2)}) collective-permute-start(bf16[128,1536]{1,0:T(8,128)(2,1)} %get-tuple-element.218), channel_id=1, source_target_pairs={{0,6},{2,4},{4,2},{6,0},{1,7},{3,5},{5,3},{7,1},{8,14},{10,12},{12... | collective-permute-start | bytes 1179656 | tf_op jit(solution)/shard_map/ppermute | solution.py:545
  456.7 29.7 %all-to-all-start.9 = ((bf16[8,48,1152]{2,1,0:T(8,128)(2,1)}), bf16[8,48,1152]{2,1,0:T(8,128)(2,1)S(1)}, u32[]{:S(2)}, u32[]{:S(2)}) async-start(bf16[8,48,1152]{2,1,0:T(8,128)(2,1)} %bitcast.185), calls=%async_computation.10 | async-start | bytes 1769472 | tf_op jit(solution)/shard_map/all_to_all | solution.py:541
  488.0 24.2 %collective-permute-start.34 = (bf16[4,48,1536]{2,1,0:T(8,128)(2,1)}, bf16[4,48,1536]{2,1,0:T(8,128)(2,1)}, u32[]{:S(2)}, u32[]{:S(2)}) collective-permute-start(bf16[4,48,1536]{2,1,0:T(8,128)(2,1)} %dynamic-slice_bitcast_fusion.1), channel_id=1, source_target_pairs={{0,1},{1,0},{2,3},{3,2},{4,5},{5,4},{6,7},{7,6},{8,9},{9,8},{10,11... | collective-permute-start | bytes 1769480 | tf_op jit(solution)/shard_map/ppermute | solution.py:545
  497.2 25.6 %all-to-all-start.10 = ((bf16[8,48,1152]{2,1,0:T(8,128)(2,1)}), bf16[8,48,1152]{2,1,0:T(8,128)(2,1)}, u32[]{:S(2)}, u32[]{:S(2)}) async-start(bf16[8,48,1152]{2,1,0:T(8,128)(2,1)} %bitcast.184), calls=%async_computation.12 | async-start | bytes 1769472 | tf_op jit(solution)/shard_map/all_to_all | solution.py:541
  (89 other events, 1065.0 us)
Sparse Core Ops, SparseCore 0:
  21.7 35.1 all-gather.4
  128.8 51.0 all-gather.2
  353.3 41.5 reduce-scatter.3
  397.5 58.1 reduce-scatter.5
  458.1 48.8 reduce-scatter.7

commit v4 on v3

--- a/solution.py
+++ b/solution.py
@@ -448,6 +448,35 @@
         cost_estimate=cost(2 * depth * width * sum(across), 2 * (depth + width) * (width + sum(across))),
         name=name,
     )(*lefts, *flat)
+
+
+def outer_by_core_kernel(core_ref, *refs, counts):
+    outer_kernel(*refs, counts=counts)
+
+
+def outer_by_core(core, lefts, rights, name):
+    depth = sum(x.shape[0] for x in lefts)
+    width = lefts[0].shape[1]
+    across = [blocks[0].shape[1] for blocks in rights]
+    tile = width // 4
+    flat = [x for blocks in rights for x in blocks]
+    return pl.pallas_call(
+        functools.partial(outer_by_core_kernel, counts=(len(lefts), *map(len, rights))),
+        grid_spec=pltpu.PrefetchScalarGridSpec(
+            num_scalar_prefetch=1,
+            grid=(4,),
+            in_specs=[
+                pl.BlockSpec((x.shape[0], tile), lambda i, c: (0, 2 * lax.rem(i, 2) + (c[0] ^ lax.div(i, 2))))
+                for x in lefts
+            ]
+            + [pl.BlockSpec(x.shape, lambda i, c: (0, 0), pipeline_mode=pl.Buffered(1)) for x in flat],
+            out_specs=[pl.BlockSpec((tile, n), lambda i, c: (i, 0)) for n in across],
+        ),
+        out_shape=[shape((width, n), BF) for n in across],
+        compiler_params=params(),
+        cost_estimate=cost(2 * depth * width * sum(across), 2 * (depth + width) * (width + sum(across))),
+        name=name,
+    )(core, *lefts, *flat)
 
 
 def middle_kernel(
@@ -710,11 +739,15 @@
     cots = [cot_near[0], cot_other[0], cot_near[1], cot_other[1]]
     forth_got = [hop(after(x, *sums), "y") for x in forth_other]
     grads_gate, grads_up = after((grads_gate, grads_up), far, forth_got[0])
-    grad_w_gate, grad_w_up = outer_blocks(x_all, [grads_gate, grads_up], "gate_up_grads")
-    grad_w_gate, grad_w_up = scatter_sum(grad_w_gate, "seq"), scatter_sum(grad_w_up, "seq")
+    grad_w_gate, grad_w_up = outer_by_core(core, x_all, [grads_gate, grads_up], "gate_up_grads")
+    grads_two = [add_low(v[:WIDTH // 2], hop(v[WIDTH // 2:], "seq", seq, 1)) for v in (grad_w_gate, grad_w_up)]
 
     grad_middle, grad_branch, grad_mixed, norm_mlp_sum = middle_back(core, far, middle, cotangent, mlp_gain, out_weight)
-    grad_mixed, forth_got = together(grad_mixed, forth_got)
+    grad_mixed, forth_got, grads_two = together(grad_mixed, forth_got, grads_two)
+    pairs = [[n, n + 2] for n in range(2)]
+    grad_w_gate, grad_w_up = (
+        lax.psum_scatter(v, "seq", scatter_dimension=0, axis_index_groups=pairs, tiled=True) for v in grads_two
+    )
     dq, dkv, keep, send = attention_backward(
         core, queries, kv, grad_mixed, lo, hi, logsum, cosine, sine, cosine_own, sine_own, normed, mixed, grad_branch
     )

time: 575 us -> 570 us (level)
  Pallas kernels: 133 us -> 123 us
  other arithmetic: 39 us -> 45.5 us
    pallas_call x3 -> x2, Pallas kernels: 25.2 us -> 11.5 us  [outer_blocks(): pl.pallas_call(functools.partial(outer_kernel, counts=(len(lefts), *map(l...]
    pallas_call x0 -> x1, Pallas kernels: none -> 13.4 us  [outer_by_core(): pl.pallas_call(functools.partial(outer_by_core_kernel, counts=(len(lefts)...]
    ppermute x49 -> x51, waiting for transfers between devices: 174 us -> 162 us  [hop(): return lax.ppermute(value, axis, [(i, i ^ flip) for i in range(size)])]
    pallas_call x2, Pallas kernels: 47.4 us -> 39.1 us  [mlp(): pl.pallas_call(mlp_kernel, grid=(1,), in_specs=[whole(near)] * 4 + [part(...]
    convert_element_type x12 -> x14, other arithmetic: 14.9 us -> 21.4 us  [add_low(): return (left.astype(F32) + right.astype(F32)).astype(BF)]
    all_to_all x11, waiting for transfers between devices: 66 us -> 72 us  [swap(): return lax.all_to_all(value, axis, 0, 0, tiled=True)]
    ppermute x49 -> x51, starting transfers between devices: 54.5 us -> 57.2 us  [hop(): return lax.ppermute(value, axis, [(i, i ^ flip) for i in range(size)])]
  transfers between devices with their start and end apart: 65 -> 67, of which waited for: 30 -> 32; matrix products, arithmetic and copies ran while one was open for 9% -> 11% of each run, Pallas kernels for 21% -> 16%
where the time goes in v4:
time: 570 us; the launch traced here: 561 us
  waiting for transfers between devices  238 us (42%)
  Pallas kernels  123 us (22%)
  starting transfers between devices  110 us (19%)
  other arithmetic  45.5 us (8%)
  local copies, waits for them, and re-layouts  30.2 us (5%)
  between operations  15.1 us (3%)
    ppermute x51, waiting for transfers between devices, hop(): return lax.ppermute(value, axis, [(i, i ^ flip) for i in range(size)])  162 us
    all_to_all x11, waiting for transfers between devices, swap(): return lax.all_to_all(value, axis, 0, 0, tiled=True)  72 us
    ppermute x51, starting transfers between devices, hop(): return lax.ppermute(value, axis, [(i, i ^ flip) for i in range(size)])  57.2 us
    all_to_all x11, starting transfers between devices, swap(): return lax.all_to_all(value, axis, 0, 0, tiled=True)  52.6 us
    pallas_call x2, Pallas kernels, mlp(): pl.pallas_call(mlp_kernel, grid=(1,), in_specs=[whole(near)] * 4 + [part(...  39.1 us
    convert_element_type x14, other arithmetic, add_low(): return (left.astype(F32) + right.astype(F32)).astype(BF)  21.4 us
    pallas_call x1, Pallas kernels, attention_backward(): pl.pallas_call(backward_kernel, grid=(HEADS // many,), in_specs=[SMEM, he...  18.6 us
    pallas_call x1, Pallas kernels, outer_by_core(): pl.pallas_call(functools.partial(outer_by_core_kernel, counts=(len(lefts)...  13.4 us
  transfers between devices with their start and end apart: 67, of which 32 were waited for; matrix products, arithmetic and copies ran while one was open for 11% of the time, Pallas kernels for 16%

profile of v4, /device:TPU:0, one launch (start us, length us, event | category | flops | bytes accessed | tf_op | source)
XLA Modules:
  0.0 561.5 jit_solution(11903470339701383283)
XLA Ops:
  13.0 6.3 %all-to-all-start = ((bf16[4,48,2176]{2,1,0:T(8,128)(2,1)}), bf16[4,48,2176]{2,1,0:T(8,128)(2,1)S(1)}, u32[]{:S(2)}, u32[]{:S(2)}) async-start(bf16[4,48,2176]{2,1,0:T(8,128)(2,1)} %broadcast_in_dim.15), calls=%async_computation | async-start | bytes 1671168 | tf_op jit(solution)/shard_map/all_to_all | solution.py:570
  23.7 17.2 %all-to-all-done = bf16[4,48,2176]{2,1,0:T(8,128)(2,1)S(1)} async-done(((bf16[4,48,2176]{2,1,0:T(8,128)(2,1)}), bf16[4,48,2176]{2,1,0:T(8,128)(2,1)S(1)}, u32[]{:S(2)}, u32[]{:S(2)}) %all-to-all-start) | async-done | bytes 835616 | tf_op jit(solution)/shard_map/all_to_all | solution.py:570
  55.6 6.3 %collective-permute-done.1 = bf16[4,48,1152]{2,1,0:T(8,128)(2,1)S(1)} collective-permute-done((bf16[4,48,1152]{2,1,0:T(8,128)(2,1)S(1)}, bf16[4,48,1152]{2,1,0:T(8,128)(2,1)S(1)}, u32[]{:S(2)}, u32[]{:S(2)}) %collective-permute-start.1) | collective-permute-done | bytes 442400 | tf_op jit(solution)/shard_map/ppermute | solution.py:574
  72.8 32.6 %collective-permute-done.7 = bf16[4,48,768]{2,1,0:T(8,128)(2,1)} collective-permute-done((bf16[4,48,768]{2,1,0:T(8,128)(2,1)}, bf16[4,48,768]{2,1,0:T(8,128)(2,1)}, u32[]{:S(2)}, u32[]{:S(2)}) %collective-permute-start.7) | collective-permute-done | bytes 294944 | tf_op jit(solution)/shard_map/ppermute | solution.py:574
  111.8 14.7 %collective-permute-done.11 = bf16[4,2,48,768]{3,2,0,1:T(8,128)(2,1)S(1)} collective-permute-done((bf16[4,2,48,768]{3,2,0,1:T(8,128)(2,1)S(1)}, bf16[4,2,48,768]{3,2,0,1:T(8,128)(2,1)S(1)}, u32[]{:S(2)}, u32[]{:S(2)}) %collective-permute-start.11) | collective-permute-done | bytes 589856 | tf_op jit(solution)/shard_map/ppermute | solution.py:574
  145.5 8.6 %all-to-all-done.2 = bf16[4,64,1536]{2,1,0:T(8,128)(2,1)S(1)} async-done(((bf16[4,64,1536]{2,1,0:T(8,128)(2,1)}), bf16[4,64,1536]{2,1,0:T(8,128)(2,1)S(1)}, u32[]{:S(2)}, u32[]{:S(2)}) %all-to-all-start.2) | async-done | bytes 786464 | tf_op jit(solution)/shard_map/all_to_all | solution.py:570
  160.6 11.7 %all-to-all-done.3 = bf16[4,128,512]{2,1,0:T(8,128)(2,1)} async-done(((bf16[4,128,512]{2,1,0:T(8,128)(2,1)}), bf16[4,128,512]{2,1,0:T(8,128)(2,1)}, u32[]{:S(2)}, u32[]{:S(2)}) %all-to-all-start.3) | async-done | bytes 524320 | tf_op jit(solution)/shard_map/all_to_all | solution.py:570
  189.2 8.2 %attention_forward.1 = (bf16[128,1536]{1,0:T(8,128)(2,1)}, f32[12,128,1]{2,1,0:T(8,128)}) custom-call(bf16[128,1536]{1,0:T(8,128)(2,1)} %get-tuple-element.127.q_ref, bf16[1024,512]{1,0:T(8,128)(2,1)} %bitcast.180, bf16[1024,512]{1,0:T(8,128)(2,1)} %bitcast.181, s32[128,1]{1,0:T(8,128)} %copy.45.lo_ref, s32[128,1]{1,0:T(8,128)} %iota_add_fusion.hi_ref), custom_call_target="tpu_custom_call" | custom-call | flops 805306368 | bytes 1835008 | tf_op jit(solution)/shard_map/attention_forward/pallas_call | solution.py:248
  197.5 5.9 %collective-permute-done.16.cot_other_ref.refs_3_ = bf16[256,1536]{1,0:T(8,128)(2,1)} collective-permute-done((bf16[256,1536]{1,0:T(8,128)(2,1)}, bf16[256,1536]{1,0:T(8,128)(2,1)}, u32[]{:S(2)}, u32[]{:S(2)}) %collective-permute-start.16) | collective-permute-done | bytes 786464 | tf_op jit(solution)/shard_map/ppermute | solution.py:574
  212.5 16.3 %collective-permute-done.19.cot_other_ref.refs_5_ = bf16[256,1536]{1,0:T(8,128)(2,1)S(1)} collective-permute-done((bf16[256,1536]{1,0:T(8,128)(2,1)}, bf16[256,1536]{1,0:T(8,128)(2,1)S(1)}, u32[]{:S(2)}, u32[]{:S(2)}) %collective-permute-start.19) | collective-permute-done | bytes 786464 | tf_op jit(solution)/shard_map/ppermute | solution.py:574
  234.1 17.9 %all-to-all-done.7 = bf16[4,64,1536]{2,1,0:T(8,128)(2,1)S(1)} async-done(((bf16[4,64,1536]{2,1,0:T(8,128)(2,1)}), bf16[4,64,1536]{2,1,0:T(8,128)(2,1)S(1)}, u32[]{:S(2)}, u32[]{:S(2)}) %all-to-all-start.7) | async-done | bytes 786464 | tf_op jit(solution)/shard_map/all_to_all | solution.py:570
  253.5 19.4 %mlp.2 = (bf16[512,1152]{1,0:T(8,128)(2,1)}, bf16[512,1152]{1,0:T(8,128)(2,1)}, bf16[512,1152]{1,0:T(8,128)(2,1)}, bf16[256,1536]{1,0:T(8,128)(2,1)}, bf16[256,1...) custom-call(bf16[256,1536]{1,0:T(8,128)(2,1)} %bitcast.190, bf16[256,1536]{1,0:T(8,128)(2,1)} %copy-done.42, ...), custom_call_target="tpu_custom_call" | custom-call | flops 10871635968 | bytes 21626880 | tf_op jit(solution)/shard_map/mlp/pallas_call | solution.py:413
  274.4 19.7 %mlp.3 = (bf16[512,1152]{1,0:T(8,128)(2,1)}, bf16[512,1152]{1,0:T(8,128)(2,1)}, bf16[512,1152]{1,0:T(8,128)(2,1)}, bf16[256,1536]{1,0:T(8,128)(2,1)}, bf16[256,1...) custom-call(bf16[256,1536]{1,0:T(8,128)(2,1)} %bitcast.193, ...), custom_call_target="tpu_custom_call" | custom-call | flops 10871635968 | bytes 21626880 | tf_op jit(solution)/shard_map/mlp/pallas_call | solution.py:413
  299.5 13.8 %collective-permute-done.21 = bf16[256,1536]{1,0:T(8,128)(2,1)S(1)} collective-permute-done((bf16[256,1536]{1,0:T(8,128)(2,1)}, bf16[256,1536]{1,0:T(8,128)(2,1)S(1)}, u32[]{:S(2)}, u32[]{:S(2)}) %collective-permute-start.21) | collective-permute-done | bytes 786464 | tf_op jit(solution)/shard_map/ppermute | solution.py:574
  324.5 7.2 %collective-permute-done.23.refs_6_ = bf16[64,1536]{1,0:T(8,128)(2,1)S(1)} collective-permute-done((bf16[64,1536]{1,0:T(8,128)(2,1)S(1)}, bf16[64,1536]{1,0:T(8,128)(2,1)S(1)}, u32[]{:S(2)}, u32[]{:S(2)}) %collective-permute-start.23) | collective-permute-done | bytes 196640 | tf_op jit(solution)/shard_map/ppermute | solution.py:574
  332.4 13.4 %gate_up_grads.1 = (bf16[1536,1152]{1,0:T(8,128)(2,1)}, bf16[1536,1152]{1,0:T(8,128)(2,1)}) custom-call(s32[1]{0:T(128)} %bitcast.core_ref, bf16[256,1536]{1,0:T(8,128)(2,1)} %bitcast.191, bf16[256,1536]{1,0:T(8,128)(2,1)} %copy-done.42, bf16[256,1536]{1,0:T(8,128)(2,1)} %bitcast.194, bf16[256,1536]{1,0:T(8,128)(2,1)} %collective-permute-done.20.other_ref.refs_3_, ...), custom_call_target="tpu_custom_call" | custom-call | flops 7247757312 | bytes 19660800 | tf_op jit(solution)/shard_map/gate_up_grads/pallas_call | solution.py:463
  363.8 6.1 %collective-permute-done.26 = bf16[256,1536]{1,0:T(8,128)(2,1)} collective-permute-done((bf16[256,1536]{1,0:T(8,128)(2,1)}, bf16[256,1536]{1,0:T(8,128)(2,1)}, u32[]{:S(2)}, u32[]{:S(2)}) %collective-permute-start.26) | collective-permute-done | bytes 786464 | tf_op jit(solution)/shard_map/ppermute | solution.py:574
  369.9 18.6 %attention_backward.1 = (bf16[128,1536]{1,0:T(8,128)(2,1)}, bf16[1024,512]{1,0:T(8,128)(2,1)}, bf16[768,3072]{1,0:T(8,128)(2,1)}, bf16[768,3072]{1,0:T(8,128)(2,1)}) custom-call(s32[1]{0:T(128)} %bitcast.core_ref, bf16[128,1536]{1,0:T(8,128)(2,1)} %get-tuple-element.127.q_ref, bf16[1024,512]{1,0:T(8,128)(2,1)} %bitcast.182, bf16[1024,512]{1,0:T(8,128)(2,1)} %bitcast.183, ...), custom_call_target="tpu_custom_call" | custom-call | flops 2013265920 | bytes 4194304 | tf_op jit(solution)/shard_map/attention_backward/pallas_call | solution.py:336
  426.9 6.3 %all-to-all-start.9 = ((bf16[8,48,1152]{2,1,0:T(8,128)(2,1)}), bf16[8,48,1152]{2,1,0:T(8,128)(2,1)}, u32[]{:S(2)}, u32[]{:S(2)}) async-start(bf16[8,48,1152]{2,1,0:T(8,128)(2,1)} %bitcast.185), calls=%async_computation.10 | async-start | bytes 1769472 | tf_op jit(solution)/shard_map/all_to_all | solution.py:570
  433.2 7.6 %down_grads.1 = bf16[1152,1536]{1,0:T(8,128)(2,1)} custom-call(bf16[512,1152]{1,0:T(8,128)(2,1)} %get-tuple-element.212.refs_0_, bf16[512,1152]{1,0:T(8,128)(2,1)} %get-tuple-element.213.refs_1_, bf16[256,1536]{1,0:T(8,128)(2,1)} %bitcast.188, bf16[256,1536]{1,0:T(8,128)(2,1)} %collective-permute-done.16.cot_other_ref.refs_3_, ...), custom_call_target="tpu_custom_call" | custom-call | flops 3623878656 | bytes 11698176 | tf_op jit(solution)/shard_map/down_grads/pallas_call | solution.py:440
  456.0 6.7 %tokens_back.1 = (f32[128,1536]{1,0:T(8,128)}, f32[1,1536]{1,0:T(1,128)}, f32[1,2048]{1,0:T(1,128)}) custom-call(s32[1]{0:T(128)} %bitcast.core_ref, bf16[128,2048]{1,0:T(8,128)(2,1)} %pad_maximum_fusion.11.grads_ref, bf16[768,1024]{1,0:T(8,128)(2,1)} %bitcast.169, bf16[768,1024]{1,0:T(8,128)(2,1)} %copy-done.5, bf16[768,1152]{1,0:T(8,128)(2,1)} %bitcast.165, ...), custom_call_target="tpu_custom_call" | custom-call | flops 805306368 | bytes 8650752 | tf_op jit(solution)/shard_map/tokens_back/pallas_call | solution.py:549
  462.8 10.7 %all-to-all-done.9.gate_in_ref = bf16[8,48,1152]{2,1,0:T(8,128)(2,1)} async-done(((bf16[8,48,1152]{2,1,0:T(8,128)(2,1)}), bf16[8,48,1152]{2,1,0:T(8,128)(2,1)}, u32[]{:S(2)}, u32[]{:S(2)}) %all-to-all-start.9) | async-done | bytes 884768 | tf_op jit(solution)/shard_map/all_to_all | solution.py:570
  491.7 8.9 %collective-permute-done.44 = f32[1,5120]{1,0:T(1,128)S(1)} collective-permute-done((f32[1,5120]{1,0:T(1,128)S(1)}, f32[1,5120]{1,0:T(1,128)S(1)}, u32[]{:S(2)}, u32[]{:S(2)}) %collective-permute-start.44) | collective-permute-done | bytes 20512 | tf_op jit(solution)/shard_map/ppermute | solution.py:574
  528.8 14.7 %collective-permute-done.39 = bf16[48,3072]{1,0:T(8,128)(2,1)S(1)} collective-permute-done((bf16[48,3072]{1,0:T(8,128)(2,1)S(1)}, bf16[48,3072]{1,0:T(8,128)(2,1)S(1)}, u32[]{:S(2)}, u32[]{:S(2)}) %collective-permute-start.39) | collective-permute-done | bytes 294944 | tf_op jit(solution)/shard_map/ppermute | solution.py:574
  (321 shorter events, 247.6 us)
Async XLA Ops:
  13.0 27.8 %all-to-all-start = ((bf16[4,48,2176]{2,1,0:T(8,128)(2,1)}), bf16[4,48,2176]{2,1,0:T(8,128)(2,1)S(1)}, u32[]{:S(2)}, u32[]{:S(2)}) async-start(bf16[4,48,2176]{2,1,0:T(8,128)(2,1)} %broadcast_in_dim.15), calls=%async_computation | async-start | bytes 1671168 | tf_op jit(solution)/shard_map/all_to_all | solution.py:570
  19.3 233.2 %all-gather.5.cloned.1.call-start = ((), (), s32[]{:S(2)}) async-start(), calls=%async_computation.15 | async-start | bytes 4423680 | tf_op jit(solution)/shard_map/all_gather | solution.py:562
  62.1 43.3 %collective-permute-start.6 = (bf16[2,4,48,1152]{3,2,1,0:T(8,128)(2,1)S(1)}, bf16[2,4,48,1152]{3,2,1,0:T(8,128)(2,1)}, u32[]{:S(2)}, u32[]{:S(2)}) collective-permute-start(bf16[2,4,48,1152]{3,2,1,0:T(8,128)(2,1)S(1)} %pad_maximum_fusion.5), channel_id=1, source_target_pairs={{0,1},{1,0},{2,3},{3,2},{4,5},{5,4},{6,7},{7,6},{8,9},{9,8},{10,11... | collective-permute-start | bytes 2654216 | tf_op jit(solution)/shard_map/ppermute | solution.py:574
  63.8 41.6 %collective-permute-start.5 = (bf16[4,2,48,1024]{3,2,0,1:T(8,128)(2,1)S(1)}, bf16[4,2,48,1024]{3,2,0,1:T(8,128)(2,1)}, u32[]{:S(2)}, u32[]{:S(2)}) collective-permute-start(bf16[4,2,48,1024]{3,2,0,1:T(8,128)(2,1)S(1)} %pad_maximum_fusion.6), channel_id=1, source_target_pairs={{0,16},{8,24},{16,0},{24,8},{1,17},{9,25},{17,1},{25,9},{2,18},{10... | collective-permute-start | bytes 2359304 | tf_op jit(solution)/shard_map/ppermute | solution.py:574
  65.2 40.1 %collective-permute-start.7 = (bf16[4,48,768]{2,1,0:T(8,128)(2,1)}, bf16[4,48,768]{2,1,0:T(8,128)(2,1)}, u32[]{:S(2)}, u32[]{:S(2)}) collective-permute-start(bf16[4,48,768]{2,1,0:T(8,128)(2,1)} %get-tuple-element.254), channel_id=1, source_target_pairs={{0,1},{1,0},{2,3},{3,2},{4,5},{5,4},{6,7},{7,6},{8,9},{9,8},{10,11... | collective-permute-start | bytes 884744 | tf_op jit(solution)/shard_map/ppermute | solution.py:574
  65.5 39.8 %collective-permute-start.8 = (bf16[4,48,768]{2,1,0:T(8,128)(2,1)}, bf16[4,48,768]{2,1,0:T(8,128)(2,1)}, u32[]{:S(2)}, u32[]{:S(2)}) collective-permute-start(bf16[4,48,768]{2,1,0:T(8,128)(2,1)} %get-tuple-element.253), channel_id=1, source_target_pairs={{0,16},{8,24},{16,0},{24,8},{1,17},{9,25},{17,1},{25,9},{2,18},{10... | collective-permute-start | bytes 884744 | tf_op jit(solution)/shard_map/ppermute | solution.py:574
  67.2 61.4 %all-to-all-start.1 = ((bf16[8,48,2304]{2,1,0:T(8,128)(2,1)}), bf16[8,48,2304]{2,1,0:T(8,128)(2,1)}, u32[]{:S(2)}, u32[]{:S(2)}) async-start(bf16[8,48,2304]{2,1,0:T(8,128)(2,1)} %bitcast.28), calls=%async_computation.1 | async-start | bytes 3538944 | tf_op jit(solution)/shard_map/all_to_all | solution.py:570
  72.8 179.8 %all-gather.3.cloned.1.call-start = ((), (), s32[]{:S(2)}) async-start(), calls=%async_computation.14 | async-start | bytes 8847360 | tf_op jit(solution)/shard_map/all_gather | solution.py:562
  158.6 38.9 %collective-permute-start.14 = (bf16[768,768]{1,0:T(8,128)(2,1)S(1)}, bf16[768,768]{1,0:T(8,128)(2,1)S(1)}, u32[]{:S(2)}, u32[]{:S(2)}) collective-permute-start(bf16[768,768]{1,0:T(8,128)(2,1)S(1)} %bitcast.170), channel_id=1, source_target_pairs={{0,8},{8,0},{16,24},{24,16},{1,9},{9,1},{17,25},{25,17},{2,10},{10... | collective-permute-start | bytes 3538952 | tf_op jit(solution)/shard_map/ppermute | solution.py:574
  175.9 32.4 %all-to-all-start.6 = ((bf16[4,64,1536]{2,1,0:T(8,128)(2,1)}), bf16[4,64,1536]{2,1,0:T(8,128)(2,1)}, u32[]{:S(2)}, u32[]{:S(2)}) async-start(bf16[4,64,1536]{2,1,0:T(8,128)(2,1)} %broadcast_in_dim.38), calls=%async_computation.6 | async-start | bytes 1572864 | tf_op jit(solution)/shard_map/all_to_all | solution.py:570
  295.7 36.7 %all-to-all-start.5 = ((bf16[4,64,1536]{2,1,0:T(8,128)(2,1)}), bf16[4,64,1536]{2,1,0:T(8,128)(2,1)S(1)}, u32[]{:S(2)}, u32[]{:S(2)}) async-start(bf16[4,64,1536]{2,1,0:T(8,128)(2,1)} %bitcast.41), calls=%async_computation.5 | async-start | bytes 1572864 | tf_op jit(solution)/shard_map/all_to_all | solution.py:570
  299.5 127.4 %reduce-scatter.4.cloned.1.call-start = ((), (), s32[]{:S(2)}) async-start(), calls=%async_computation.16 | async-start | bytes 2654208 | tf_op jit(solution)/shard_map/reduce_scatter | solution.py:749
  388.7 32.8 %all-to-all-start.8 = ((bf16[8,128,512]{2,1,0:T(8,128)(2,1)}), bf16[8,128,512]{2,1,0:T(8,128)(2,1)}, u32[]{:S(2)}, u32[]{:S(2)}) async-start(bf16[8,128,512]{2,1,0:T(8,128)(2,1)} %bitcast.49), calls=%async_computation.8 | async-start | bytes 2097152 | tf_op jit(solution)/shard_map/all_to_all | solution.py:570
  394.2 88.1 %reduce-scatter.6.cloned.1.call-start = ((), (), s32[]{:S(2)}) async-start(), calls=%async_computation.17 | async-start | bytes 2654208 | tf_op jit(solution)/shard_map/reduce_scatter | solution.py:749
  404.4 41.5 %collective-permute-start.31 = (bf16[4,2,48,1536]{3,2,0,1:T(8,128)(2,1)}, bf16[4,2,48,1536]{3,2,0,1:T(8,128)(2,1)}, u32[]{:S(2)}, u32[]{:S(2)}) collective-permute-start(bf16[4,2,48,1536]{3,2,0,1:T(8,128)(2,1)} %bitcast.159), channel_id=1, source_target_pairs={{0,16},{8,24},{16,0},{24,8},{1,17},{9,25},{17,1},{25,9},{2,18},{10... | collective-permute-start | bytes 3538952 | tf_op jit(solution)/shard_map/ppermute | solution.py:574
  408.2 40.3 %collective-permute-start.30 = (bf16[2,4,48,1536]{3,2,1,0:T(8,128)(2,1)}, bf16[2,4,48,1536]{3,2,1,0:T(8,128)(2,1)}, u32[]{:S(2)}, u32[]{:S(2)}) collective-permute-start(bf16[2,4,48,1536]{3,2,1,0:T(8,128)(2,1)} %dynamic-slice_bitcast_fusion), channel_id=1, source_target_pairs={{0,1},{1,0},{2,3},{3,2},{4,5},{5,4},{6,7},{7,6},{8,9},{9,8},{10,11... | collective-permute-start | bytes 3538952 | tf_op jit(solution)/shard_map/ppermute | solution.py:574
  410.9 51.9 %collective-permute-start.32 = (bf16[128,1536]{1,0:T(8,128)(2,1)}, bf16[128,1536]{1,0:T(8,128)(2,1)}, u32[]{:S(2)}, u32[]{:S(2)}) collective-permute-start(bf16[128,1536]{1,0:T(8,128)(2,1)} %get-tuple-element.224), channel_id=1, source_target_pairs={{0,2},{2,0},{4,6},{6,4},{1,3},{3,1},{5,7},{7,5},{8,10},{10,8},{12,... | collective-permute-start | bytes 1179656 | tf_op jit(solution)/shard_map/ppermute | solution.py:574
  414.0 48.8 %collective-permute-start.33 = (bf16[128,1536]{1,0:T(8,128)(2,1)}, bf16[128,1536]{1,0:T(8,128)(2,1)}, u32[]{:S(2)}, u32[]{:S(2)}) collective-permute-start(bf16[128,1536]{1,0:T(8,128)(2,1)} %get-tuple-element.225), channel_id=1, source_target_pairs={{0,4},{2,6},{4,0},{6,2},{1,5},{3,7},{5,1},{7,3},{8,12},{10,14},{12... | collective-permute-start | bytes 1179656 | tf_op jit(solution)/shard_map/ppermute | solution.py:574
  414.0 48.8 %collective-permute-start.34 = (bf16[128,1536]{1,0:T(8,128)(2,1)}, bf16[128,1536]{1,0:T(8,128)(2,1)}, u32[]{:S(2)}, u32[]{:S(2)}) collective-permute-start(bf16[128,1536]{1,0:T(8,128)(2,1)} %get-tuple-element.222), channel_id=1, source_target_pairs={{0,6},{2,4},{4,2},{6,0},{1,7},{3,5},{5,3},{7,1},{8,14},{10,12},{12... | collective-permute-start | bytes 1179656 | tf_op jit(solution)/shard_map/ppermute | solution.py:574
  426.9 46.5 %all-to-all-start.9 = ((bf16[8,48,1152]{2,1,0:T(8,128)(2,1)}), bf16[8,48,1152]{2,1,0:T(8,128)(2,1)}, u32[]{:S(2)}, u32[]{:S(2)}) async-start(bf16[8,48,1152]{2,1,0:T(8,128)(2,1)} %bitcast.185), calls=%async_computation.10 | async-start | bytes 1769472 | tf_op jit(solution)/shard_map/all_to_all | solution.py:570
  433.2 118.8 %reduce-scatter.8.cloned.1.call-start = ((), (), s32[]{:S(2)}) async-start(), calls=%async_computation.18 | async-start | bytes 4423680 | tf_op jit(solution)/shard_map/reduce_scatter | solution.py:566
  482.3 32.9 %all-to-all-start.10 = ((bf16[8,48,1152]{2,1,0:T(8,128)(2,1)}), bf16[8,48,1152]{2,1,0:T(8,128)(2,1)}, u32[]{:S(2)}, u32[]{:S(2)}) async-start(bf16[8,48,1152]{2,1,0:T(8,128)(2,1)} %bitcast.184), calls=%async_computation.12 | async-start | bytes 1769472 | tf_op jit(solution)/shard_map/all_to_all | solution.py:570
  486.6 28.1 %collective-permute-start.35 = (bf16[4,48,1536]{2,1,0:T(8,128)(2,1)S(1)}, bf16[4,48,1536]{2,1,0:T(8,128)(2,1)S(1)}, u32[]{:S(2)}, u32[]{:S(2)}) collective-permute-start(bf16[4,48,1536]{2,1,0:T(8,128)(2,1)S(1)} %dynamic-slice_bitcast_fusion.2), channel_id=1, source_target_pairs={{0,16},{8,24},{16,0},{24,8},{1,17},{9,25},{17,1},{25,9},{2,18},{10... | collective-permute-start | bytes 1769480 | tf_op jit(solution)/shard_map/ppermute | solution.py:574
  488.0 26.9 %collective-permute-start.36 = (bf16[4,48,1536]{2,1,0:T(8,128)(2,1)}, bf16[4,48,1536]{2,1,0:T(8,128)(2,1)S(1)}, u32[]{:S(2)}, u32[]{:S(2)}) collective-permute-start(bf16[4,48,1536]{2,1,0:T(8,128)(2,1)} %dynamic-slice_bitcast_fusion.1), channel_id=1, source_target_pairs={{0,1},{1,0},{2,3},{3,2},{4,5},{5,4},{6,7},{7,6},{8,9},{9,8},{10,11... | collective-permute-start | bytes 1769480 | tf_op jit(solution)/shard_map/ppermute | solution.py:574
  (90 other events, 1088.6 us)
Sparse Core Ops, SparseCore 0:
  21.7 35.1 all-gather.4
  128.8 51.0 all-gather.2
  388.8 38.0 reduce-scatter.3
  429.1 32.8 reduce-scatter.5
  464.5 53.2 reduce-scatter.7

commit v5 on v4

--- a/solution.py
+++ b/solution.py
@@ -164,21 +164,17 @@
         query_ref[:, lanes] = rotate(query[:, lanes], cosine, sine).astype(BF)
     for g in range(KV_HEADS):
         lanes = slice(g * HEAD_DIM, (g + 1) * HEAD_DIM)
-        turned = rotate(key[:, lanes], cosine, sine).astype(BF)
-        for i in range(pair_out_ref.shape[0]):
-            pair_out_ref[i, :, lanes] = turned
-    value = (pair[:, KV_WIDTH:] + vbias_ref[...]).astype(BF)
-    for i in range(pair_out_ref.shape[0]):
-        pair_out_ref[i, :, KV_WIDTH:] = value
-
-
-def project(core, tokens, left, right, gain, qbias, kbias, vbias, cosine, sine, copies):
+        pair_out_ref[:, lanes] = rotate(key[:, lanes], cosine, sine).astype(BF)
+    pair_out_ref[:, KV_WIDTH:] = (pair[:, KV_WIDTH:] + vbias_ref[...]).astype(BF)
+
+
+def project(core, tokens, left, right, gain, qbias, kbias, vbias, cosine, sine):
     rows = tokens.shape[0]
     return pl.pallas_call(
         project_kernel,
         in_specs=[SMEM] + [VMEM] * 11,
         out_specs=[VMEM] * 3,
-        out_shape=[shape((rows, WIDTH), BF), shape((rows, WIDTH), BF), shape((copies, rows, 2 * KV_WIDTH), BF)],
+        out_shape=[shape((rows, WIDTH), BF), shape((rows, WIDTH), BF), shape((rows, 2 * KV_WIDTH), BF)],
         compiler_params=params(),
         cost_estimate=cost(2 * rows * WIDTH * QKV, 2 * WIDTH * QKV + 6 * rows * WIDTH),
         name="project",
@@ -713,9 +709,9 @@
     value_bias = vectors[3].reshape(devices, share)[:, :vshare].reshape(1, KV_WIDTH)
 
     normed, queries, kv = project(
-        core, tokens, left, right, attn_gain, query_bias, b_key.astype(F32)[None], value_bias, cosine_own, sine_own, nz
-    )
-    near = share_near(after(kv, cot_near[0]))
+        core, tokens, left, right, attn_gain, query_bias, b_key.astype(F32)[None], value_bias, cosine_own, sine_own
+    )
+    near = gather_z(kv, nz, own_z)
     cot_near.append(gather_near(after(cotangent, near)[cuts[1]], nz).reshape(count, WIDTH))
     other = hop(near, "y")
     cot_other = [hop(after(x, other), "y") for x in cot_near]

time: 570 us -> 565 us (level)
  waiting for transfers between devices: 238 us -> 228 us
    all_to_all x11 -> x10, waiting for transfers between devices: 72 us -> 56.9 us  [swap(): return lax.all_to_all(value, axis, 0, 0, tiled=True)]
    ppermute x51 -> x54, waiting for transfers between devices: 162 us -> 169 us  [hop(): return lax.ppermute(value, axis, [(i, i ^ flip) for i in range(size)])]
    ppermute x51 -> x54, starting transfers between devices: 57.2 us -> 62.8 us  [hop(): return lax.ppermute(value, axis, [(i, i ^ flip) for i in range(size)])]
    all_to_all x11 -> x10, starting transfers between devices: 52.6 us -> 49.9 us  [swap(): return lax.all_to_all(value, axis, 0, 0, tiled=True)]
  transfers between devices with their start and end apart: 67 -> 69, of which waited for: 32 -> 31; matrix products, arithmetic and copies ran while one was open for 11% -> 11% of each run, Pallas kernels for 16% -> 16%
where the time goes in v5:
time: 565 us; the launch traced here: 556 us
  waiting for transfers between devices  228 us (40%)
  Pallas kernels  124 us (22%)
  starting transfers between devices  113 us (20%)
  other arithmetic  45.6 us (8%)
  local copies, waits for them, and re-layouts  30.9 us (5%)
  between operations  15.2 us (3%)
    ppermute x54, waiting for transfers between devices, hop(): return lax.ppermute(value, axis, [(i, i ^ flip) for i in range(size)])  169 us
    ppermute x54, starting transfers between devices, hop(): return lax.ppermute(value, axis, [(i, i ^ flip) for i in range(size)])  62.8 us
    all_to_all x10, waiting for transfers between devices, swap(): return lax.all_to_all(value, axis, 0, 0, tiled=True)  56.9 us
    all_to_all x10, starting transfers between devices, swap(): return lax.all_to_all(value, axis, 0, 0, tiled=True)  49.9 us
    pallas_call x2, Pallas kernels, mlp(): pl.pallas_call(mlp_kernel, grid=(1,), in_specs=[whole(near)] * 4 + [part(...  39 us
    convert_element_type x14, other arithmetic, add_low(): return (left.astype(F32) + right.astype(F32)).astype(BF)  21.3 us
    pallas_call x1, Pallas kernels, attention_backward(): pl.pallas_call(backward_kernel, grid=(HEADS // many,), in_specs=[SMEM, he...  18.6 us
    pallas_call x1, Pallas kernels, outer_by_core(): pl.pallas_call(functools.partial(outer_by_core_kernel, counts=(len(lefts)...  13.4 us
  transfers between devices with their start and end apart: 69, of which 31 were waited for; matrix products, arithmetic and copies ran while one was open for 11% of the time, Pallas kernels for 16%

profile of v5, /device:TPU:0, one launch (start us, length us, event | category | flops | bytes accessed | tf_op | source)
XLA Modules:
  0.0 555.9 jit_solution(1074522701736090684)
XLA Ops:
  13.0 6.3 %all-to-all-start = ((bf16[4,48,2176]{2,1,0:T(8,128)(2,1)}), bf16[4,48,2176]{2,1,0:T(8,128)(2,1)S(1)}, u32[]{:S(2)}, u32[]{:S(2)}) async-start(bf16[4,48,2176]{2,1,0:T(8,128)(2,1)} %broadcast_in_dim.15), calls=%async_computation | async-start | bytes 1671168 | tf_op jit(solution)/shard_map/all_to_all | solution.py:566
  23.7 17.2 %all-to-all-done = bf16[4,48,2176]{2,1,0:T(8,128)(2,1)S(1)} async-done(((bf16[4,48,2176]{2,1,0:T(8,128)(2,1)}), bf16[4,48,2176]{2,1,0:T(8,128)(2,1)S(1)}, u32[]{:S(2)}, u32[]{:S(2)}) %all-to-all-start) | async-done | bytes 835616 | tf_op jit(solution)/shard_map/all_to_all | solution.py:566
  55.6 6.3 %collective-permute-done.1 = bf16[4,48,1152]{2,1,0:T(8,128)(2,1)S(1)} collective-permute-done((bf16[4,48,1152]{2,1,0:T(8,128)(2,1)S(1)}, bf16[4,48,1152]{2,1,0:T(8,128)(2,1)S(1)}, u32[]{:S(2)}, u32[]{:S(2)}) %collective-permute-start.1) | collective-permute-done | bytes 442400 | tf_op jit(solution)/shard_map/ppermute | solution.py:570
  72.8 32.6 %collective-permute-done.7 = bf16[4,48,768]{2,1,0:T(8,128)(2,1)} collective-permute-done((bf16[4,48,768]{2,1,0:T(8,128)(2,1)}, bf16[4,48,768]{2,1,0:T(8,128)(2,1)}, u32[]{:S(2)}, u32[]{:S(2)}) %collective-permute-start.7) | collective-permute-done | bytes 294944 | tf_op jit(solution)/shard_map/ppermute | solution.py:570
  111.8 14.7 %collective-permute-done.11 = bf16[4,2,48,768]{3,2,0,1:T(8,128)(2,1)S(1)} collective-permute-done((bf16[4,2,48,768]{3,2,0,1:T(8,128)(2,1)S(1)}, bf16[4,2,48,768]{3,2,0,1:T(8,128)(2,1)S(1)}, u32[]{:S(2)}, u32[]{:S(2)}) %collective-permute-start.11) | collective-permute-done | bytes 589856 | tf_op jit(solution)/shard_map/ppermute | solution.py:570
  133.8 6.4 %project.1 = (bf16[128,1536]{1,0:T(8,128)(2,1)}, bf16[128,1536]{1,0:T(8,128)(2,1)}, bf16[128,512]{1,0:T(8,128)(2,1)}) custom-call(s32[1]{0:T(128)} %bitcast.core_ref, bf16[128,1536]{1,0:T(8,128)(2,1)} %tokens_ref.3, bf16[768,1024]{1,0:T(8,128)(2,1)} %bitcast.172, bf16[768,1024]{1,0:T(8,128)(2,1)} %copy-done.5, bf16[768,1152]{1,0:T(8,128)(2,1)} %bitcast.168, ...), custom_call_target="tpu_custom_call" | custom-call | flops 805306368 | bytes 7471104 | tf_op jit(solution)/shard_map/project/pallas_call | solution.py:173
  150.6 10.0 %collective-permute-done.14 = bf16[128,512]{1,0:T(8,128)(2,1)} collective-permute-done((bf16[128,512]{1,0:T(8,128)(2,1)}, bf16[128,512]{1,0:T(8,128)(2,1)}, u32[]{:S(2)}, u32[]{:S(2)}) %collective-permute-start.14) | collective-permute-done | bytes 131104 | tf_op jit(solution)/shard_map/ppermute | solution.py:570
  181.7 8.2 %attention_forward.1 = (bf16[128,1536]{1,0:T(8,128)(2,1)}, f32[12,128,1]{2,1,0:T(8,128)}) custom-call(bf16[128,1536]{1,0:T(8,128)(2,1)} %get-tuple-element.126.q_ref, bf16[1024,512]{1,0:T(8,128)(2,1)} %bitcast.184, bf16[1024,512]{1,0:T(8,128)(2,1)} %bitcast.185, s32[128,1]{1,0:T(8,128)} %copy.45.lo_ref, s32[128,1]{1,0:T(8,128)} %iota_add_fusion.hi_ref), custom_call_target="tpu_custom_call" | custom-call | flops 805306368 | bytes 1835008 | tf_op jit(solution)/shard_map/attention_forward/pallas_call | solution.py:244
  207.2 15.7 %collective-permute-done.22.cot_other_ref.refs_5_ = bf16[256,1536]{1,0:T(8,128)(2,1)S(1)} collective-permute-done((bf16[256,1536]{1,0:T(8,128)(2,1)}, bf16[256,1536]{1,0:T(8,128)(2,1)S(1)}, u32[]{:S(2)}, u32[]{:S(2)}) %collective-permute-start.22) | collective-permute-done | bytes 786464 | tf_op jit(solution)/shard_map/ppermute | solution.py:570
  229.4 16.7 %all-to-all-done.6 = bf16[4,64,1536]{2,1,0:T(8,128)(2,1)S(1)} async-done(((bf16[4,64,1536]{2,1,0:T(8,128)(2,1)}), bf16[4,64,1536]{2,1,0:T(8,128)(2,1)S(1)}, u32[]{:S(2)}, u32[]{:S(2)}) %all-to-all-start.6) | async-done | bytes 786464 | tf_op jit(solution)/shard_map/all_to_all | solution.py:566
  249.4 19.4 %mlp.2 = (bf16[512,1152]{1,0:T(8,128)(2,1)}, bf16[512,1152]{1,0:T(8,128)(2,1)}, bf16[512,1152]{1,0:T(8,128)(2,1)}, bf16[256,1536]{1,0:T(8,128)(2,1)}, bf16[256,1...) custom-call(bf16[256,1536]{1,0:T(8,128)(2,1)} %bitcast.191, bf16[256,1536]{1,0:T(8,128)(2,1)} %copy-done.45, ...), custom_call_target="tpu_custom_call" | custom-call | flops 10871635968 | bytes 21626880 | tf_op jit(solution)/shard_map/mlp/pallas_call | solution.py:409
  268.9 19.7 %mlp.3 = (bf16[512,1152]{1,0:T(8,128)(2,1)}, bf16[512,1152]{1,0:T(8,128)(2,1)}, bf16[512,1152]{1,0:T(8,128)(2,1)}, bf16[256,1536]{1,0:T(8,128)(2,1)}, bf16[256,1...) custom-call(bf16[256,1536]{1,0:T(8,128)(2,1)} %bitcast.194, ...), custom_call_target="tpu_custom_call" | custom-call | flops 10871635968 | bytes 21626880 | tf_op jit(solution)/shard_map/mlp/pallas_call | solution.py:409
  295.2 12.9 %collective-permute-done.24 = bf16[256,1536]{1,0:T(8,128)(2,1)S(1)} collective-permute-done((bf16[256,1536]{1,0:T(8,128)(2,1)}, bf16[256,1536]{1,0:T(8,128)(2,1)S(1)}, u32[]{:S(2)}, u32[]{:S(2)}) %collective-permute-start.24) | collective-permute-done | bytes 786464 | tf_op jit(solution)/shard_map/ppermute | solution.py:570
  320.6 7.0 %collective-permute-done.26.refs_6_ = bf16[64,1536]{1,0:T(8,128)(2,1)S(1)} collective-permute-done((bf16[64,1536]{1,0:T(8,128)(2,1)S(1)}, bf16[64,1536]{1,0:T(8,128)(2,1)S(1)}, u32[]{:S(2)}, u32[]{:S(2)}) %collective-permute-start.26) | collective-permute-done | bytes 196640 | tf_op jit(solution)/shard_map/ppermute | solution.py:570
  328.3 13.4 %gate_up_grads.1 = (bf16[1536,1152]{1,0:T(8,128)(2,1)}, bf16[1536,1152]{1,0:T(8,128)(2,1)}) custom-call(s32[1]{0:T(128)} %bitcast.core_ref, bf16[256,1536]{1,0:T(8,128)(2,1)} %bitcast.192, bf16[256,1536]{1,0:T(8,128)(2,1)} %copy-done.45, bf16[256,1536]{1,0:T(8,128)(2,1)} %bitcast.195, bf16[256,1536]{1,0:T(8,128)(2,1)} %collective-permute-done.23.other_ref.refs_3_, ...), custom_call_target="tpu_custom_call" | custom-call | flops 7247757312 | bytes 19660800 | tf_op jit(solution)/shard_map/gate_up_grads/pallas_call | solution.py:459
  358.8 7.1 %collective-permute-done.29 = bf16[256,1536]{1,0:T(8,128)(2,1)} collective-permute-done((bf16[256,1536]{1,0:T(8,128)(2,1)}, bf16[256,1536]{1,0:T(8,128)(2,1)}, u32[]{:S(2)}, u32[]{:S(2)}) %collective-permute-start.29) | collective-permute-done | bytes 786464 | tf_op jit(solution)/shard_map/ppermute | solution.py:570
  365.9 18.6 %attention_backward.1 = (bf16[128,1536]{1,0:T(8,128)(2,1)}, bf16[1024,512]{1,0:T(8,128)(2,1)}, bf16[768,3072]{1,0:T(8,128)(2,1)}, bf16[768,3072]{1,0:T(8,128)(2,1)}) custom-call(s32[1]{0:T(128)} %bitcast.core_ref, bf16[128,1536]{1,0:T(8,128)(2,1)} %get-tuple-element.126.q_ref, bf16[1024,512]{1,0:T(8,128)(2,1)} %bitcast.186, bf16[1024,512]{1,0:T(8,128)(2,1)} %bitcast.187, ...), custom_call_target="tpu_custom_call" | custom-call | flops 2013265920 | bytes 4194304 | tf_op jit(solution)/shard_map/attention_backward/pallas_call | solution.py:332
  410.8 6.0 %all-to-all-done.7 = bf16[8,128,512]{2,1,0:T(8,128)(2,1)} async-done(((bf16[8,128,512]{2,1,0:T(8,128)(2,1)}), bf16[8,128,512]{2,1,0:T(8,128)(2,1)}, u32[]{:S(2)}, u32[]{:S(2)}) %all-to-all-start.7) | async-done | bytes 1048608 | tf_op jit(solution)/shard_map/all_to_all | solution.py:566
  419.9 7.6 %all-to-all-start.8 = ((bf16[8,48,1152]{2,1,0:T(8,128)(2,1)}), bf16[8,48,1152]{2,1,0:T(8,128)(2,1)}, u32[]{:S(2)}, u32[]{:S(2)}) async-start(bf16[8,48,1152]{2,1,0:T(8,128)(2,1)} %bitcast.189), calls=%async_computation.9 | async-start | bytes 1769472 | tf_op jit(solution)/shard_map/all_to_all | solution.py:566
  427.5 7.6 %down_grads.1 = bf16[1152,1536]{1,0:T(8,128)(2,1)} custom-call(bf16[512,1152]{1,0:T(8,128)(2,1)} %get-tuple-element.210.refs_0_, bf16[512,1152]{1,0:T(8,128)(2,1)} %get-tuple-element.211.refs_1_, bf16[256,1536]{1,0:T(8,128)(2,1)} %bitcast.43.cot_near_ref.refs_2_, bf16[256,1536]{1,0:T(8,128)(2,1)} %collective-permute-done.19.cot_other_ref.refs_3_, ...), custom_call_target="tpu_custom_call" | custom-call | flops 3623878656 | bytes 11698176 | tf_op jit(solution)/shard_map/down_grads/pallas_call | solution.py:436
  450.7 6.7 %tokens_back.1 = (f32[128,1536]{1,0:T(8,128)}, f32[1,1536]{1,0:T(1,128)}, f32[1,2048]{1,0:T(1,128)}) custom-call(s32[1]{0:T(128)} %bitcast.core_ref, bf16[128,2048]{1,0:T(8,128)(2,1)} %pad_maximum_fusion.13.grads_ref, bf16[768,1024]{1,0:T(8,128)(2,1)} %bitcast.173, bf16[768,1024]{1,0:T(8,128)(2,1)} %copy-done.5, bf16[768,1152]{1,0:T(8,128)(2,1)} %bitcast.169, ...), custom_call_target="tpu_custom_call" | custom-call | flops 805306368 | bytes 8650752 | tf_op jit(solution)/shard_map/tokens_back/pallas_call | solution.py:545
  457.4 11.8 %all-to-all-done.8.gate_in_ref = bf16[8,48,1152]{2,1,0:T(8,128)(2,1)} async-done(((bf16[8,48,1152]{2,1,0:T(8,128)(2,1)}), bf16[8,48,1152]{2,1,0:T(8,128)(2,1)}, u32[]{:S(2)}, u32[]{:S(2)}) %all-to-all-start.8) | async-done | bytes 884768 | tf_op jit(solution)/shard_map/all_to_all | solution.py:566
  486.1 9.5 %collective-permute-done.47 = f32[1,5120]{1,0:T(1,128)S(1)} collective-permute-done((f32[1,5120]{1,0:T(1,128)S(1)}, f32[1,5120]{1,0:T(1,128)S(1)}, u32[]{:S(2)}, u32[]{:S(2)}) %collective-permute-start.47) | collective-permute-done | bytes 20512 | tf_op jit(solution)/shard_map/ppermute | solution.py:570
  523.3 14.7 %collective-permute-done.42 = bf16[48,3072]{1,0:T(8,128)(2,1)S(1)} collective-permute-done((bf16[48,3072]{1,0:T(8,128)(2,1)S(1)}, bf16[48,3072]{1,0:T(8,128)(2,1)S(1)}, u32[]{:S(2)}, u32[]{:S(2)}) %collective-permute-start.42) | collective-permute-done | bytes 294944 | tf_op jit(solution)/shard_map/ppermute | solution.py:570
  (333 shorter events, 244.9 us)
Async XLA Ops:
  13.0 27.8 %all-to-all-start = ((bf16[4,48,2176]{2,1,0:T(8,128)(2,1)}), bf16[4,48,2176]{2,1,0:T(8,128)(2,1)S(1)}, u32[]{:S(2)}, u32[]{:S(2)}) async-start(bf16[4,48,2176]{2,1,0:T(8,128)(2,1)} %broadcast_in_dim.15), calls=%async_computation | async-start | bytes 1671168 | tf_op jit(solution)/shard_map/all_to_all | solution.py:566
  19.3 229.1 %all-gather.5.cloned.1.call-start = ((), (), s32[]{:S(2)}) async-start(), calls=%async_computation.14 | async-start | bytes 4423680 | tf_op jit(solution)/shard_map/all_gather | solution.py:558
  62.0 43.3 %collective-permute-start.6 = (bf16[2,4,48,1152]{3,2,1,0:T(8,128)(2,1)S(1)}, bf16[2,4,48,1152]{3,2,1,0:T(8,128)(2,1)}, u32[]{:S(2)}, u32[]{:S(2)}) collective-permute-start(bf16[2,4,48,1152]{3,2,1,0:T(8,128)(2,1)S(1)} %pad_maximum_fusion.5), channel_id=1, source_target_pairs={{0,1},{1,0},{2,3},{3,2},{4,5},{5,4},{6,7},{7,6},{8,9},{9,8},{10,11... | collective-permute-start | bytes 2654216 | tf_op jit(solution)/shard_map/ppermute | solution.py:570
  63.7 41.6 %collective-permute-start.5 = (bf16[4,2,48,1024]{3,2,0,1:T(8,128)(2,1)S(1)}, bf16[4,2,48,1024]{3,2,0,1:T(8,128)(2,1)}, u32[]{:S(2)}, u32[]{:S(2)}) collective-permute-start(bf16[4,2,48,1024]{3,2,0,1:T(8,128)(2,1)S(1)} %pad_maximum_fusion.6), channel_id=1, source_target_pairs={{0,16},{8,24},{16,0},{24,8},{1,17},{9,25},{17,1},{25,9},{2,18},{10... | collective-permute-start | bytes 2359304 | tf_op jit(solution)/shard_map/ppermute | solution.py:570
  65.2 40.1 %collective-permute-start.7 = (bf16[4,48,768]{2,1,0:T(8,128)(2,1)}, bf16[4,48,768]{2,1,0:T(8,128)(2,1)}, u32[]{:S(2)}, u32[]{:S(2)}) collective-permute-start(bf16[4,48,768]{2,1,0:T(8,128)(2,1)} %get-tuple-element.252), channel_id=1, source_target_pairs={{0,1},{1,0},{2,3},{3,2},{4,5},{5,4},{6,7},{7,6},{8,9},{9,8},{10,11... | collective-permute-start | bytes 884744 | tf_op jit(solution)/shard_map/ppermute | solution.py:570
  65.5 39.8 %collective-permute-start.8 = (bf16[4,48,768]{2,1,0:T(8,128)(2,1)}, bf16[4,48,768]{2,1,0:T(8,128)(2,1)}, u32[]{:S(2)}, u32[]{:S(2)}) collective-permute-start(bf16[4,48,768]{2,1,0:T(8,128)(2,1)} %get-tuple-element.251), channel_id=1, source_target_pairs={{0,16},{8,24},{16,0},{24,8},{1,17},{9,25},{17,1},{25,9},{2,18},{10... | collective-permute-start | bytes 884744 | tf_op jit(solution)/shard_map/ppermute | solution.py:570
  67.2 61.2 %all-to-all-start.1 = ((bf16[8,48,2304]{2,1,0:T(8,128)(2,1)}), bf16[8,48,2304]{2,1,0:T(8,128)(2,1)}, u32[]{:S(2)}, u32[]{:S(2)}) async-start(bf16[8,48,2304]{2,1,0:T(8,128)(2,1)} %bitcast.41), calls=%async_computation.1 | async-start | bytes 3538944 | tf_op jit(solution)/shard_map/all_to_all | solution.py:566
  72.7 175.7 %all-gather.3.cloned.1.call-start = ((), (), s32[]{:S(2)}) async-start(), calls=%async_computation.13 | async-start | bytes 8847360 | tf_op jit(solution)/shard_map/all_gather | solution.py:558
  150.4 39.5 %collective-permute-start.17 = (bf16[768,768]{1,0:T(8,128)(2,1)S(1)}, bf16[768,768]{1,0:T(8,128)(2,1)S(1)}, u32[]{:S(2)}, u32[]{:S(2)}) collective-permute-start(bf16[768,768]{1,0:T(8,128)(2,1)S(1)} %bitcast.174), channel_id=1, source_target_pairs={{0,8},{8,0},{16,24},{24,16},{1,9},{9,1},{17,25},{25,17},{2,10},{10... | collective-permute-start | bytes 3538952 | tf_op jit(solution)/shard_map/ppermute | solution.py:570
  172.3 28.4 %all-to-all-start.5 = ((bf16[4,64,1536]{2,1,0:T(8,128)(2,1)}), bf16[4,64,1536]{2,1,0:T(8,128)(2,1)}, u32[]{:S(2)}, u32[]{:S(2)}) async-start(bf16[4,64,1536]{2,1,0:T(8,128)(2,1)} %broadcast_in_dim.38), calls=%async_computation.5 | async-start | bytes 1572864 | tf_op jit(solution)/shard_map/all_to_all | solution.py:566
  291.6 36.7 %all-to-all-start.4 = ((bf16[4,64,1536]{2,1,0:T(8,128)(2,1)}), bf16[4,64,1536]{2,1,0:T(8,128)(2,1)S(1)}, u32[]{:S(2)}, u32[]{:S(2)}) async-start(bf16[4,64,1536]{2,1,0:T(8,128)(2,1)} %bitcast.45), calls=%async_computation.4 | async-start | bytes 1572864 | tf_op jit(solution)/shard_map/all_to_all | solution.py:566
  295.1 124.7 %reduce-scatter.4.cloned.1.call-start = ((), (), s32[]{:S(2)}) async-start(), calls=%async_computation.15 | async-start | bytes 2654208 | tf_op jit(solution)/shard_map/reduce_scatter | solution.py:745
  384.6 32.2 %all-to-all-start.7 = ((bf16[8,128,512]{2,1,0:T(8,128)(2,1)}), bf16[8,128,512]{2,1,0:T(8,128)(2,1)}, u32[]{:S(2)}, u32[]{:S(2)}) async-start(bf16[8,128,512]{2,1,0:T(8,128)(2,1)} %bitcast.53), calls=%async_computation.7 | async-start | bytes 2097152 | tf_op jit(solution)/shard_map/all_to_all | solution.py:566
  389.2 88.2 %reduce-scatter.6.cloned.1.call-start = ((), (), s32[]{:S(2)}) async-start(), calls=%async_computation.16 | async-start | bytes 2654208 | tf_op jit(solution)/shard_map/reduce_scatter | solution.py:745
  400.3 40.2 %collective-permute-start.34 = (bf16[4,2,48,1536]{3,2,0,1:T(8,128)(2,1)}, bf16[4,2,48,1536]{3,2,0,1:T(8,128)(2,1)}, u32[]{:S(2)}, u32[]{:S(2)}) collective-permute-start(bf16[4,2,48,1536]{3,2,0,1:T(8,128)(2,1)} %bitcast.163), channel_id=1, source_target_pairs={{0,16},{8,24},{16,0},{24,8},{1,17},{9,25},{17,1},{25,9},{2,18},{10... | collective-permute-start | bytes 3538952 | tf_op jit(solution)/shard_map/ppermute | solution.py:570
  403.1 40.0 %collective-permute-start.33 = (bf16[2,4,48,1536]{3,2,1,0:T(8,128)(2,1)}, bf16[2,4,48,1536]{3,2,1,0:T(8,128)(2,1)}, u32[]{:S(2)}, u32[]{:S(2)}) collective-permute-start(bf16[2,4,48,1536]{3,2,1,0:T(8,128)(2,1)} %dynamic-slice_bitcast_fusion), channel_id=1, source_target_pairs={{0,1},{1,0},{2,3},{3,2},{4,5},{5,4},{6,7},{7,6},{8,9},{9,8},{10,11... | collective-permute-start | bytes 3538952 | tf_op jit(solution)/shard_map/ppermute | solution.py:570
  405.3 52.0 %collective-permute-start.35 = (bf16[128,1536]{1,0:T(8,128)(2,1)}, bf16[128,1536]{1,0:T(8,128)(2,1)}, u32[]{:S(2)}, u32[]{:S(2)}) collective-permute-start(bf16[128,1536]{1,0:T(8,128)(2,1)} %get-tuple-element.222), channel_id=1, source_target_pairs={{0,2},{2,0},{4,6},{6,4},{1,3},{3,1},{5,7},{7,5},{8,10},{10,8},{12,... | collective-permute-start | bytes 1179656 | tf_op jit(solution)/shard_map/ppermute | solution.py:570
  408.5 48.9 %collective-permute-start.36 = (bf16[128,1536]{1,0:T(8,128)(2,1)}, bf16[128,1536]{1,0:T(8,128)(2,1)}, u32[]{:S(2)}, u32[]{:S(2)}) collective-permute-start(bf16[128,1536]{1,0:T(8,128)(2,1)} %get-tuple-element.223), channel_id=1, source_target_pairs={{0,4},{2,6},{4,0},{6,2},{1,5},{3,7},{5,1},{7,3},{8,12},{10,14},{12... | collective-permute-start | bytes 1179656 | tf_op jit(solution)/shard_map/ppermute | solution.py:570
  408.5 48.9 %collective-permute-start.37 = (bf16[128,1536]{1,0:T(8,128)(2,1)}, bf16[128,1536]{1,0:T(8,128)(2,1)}, u32[]{:S(2)}, u32[]{:S(2)}) collective-permute-start(bf16[128,1536]{1,0:T(8,128)(2,1)} %get-tuple-element.220), channel_id=1, source_target_pairs={{0,6},{2,4},{4,2},{6,0},{1,7},{3,5},{5,3},{7,1},{8,14},{10,12},{12... | collective-permute-start | bytes 1179656 | tf_op jit(solution)/shard_map/ppermute | solution.py:570
  419.9 49.3 %all-to-all-start.8 = ((bf16[8,48,1152]{2,1,0:T(8,128)(2,1)}), bf16[8,48,1152]{2,1,0:T(8,128)(2,1)}, u32[]{:S(2)}, u32[]{:S(2)}) async-start(bf16[8,48,1152]{2,1,0:T(8,128)(2,1)} %bitcast.189), calls=%async_computation.9 | async-start | bytes 1769472 | tf_op jit(solution)/shard_map/all_to_all | solution.py:566
  427.4 119.0 %reduce-scatter.8.cloned.1.call-start = ((), (), s32[]{:S(2)}) async-start(), calls=%async_computation.17 | async-start | bytes 4423680 | tf_op jit(solution)/shard_map/reduce_scatter | solution.py:562
  477.3 32.9 %all-to-all-start.9 = ((bf16[8,48,1152]{2,1,0:T(8,128)(2,1)}), bf16[8,48,1152]{2,1,0:T(8,128)(2,1)}, u32[]{:S(2)}, u32[]{:S(2)}) async-start(bf16[8,48,1152]{2,1,0:T(8,128)(2,1)} %bitcast.188), calls=%async_computation.11 | async-start | bytes 1769472 | tf_op jit(solution)/shard_map/all_to_all | solution.py:566
  481.6 28.1 %collective-permute-start.38 = (bf16[4,48,1536]{2,1,0:T(8,128)(2,1)S(1)}, bf16[4,48,1536]{2,1,0:T(8,128)(2,1)S(1)}, u32[]{:S(2)}, u32[]{:S(2)}) collective-permute-start(bf16[4,48,1536]{2,1,0:T(8,128)(2,1)S(1)} %dynamic-slice_bitcast_fusion.2), channel_id=1, source_target_pairs={{0,16},{8,24},{16,0},{24,8},{1,17},{9,25},{17,1},{25,9},{2,18},{10... | collective-permute-start | bytes 1769480 | tf_op jit(solution)/shard_map/ppermute | solution.py:570
  482.4 27.4 %collective-permute-start.39 = (bf16[4,48,1536]{2,1,0:T(8,128)(2,1)}, bf16[4,48,1536]{2,1,0:T(8,128)(2,1)S(1)}, u32[]{:S(2)}, u32[]{:S(2)}) collective-permute-start(bf16[4,48,1536]{2,1,0:T(8,128)(2,1)} %dynamic-slice_bitcast_fusion.1), channel_id=1, source_target_pairs={{0,1},{1,0},{2,3},{3,2},{4,5},{5,4},{6,7},{7,6},{8,9},{9,8},{10,11... | collective-permute-start | bytes 1769480 | tf_op jit(solution)/shard_map/ppermute | solution.py:570
  (94 other events, 1134.3 us)
Sparse Core Ops, SparseCore 0:
  21.7 35.2 all-gather.4
  128.6 50.4 all-gather.2
  384.7 35.1 reduce-scatter.3
  422.1 34.3 reduce-scatter.5
  458.9 53.0 reduce-scatter.7
